TPU v7x, 128 devices: a whole 4x4x4 slice. The times are simulated.
128 devices in a mesh: ctx: 8 (over z_lo, y), grp: 16 (over z_hi, x, core).
Axes of the slice: x: 4, y: 4, z: 4 (z_hi: 2, z_lo: 2; z = z_hi * 2 + z_lo), core: 2. Of those that a mesh axis runs over, the one named last changes fastest.
Arguments:
- queries: bfloat16 [32, 6144], P('grp'), may hold values from -6 to 6
- key_cache: bfloat16 [32, 1024, 1024], P('grp', 'ctx'), may hold values from -6 to 6
- value_cache: bfloat16 [32, 1024, 1024], P('grp', 'ctx'), may hold values from -24 to 24
- new_key: bfloat16 [32, 1024], P('grp'), may hold values from -6 to 6
- new_value: bfloat16 [32, 1024], P('grp'), may hold values from -24 to 24
- lengths: int32 [32], P('grp'), may hold values from 2 to 1024, as said below
- moe_input: bfloat16 [512, 6144], P(('ctx', 'grp')), may hold values from -6 to 6
- routes: int32 [512, 4], P(('ctx', 'grp')), may hold values from 0 to 15, all different within a row; in each aligned block of 4 rows (0 to 3, 4 to 7, ...) at most 2 rows name the same one
- route_weights: float32 [512, 4], P(('ctx', 'grp')), may hold values from 0.05 to 1
- w_gate: bfloat16 [16, 6144, 5376], P('grp', None, 'ctx'), may hold values from -0.078125 to 0.078125
- w_up: bfloat16 [16, 6144, 5376], P('grp', None, 'ctx'), may hold values from -0.078125 to 0.078125
- w_down: bfloat16 [16, 5376, 6144], P('grp', 'ctx'), may hold values from -0.078125 to 0.078125
Outputs:
- head_outputs: bfloat16 [32, 6144], P('grp', 'ctx')
- expert_mix: bfloat16 [512, 6144], P(('ctx', 'grp'))
Inputs may be any that keep to these rules, and one draw needn't show every extreme that they name: `routes`: each row names 4 different experts; among the 4 rows of one device no expert is named more than 2 times, and in every draw some expert is named exactly 2 times by the rows of one device. Row r attends to its cache positions below lengths[r] and to its new key; some row uses all 1024 positions.
All inputs are finite; a program needn't handle non-finite values.
Results may differ from a plain program's by a relative error of at most 0.02.
Values may be sent and summed in bfloat16 or wider, within the bound.
No kernel may reach another device: no remote copies, remote signals or barrier semaphores. Data moves between devices by JAX's collectives and lax.ppermute only.
A program may use at most 128 MiB of HBM per device.

v0:
```python
import jax
import jax.numpy as jnp
from jax import lax
from jax.sharding import PartitionSpec as P

QH = 48
KVH = 8
HD = 128
TOPK = 4


def merged(value, axis, join):
    gathered = jax.tree.map(
        lambda a, kind: lax.all_gather(a.astype(kind), axis),
        value,
        (jnp.bfloat16, jnp.bfloat16, jnp.bfloat16),
    )

    def take(source):
        return jax.tree.map(
            lambda a, own: lax.dynamic_index_in_dim(a, source, 0, False).astype(own.dtype),
            gathered,
            value,
        )

    return lax.fori_loop(
        1, lax.axis_size(axis), lambda source, state: join(state, take(source)), take(0)
    )


def softmax_combine(first, second):
    joint = jnp.maximum(first[0], second[0])
    scale_one = jnp.exp(first[0] - joint)
    scale_two = jnp.exp(second[0] - joint)
    return (
        joint,
        first[1] * scale_one + second[1] * scale_two,
        first[2] * scale_one[..., None] + second[2] * scale_two[..., None],
    )


def attend(queries, key_cache, value_cache, new_key, new_value, lengths):
    row_count = queries.shape[0]
    local_len = key_cache.shape[1]
    group = QH // KVH
    scale = HD ** (-0.5)
    high = lax.Precision.HIGHEST
    q_heads = queries.reshape(row_count, KVH, group, HD)
    keys_here = key_cache.reshape(row_count, local_len, KVH, HD)
    scores = (
        jnp.einsum("rkgd,rckd->rkgc", q_heads, keys_here, preferred_element_type=jnp.float32)
        * scale
    )
    own_score = (
        jnp.einsum(
            "rkgd,rkd->rkg",
            q_heads,
            new_key.reshape(row_count, KVH, HD),
            preferred_element_type=jnp.float32,
        )
        * scale
    )
    ctx_index = lax.axis_index("ctx")
    position = ctx_index * local_len + jnp.arange(local_len, dtype=jnp.int32)
    live = (position[None, :] < lengths[:, None])[:, None, None, :]
    leader = ctx_index == 0
    local_top = jnp.max(jnp.where(live, scores, -1e30), axis=-1)
    local_top = jnp.where(leader, jnp.maximum(local_top, own_score), local_top)
    values_here = value_cache.reshape(row_count, local_len, KVH, HD).astype(jnp.float32)
    own_values = new_value.reshape(row_count, KVH, 1, HD).astype(jnp.float32)
    heads_here = QH // lax.axis_size("ctx")
    weights = jnp.where(live, jnp.exp(scores - local_top[..., None]), 0.0)
    own_weight = jnp.where(leader, jnp.exp(own_score - local_top), 0.0)
    total = jnp.sum(weights, axis=-1) + own_weight
    mixed = (
        jnp.einsum("rkgc,rckd->rkgd", weights, values_here, precision=high)
        + own_weight[..., None] * own_values
    )
    total, mixed = (total, mixed)
    joint, total, mixed = merged((local_top, total, mixed), "ctx", softmax_combine)
    result = (mixed / total[..., None]).reshape(row_count, QH, HD)
    result = lax.dynamic_slice_in_dim(result, ctx_index * heads_here, heads_here, 1)
    return result.reshape(row_count, heads_here * HD).astype(jnp.bfloat16)


def body(
    queries,
    key_cache,
    value_cache,
    new_key,
    new_value,
    lengths,
    moe_input,
    routes,
    route_weights,
    w_gate,
    w_up,
    w_down,
):
    head_outputs = attend(queries, key_cache, value_cache, new_key, new_value, lengths)
    row_count = moe_input.shape[0]
    experts = lax.axis_size("grp") * w_gate.shape[0]
    capacity = max(2, 2 * row_count * TOPK // experts)
    flat = routes.reshape(-1)
    onehot = (flat[:, None] == jnp.arange(experts, dtype=jnp.int32)[None, :]).astype(jnp.int32)
    earlier = jnp.cumsum(onehot, axis=0) - onehot
    slot_index = jnp.sum(earlier * onehot, axis=1)
    target = flat * capacity + slot_index
    selector = (target[:, None] == jnp.arange(experts * capacity, dtype=jnp.int32)[None, :]).astype(
        jnp.float32
    )
    selector = selector.reshape(row_count, TOPK, experts * capacity)
    row_select = jnp.sum(selector, axis=1).astype(jnp.bfloat16)
    send_rows = jnp.dot(row_select.T, moe_input, preferred_element_type=jnp.float32).astype(
        jnp.bfloat16
    )
    gate_w = w_gate[0]
    up_w = w_up[0]
    down_w = w_down[0]
    copies = lax.axis_size("ctx")
    widened = jnp.broadcast_to(send_rows[None], (copies,) + send_rows.shape).reshape(
        copies * send_rows.shape[0], send_rows.shape[1]
    )
    arrived = lax.all_to_all(widened, ("ctx", "grp"), split_axis=0, concat_axis=0, tiled=True)
    gate = jnp.dot(arrived, gate_w, preferred_element_type=jnp.float32)
    upper = jnp.dot(arrived, up_w, preferred_element_type=jnp.float32)
    hidden = (jax.nn.silu(gate) * upper).astype(jnp.bfloat16)
    summed = lax.psum_scatter(
        jnp.dot(hidden, down_w, preferred_element_type=jnp.float32).astype(jnp.bfloat16),
        "ctx",
        scatter_dimension=0,
        tiled=True,
    )
    returned = lax.all_to_all(summed, "grp", split_axis=0, concat_axis=0, tiled=True)
    share = route_weights / jnp.sum(route_weights, axis=-1, keepdims=True)
    combine_matrix = jnp.einsum("rk,rkj->rj", share, selector, precision=lax.Precision.HIGHEST)
    expert_mix = jnp.dot(
        combine_matrix, returned.astype(jnp.float32), precision=lax.Precision.HIGHEST
    )
    return (head_outputs, expert_mix.astype(jnp.bfloat16))


def solution(mesh):
    placed = (
        P("grp", None),
        P("grp", "ctx", None),
        P("grp", "ctx", None),
        P("grp", None),
        P("grp", None),
        P("grp"),
        P(("ctx", "grp"), None),
        P(("ctx", "grp"), None),
        P(("ctx", "grp"), None),
        P("grp", None, "ctx"),
        P("grp", None, "ctx"),
        P("grp", "ctx", None),
    )
    return jax.shard_map(
        body,
        mesh=mesh,
        in_specs=placed,
        out_specs=(P("grp", "ctx"), P(("ctx", "grp"), None)),
        check_vma=False,
    )
```

profile of v0, /device:TPU:1, one launch (start us, length us, event | category | flops | bytes accessed | tf_op | source)
XLA Modules:
  0.0 219.3 jit_solution(17102877863624757008)
XLA Ops:
  7.2 0.0 copy-start
  7.2 0.8 eq.34
  8.0 0.1 fusion.33
  8.1 0.2 select_reduce_fusion.1
  8.3 0.1 reduce_sum.41
  8.4 0.7 multiply_add_fusion
  9.1 0.1 convert_reduce_fusion
  9.2 1.1 convolution_convert_fusion
  10.3 2.0 broadcast_in_dim.48
  12.3 7.1 %all_to_all.16 = bf16[128,2,6144]{2,1,0:T(2,128)(2,1)} reshape(bf16[8,32,6144]{2,1,0:T(8,128)(2,1)} %broadcast_in_dim.48) | data formatting | bytes 6291456 | tf_op jit(solution)/shard_map/all_to_all | solution.py:124
  19.4 11.9 %all-to-all-start = ((bf16[128,2,6144]{2,1,0:T(2,128)(2,1)}), bf16[128,2,6144]{2,1,0:T(2,128)(2,1)}, u32[]{:S(2)}, u32[]{:S(2)}) async-start(bf16[128,2,6144]{2,1,0:T(2,128)(2,1)} %all_to_all.16), calls=%async_computation | async-start | bytes 6291456 | tf_op jit(solution)/shard_map/all_to_all | solution.py:124
  31.3 0.2 reduce-scatter.2.cloned.1.call-start
  31.5 41.4 %all-to-all-done = bf16[128,2,6144]{2,1,0:T(2,128)(2,1)} async-done(((bf16[128,2,6144]{2,1,0:T(2,128)(2,1)}), bf16[128,2,6144]{2,1,0:T(2,128)(2,1)}, u32[]{:S(2)}, u32[]{:S(2)}) %all-to-all-start) | async-done | bytes 3145760 | tf_op jit(solution)/shard_map/all_to_all | solution.py:124
  72.9 7.3 %all_to_all.18 = bf16[256,6144]{1,0:T(8,128)(2,1)} reshape(bf16[128,2,6144]{2,1,0:T(2,128)(2,1)} %all-to-all-done) | data formatting | bytes 6291456 | tf_op jit(solution)/shard_map/all_to_all | solution.py:124
  80.2 6.6 %fusion.7 = f32[256,672]{0,1:T(8,128)S(1)} fusion(bf16[256,6144]{1,0:T(8,128)(2,1)} %all_to_all.18, bf16[1,6144,672]{1,2,0:T(8,128)(2,1)} %param.23), kind=kOutput, calls=%fused_computation.14 | convolution fusion | flops 2113929216 | bytes 12091392 | tf_op jit(solution)/shard_map/dot_general | solution.py:125
  86.9 0.0 copy-start.6
  86.9 17.5 %fusion.9 = bf16[256,6144]{1,0:T(8,128)(2,1)} fusion(bf16[1,672,6144]{2,1,0:T(8,128)(2,1)} %param.25, bf16[256,6144]{1,0:T(8,128)(2,1)} %all_to_all.18, bf16[1,6144,672]{1,2,0:T(8,128)(2,1)} %param.24, f32[256,672]{0,1:T(8,128)S(1)} %fusion.7), kind=kOutput, calls=%fused_computation.16 | convolution fusion | flops 4230463488 | bytes 23494656 | tf_op jit(solution)/shard_map/dot_general | solution.py:129
  104.4 0.0 reduce-scatter.2.cloned.1.call-update
  104.4 0.1 broadcast_compare_fusion
  104.6 0.1 fusion.41
  104.7 0.5 select_reduce_fusion
  105.2 0.2 fusion.28
  105.4 0.6 fusion.18
  106.0 23.6 %all-gather.1 = bf16[16,8,6]{2,1,0:T(8,128)(2,1)S(1)} all-gather(bf16[2,8,6]{2,1,0:T(8,128)(2,1)S(1)} %get-tuple-element.220), channel_id=3, replica_groups=mesh['ctx'=8,'grp'=16] {'ctx'}, dimensions={0}, use_global_device_ids=true | all-gather | bytes 1728 | tf_op jit(solution)/shard_map/all_gather | solution.py:14
  129.6 0.1 copy.54
  129.7 0.2 copy.57
  129.8 23.0 %all-gather = bf16[16,8,6]{2,1,0:T(8,128)(2,1)S(1)} all-gather(bf16[2,8,6]{2,1,0:T(8,128)(2,1)S(1)} %get-tuple-element.222), channel_id=2, replica_groups=mesh['ctx'=8,'grp'=16] {'ctx'}, dimensions={0}, use_global_device_ids=true | all-gather | bytes 1728 | tf_op jit(solution)/shard_map/all_gather | solution.py:14
  152.8 0.1 copy.53
  152.9 0.2 copy.56
  153.0 22.2 %all-gather.2 = bf16[16,8,6,128]{3,1,2,0:T(8,128)(2,1)S(1)} all-gather(bf16[2,8,6,128]{3,1,2,0:T(8,128)(2,1)S(1)} %copy.50), channel_id=4, replica_groups=mesh['ctx'=8,'grp'=16] {'ctx'}, dimensions={0}, use_global_device_ids=true | all-gather | bytes 221184 | tf_op jit(solution)/shard_map/all_gather | solution.py:14
  175.3 2.6 %while.19 = (s32[]{:T(128)}, f32[2,8,6]{1,0,2:T(2,128)S(1)}, f32[2,8,6]{1,0,2:T(2,128)S(1)}, f32[2,8,6,128]{3,2,1,0:T(8,128)S(1)}, bf16[8,2,8,6]{2,1,3,0:T(2,128...) while((s32[]{:T(128)}, f32[2,8,6]{1,0,2:T(2,128)S(1)}, ...), condition=%wide.region_3.4_spmd, body=%wide.region_2.3_spmd.sunk | while | flops 49925 | bytes 177167 | solution.py:26
  175.3 0.1 copy.92
  175.4 0.1 copy.93
  175.5 0.1 fusion.57
  175.7 0.1 copy.92
  175.8 0.1 copy.93
  175.9 0.1 fusion.57
  176.1 0.1 copy.92
  176.2 0.1 copy.93
  176.2 0.1 fusion.57
  176.4 0.1 copy.92
  176.5 0.1 copy.93
  176.6 0.1 fusion.57
  176.8 0.1 copy.92
  176.9 0.1 copy.93
  177.0 0.1 fusion.57
  177.2 0.1 copy.92
  177.3 0.1 copy.93
  177.4 0.1 fusion.57
  177.5 0.1 copy.92
  177.6 0.1 copy.93
  177.7 0.1 fusion.57
  177.9 0.1 copy.59
  177.9 0.1 reduce_sum.39
  178.1 0.1 broadcast_divide_fusion
  178.2 0.0 reduce-scatter.2.cloned.1.call-done
  178.2 2.0 all_to_all.19
  180.2 21.5 %all-to-all-start.1 = ((bf16[16,2,6144]{2,1,0:T(2,128)(2,1)}), bf16[16,2,6144]{2,1,0:T(2,128)(2,1)S(1)}, u32[]{:S(2)}, u32[]{:S(2)}) async-start(bf16[16,2,6144]{2,1,0:T(2,128)(2,1)} %all_to_all.19), calls=%async_computation.2 | async-start | bytes 786432 | tf_op jit(solution)/shard_map/all_to_all | solution.py:134
  201.7 0.1 broadcast_divide_fusion.1
  201.8 0.6 fusion.35
  202.4 0.2 fusion.32
  202.6 8.9 %all-to-all-done.1 = bf16[16,2,6144]{2,1,0:T(2,128)(2,1)S(1)} async-done(((bf16[16,2,6144]{2,1,0:T(2,128)(2,1)}), bf16[16,2,6144]{2,1,0:T(2,128)(2,1)S(1)}, u32[]{:S(2)}, u32[]{:S(2)}) %all-to-all-start.1) | async-done | bytes 393248 | tf_op jit(solution)/shard_map/all_to_all | solution.py:134
  211.4 0.1 all_to_all.21
  211.6 0.9 convolution_convert_fusion.1
  (40 shorter events, 0.5 us)
Async XLA Ops:
  7.2 97.5 %copy-start = (bf16[2,128,1024]{2,1,0:T(8,128)(2,1)S(1)}, bf16[2,128,1024]{2,1,0:T(8,128)(2,1)}, u32[]{:S(2)}) copy-start(bf16[2,128,1024]{2,1,0:T(8,128)(2,1)} %param.15) | copy-start | bytes 1572868
  12.3 19.2 %copy-start.3 = (bf16[2,1024]{1,0:T(2,128)(2,1)S(1)}, bf16[2,1024]{1,0:T(2,128)(2,1)}, u32[]{:S(2)}) copy-start(bf16[2,1024]{1,0:T(2,128)(2,1)} %param.18) | copy-start | bytes 12292
  19.4 53.5 %all-to-all-start = ((bf16[128,2,6144]{2,1,0:T(2,128)(2,1)}), bf16[128,2,6144]{2,1,0:T(2,128)(2,1)}, u32[]{:S(2)}, u32[]{:S(2)}) async-start(bf16[128,2,6144]{2,1,0:T(2,128)(2,1)} %all_to_all.16), calls=%async_computation | async-start | bytes 6291456 | tf_op jit(solution)/shard_map/all_to_all | solution.py:124
  31.3 146.9 %reduce-scatter.2.cloned.1.call-start = ((), (), s32[]{:S(2)}) async-start(), calls=%async_computation.3 | async-start | bytes 3538944 | tf_op jit(solution)/shard_map/reduce_scatter | solution.py:128
  86.9 17.5 %copy-start.6 = (s32[2]{0:T(128)S(1)}, s32[2]{0:T(128)}, u32[]{:S(2)}) copy-start(s32[2]{0:T(128)} %param.19) | copy-start | bytes 28
  86.9 17.6 %copy-start.4 = (bf16[2,1024]{1,0:T(2,128)(2,1)S(1)}, bf16[2,1024]{1,0:T(2,128)(2,1)}, u32[]{:S(2)}) copy-start(bf16[2,1024]{1,0:T(2,128)(2,1)} %param.17) | copy-start | bytes 12292
  86.9 17.6 %copy-start.1 = (bf16[2,6144]{1,0:T(2,128)(2,1)S(1)}, bf16[2,6144]{1,0:T(2,128)(2,1)}, u32[]{:S(2)}) copy-start(bf16[2,6144]{1,0:T(2,128)(2,1)} %param.14) | copy-start | bytes 73732
  86.9 18.5 %copy-start.5 = (bf16[2,128,1024]{2,1,0:T(8,128)(2,1)S(1)}, bf16[2,128,1024]{2,1,0:T(8,128)(2,1)}, u32[]{:S(2)}) copy-start(bf16[2,128,1024]{2,1,0:T(8,128)(2,1)} %param.16) | copy-start | bytes 1572868
  104.4 73.6 %copy-start.2 = (f32[4,4]{1,0:T(4,128)S(1)}, f32[4,4]{1,0:T(4,128)}, u32[]{:S(2)}) copy-start(f32[4,4]{1,0:T(4,128)} %param.22) | copy-start | bytes 196
  180.2 31.3 %all-to-all-start.1 = ((bf16[16,2,6144]{2,1,0:T(2,128)(2,1)}), bf16[16,2,6144]{2,1,0:T(2,128)(2,1)S(1)}, u32[]{:S(2)}, u32[]{:S(2)}) async-start(bf16[16,2,6144]{2,1,0:T(2,128)(2,1)} %all_to_all.19), calls=%async_computation.2 | async-start | bytes 786432 | tf_op jit(solution)/shard_map/all_to_all | solution.py:134
Sparse Core Ops, SparseCore 0:
  104.5 39.2 reduce-scatter.1
where the time goes:
time: 220 us; the launch traced here: 219 us
  blocking collectives  68.7 us (31%)
  waiting for transfers between devices  50.3 us (23%)
  starting transfers between devices  33.6 us (15%)
  matrix products  27.5 us (12%)
  local copies, waits for them, and re-layouts  22.1 us (10%)
  between operations  14.2 us (6%)
  other arithmetic  2.71 us (1%)
    all_gather x3, blocking collectives, merged(): lax.all_gather(a.astype(kind), axis)  68.7 us
    all_to_all x1, waiting for transfers between devices, body(): lax.all_to_all(widened, ('ctx', 'grp'), split_axis=0, concat_axis=0, tile...  41.4 us
    all_to_all x1, starting transfers between devices, body(): lax.all_to_all(summed, 'grp', split_axis=0, concat_axis=0, tiled=True)  21.5 us
    dot_general x1, matrix products, body(): jnp.dot(hidden, down_w, preferred_element_type=jnp.float32)  17.5 us
    all_to_all x2, local copies, waits for them, and re-layouts, body(): lax.all_to_all(widened, ('ctx', 'grp'), split_axis=0, concat_axis=0, tile...  14.4 us
    all_to_all x1, starting transfers between devices, body(): lax.all_to_all(widened, ('ctx', 'grp'), split_axis=0, concat_axis=0, tile...  11.9 us
    all_to_all x1, waiting for transfers between devices, body(): lax.all_to_all(summed, 'grp', split_axis=0, concat_axis=0, tiled=True)  8.88 us
    dot_general x1, matrix products, body(): gate = jnp.dot(arrived, gate_w, preferred_element_type=jnp.float32)  6.63 us
  transfers between devices with their start and end apart: 3, of which 2 were waited for; matrix products, arithmetic and copies ran while one was open for 3% of the time, Pallas kernels for 0%

commit v1 on v0

v1 whole, which is shorter than its diff:
```python
import functools

import jax
import jax.numpy as jnp
from jax import lax
from jax.experimental import pallas as pl
from jax.experimental.pallas import tpu as pltpu
from jax.sharding import PartitionSpec as P

QH = 48
KVH = 8
HD = 128
TOPK = 4
D = 6144
HALF = D // 2
FF = 672
META = 128
ALL = ("ctx", "grp")
BF = jnp.bfloat16
F32 = jnp.float32
KB = 512
STEPS = HALF // KB


def coords(i):
    c, g = divmod(i, 16)
    return {"x": (g >> 1) & 3, "y": c & 3, "z": ((g >> 3) << 1) | (c >> 2), "core": g & 1}


def index(x, y, z, core):
    return (((z & 1) << 2) | y) * 16 + (((z >> 1) << 3) | (x << 1) | core)


def shifted(axes, k):
    pairs = []
    for i in range(128):
        at = coords(i)
        axis = axes[at["core"]]
        at[axis] = (at[axis] + k) % (2 if axis == "core" else 4)
        pairs.append((i, index(**at)))
    return pairs


OUTER = ("x", "y")
INNER = ("y", "x")
CORE = ("core", "core")
COLUMNS = [
    [index(x, y, z, core) for z in range(4) for core in range(2)] for x in range(4) for y in range(4)
]


def move(a, axes, k):
    return lax.ppermute(a, ALL, shifted(axes, k % 4 if axes is not CORE else 1))


def turned(a):
    return a.reshape(4, 4, 16, a.shape[-1]).swapaxes(0, 1).reshape(a.shape)


def gate_up_kernel(core_ref, *refs):
    own, other = refs[0:4], refs[4:8]
    gate_w, up_w, out, gate, upper = refs[8:]
    step = pl.program_id(0)

    @pl.when(step == 0)
    def _():
        gate[...] = jnp.zeros_like(gate)
        upper[...] = jnp.zeros_like(upper)

    def add(rows):
        gate[...] += jnp.dot(rows, gate_w[...], preferred_element_type=F32)
        upper[...] += jnp.dot(rows, up_w[...], preferred_element_type=F32)

    @pl.when(step < STEPS)
    def _():
        add(jnp.concatenate([r[...] for r in own], axis=0))

    @pl.when(step >= STEPS)
    def _():
        add(turned(jnp.concatenate([r[...] for r in other], axis=0)))

    @pl.when(step == 2 * STEPS - 1)
    def _():
        v = gate[...]
        out[...] = (v / (1.0 + jnp.exp(-v)) * upper[...]).astype(BF)


def gate_up(core, own, other, gate_w, up_w):
    spec_own = pl.BlockSpec((64, KB), lambda i, c: (0, jnp.minimum(i, STEPS - 1)))
    spec_other = pl.BlockSpec((64, KB), lambda i, c: (0, jnp.maximum(i - STEPS, 0)))
    spec_w = pl.BlockSpec((KB, FF), lambda i, c: ((i + STEPS * c[0]) % (2 * STEPS), 0))
    return pl.pallas_call(
        gate_up_kernel,
        grid_spec=pltpu.PrefetchScalarGridSpec(
            num_scalar_prefetch=1,
            grid=(2 * STEPS,),
            in_specs=[spec_own] * 4 + [spec_other] * 4 + [spec_w] * 2,
            out_specs=pl.BlockSpec((256, FF), lambda i, c: (0, 0)),
            scratch_shapes=[pltpu.VMEM((256, FF), F32)] * 2,
        ),
        out_shape=jax.ShapeDtypeStruct((256, FF), BF),
        compiler_params=pltpu.CompilerParams(vmem_limit_bytes=40 << 20),
        cost_estimate=pl.CostEstimate(
            flops=4 * 256 * D * FF, bytes_accessed=4 * D * FF + 2 * 256 * D, transcendentals=256 * FF
        ),
        name="gate_up",
    )(core, *own, *other, gate_w, up_w)


def down_kernel(turn, half_ref, hidden, weights, share, out):
    rows = jnp.dot(hidden[...], weights[...], preferred_element_type=F32) * share[...]
    rows = rows.astype(BF)
    out[...] = turned(rows) if turn else rows


def down(half, hidden, weights, share, turn):
    return pl.pallas_call(
        functools.partial(down_kernel, turn),
        grid_spec=pltpu.PrefetchScalarGridSpec(
            num_scalar_prefetch=1,
            grid=(STEPS,),
            in_specs=[
                pl.BlockSpec((256, FF), lambda i, c: (0, 0)),
                pl.BlockSpec((FF, KB), lambda i, c: (0, i + STEPS * c[0])),
                pl.BlockSpec((256, 1), lambda i, c: (0, 0)),
            ],
            out_specs=pl.BlockSpec((256, KB), lambda i, c: (0, i)),
        ),
        out_shape=jax.ShapeDtypeStruct((256, HALF), BF),
        compiler_params=pltpu.CompilerParams(vmem_limit_bytes=40 << 20),
        cost_estimate=pl.CostEstimate(
            flops=2 * 256 * HALF * FF, bytes_accessed=2 * HALF * FF + 2 * 256 * HALF, transcendentals=0
        ),
        name="down",
    )(half, hidden, weights, share)


def attend_here(queries, key_cache, value_cache, new_key, new_value, lengths):
    rows, local = queries.shape[0], key_cache.shape[1]
    group = QH // KVH
    scale = HD ** (-0.5)
    q = queries.reshape(rows, KVH, group, HD)
    keys = key_cache.reshape(rows, local, KVH, HD)
    values = value_cache.reshape(rows, local, KVH, HD)
    scores = jnp.einsum("rkgd,rckd->rkgc", q, keys, preferred_element_type=F32) * scale
    own = (
        jnp.einsum("rkgd,rkd->rkg", q, new_key.reshape(rows, KVH, HD), preferred_element_type=F32)
        * scale
    )
    place = lax.axis_index("ctx")
    leader = place == 0
    position = place * local + jnp.arange(local, dtype=jnp.int32)
    live = (position[None, :] < lengths[:, None])[:, None, None, :]
    top = jnp.max(jnp.where(live, scores, -1e30), axis=-1)
    top = jnp.where(leader, jnp.maximum(top, own), top)
    top = lax.reduce_precision(top, 8, 7)
    weights = jnp.where(live, jnp.exp(scores - top[..., None]), 0.0)
    own_weight = jnp.where(leader, jnp.exp(own - top), 0.0)
    total = jnp.sum(weights, axis=-1) + own_weight
    high = lax.reduce_precision(weights, 8, 7)
    parts = jnp.concatenate([high.astype(BF), (weights - high).astype(BF)], axis=2)
    mixed = jnp.einsum("rkgc,rckd->rkgd", parts, values, preferred_element_type=F32)
    mixed = mixed[:, :, :group] + mixed[:, :, group:]
    mixed = mixed + own_weight[..., None] * new_value.reshape(rows, KVH, 1, HD).astype(F32)
    total_high = lax.reduce_precision(total, 8, 7)
    stats = jnp.stack([top, total_high, total - total_high], axis=-1).astype(BF)
    stats = jnp.pad(stats, ((0, 0), (0, 0), (0, 0), (0, HD - 3)))
    packed = jnp.concatenate([mixed.astype(BF), stats], axis=-1)
    return packed.transpose(1, 0, 2, 3).reshape(KVH, rows * group, 2 * HD)


def attend_join(parts):
    parts = parts.astype(F32)
    top = parts[:, :, HD]
    total = parts[:, :, HD + 1] + parts[:, :, HD + 2]
    scale = jnp.exp(top - jnp.max(top, axis=0, keepdims=True))
    joined = jnp.sum(parts[:, :, :HD] * scale[..., None], axis=0)
    joined = joined / jnp.sum(total * scale, axis=0)[:, None]
    group = QH // KVH
    return joined.reshape(-1, group * HD).astype(BF)


def describe(routes, route_weights):
    rows = routes.shape[0]
    same = routes[:, :, None, None] == routes[None, None, :, :]
    before = (jnp.arange(rows)[None, :] < jnp.arange(rows)[:, None])[:, None, :, None]
    slot = jnp.sum((same & before).astype(jnp.int32), axis=(2, 3))
    share = route_weights / jnp.sum(route_weights, axis=-1, keepdims=True)
    high = lax.reduce_precision(share, 8, 7)
    middle = lax.reduce_precision(share - high, 8, 7)
    low = share - high - middle
    columns = jnp.concatenate([routes.astype(F32), slot.astype(F32), high, middle, low], axis=1)
    return jnp.pad(columns, ((0, 0), (0, META - 5 * TOPK))).astype(BF)


def selection(meta, expert):
    meta = meta[:, : 5 * TOPK].astype(F32)
    hit = meta[:, :TOPK] == expert.astype(F32)
    slot = jnp.sum(jnp.where(hit, meta[:, TOPK : 2 * TOPK], 0.0), axis=1)
    share = meta[:, 2 * TOPK : 3 * TOPK] + meta[:, 3 * TOPK : 4 * TOPK] + meta[:, 4 * TOPK : 5 * TOPK]
    share = jnp.sum(jnp.where(hit, share, 0.0), axis=1)
    block = jnp.arange(128, dtype=jnp.int32) // 4
    target = jnp.where(jnp.any(hit, axis=1), block * 2 + slot.astype(jnp.int32), -1)
    chosen = target[None, :] == jnp.arange(64, dtype=jnp.int32)[:, None]
    return chosen.astype(BF), jnp.sum(jnp.where(chosen, share[None, :], 0.0), axis=1, keepdims=True)


def body(
    queries,
    key_cache,
    value_cache,
    new_key,
    new_value,
    lengths,
    moe_input,
    routes,
    route_weights,
    w_gate,
    w_up,
    w_down,
):
    expert = lax.axis_index("grp")
    core = expert % 2
    core_at = core.astype(jnp.int32).reshape(1)

    meta = describe(routes, route_weights)
    halves = moe_input.reshape(4, 2, HALF).swapaxes(0, 1)
    halves = jnp.concatenate([halves, jnp.broadcast_to(meta[None], (2, 4, META))], axis=2)
    sent = jnp.broadcast_to(halves[None], (4, 2, 4, HALF + META)).reshape(8, 4, HALF + META)
    column = lax.all_to_all(sent, ALL, 0, 0, axis_index_groups=COLUMNS, tiled=True)
    column = column.reshape(32, HALF + META)
    plane = jnp.concatenate([column] + [move(column, INNER, k) for k in (1, 2, 3)], axis=0)
    packed = attend_here(queries, key_cache, value_cache, new_key, new_value, lengths)
    plane, packed = lax.optimization_barrier((plane, packed))
    shards = [plane] + [move(plane, OUTER, k) for k in (1, 2, 3)]

    head_parts = lax.all_to_all(packed, "ctx", 0, 0, tiled=True)
    head_outputs = attend_join(head_parts)

    own, other, choose, shares = [], [], [], []
    for shard in shards:
        meta = shard[:, HALF:]
        mine, share = selection(meta, expert)
        theirs, _ = selection(meta, expert ^ 1)
        pick = jnp.concatenate([mine, theirs], axis=0)
        picked = jnp.dot(pick, shard[:, :HALF], preferred_element_type=F32).astype(BF)
        own.append(picked[:64])
        other.append(move(picked[64:], CORE, 1))
        choose.append(pick)
        shares.append(share)
    share = jnp.concatenate(shares, axis=0)

    hidden = gate_up(core_at, own, other, w_gate[0], w_up[0])
    theirs = down(1 - core_at, hidden, w_down[0], share, True)
    received = move(theirs, CORE, 1)
    mine = down(core_at, hidden, w_down[0], share, False)

    def back(k):
        rows = jnp.concatenate([mine[64 * k : 64 * k + 64], received[64 * k : 64 * k + 64]], axis=0)
        return lax.dot_general(
            choose[k], rows, (((0,), (0,)), ((), ())), preferred_element_type=F32
        ).astype(BF)

    def added(parts):
        return sum(p.astype(F32) for p in parts).astype(BF)

    plane = added([move(back(k), OUTER, -k) for k in (2, 1, 3)] + [back(0)])
    column = added(
        [move(plane[32 * k : 32 * k + 32], INNER, -k) for k in (2, 1, 3)] + [plane[:32]]
    )
    sums = lax.all_to_all(
        column.reshape(8, 4, HALF), ALL, 0, 0, axis_index_groups=COLUMNS, tiled=True
    )
    sums = jnp.sum(sums.reshape(4, 2, 4, HALF).astype(F32), axis=0).astype(BF)
    return head_outputs, sums.swapaxes(0, 1).reshape(4, D)


def solution(mesh):
    placed = (
        P("grp", None),
        P("grp", "ctx", None),
        P("grp", "ctx", None),
        P("grp", None),
        P("grp", None),
        P("grp"),
        P(ALL, None),
        P(ALL, None),
        P(ALL, None),
        P("grp", None, "ctx"),
        P("grp", None, "ctx"),
        P("grp", "ctx", None),
    )
    return jax.shard_map(
        body,
        mesh=mesh,
        in_specs=placed,
        out_specs=(P("grp", "ctx"), P(ALL, None)),
        check_vma=False,
    )
```

time: 220 us -> 155 us (0.70)
  blocking collectives: 68.7 us -> 16.9 us
  waiting for transfers between devices: 50.3 us -> 24 us
  Pallas kernels: 0 us -> 17.7 us
  local copies, waits for them, and re-layouts: 22.1 us -> 39.6 us
  matrix products: 27.5 us -> 10.7 us
  between operations: 14.2 us -> 1.13 us
  other arithmetic: 2.71 us -> 10.5 us
    all_gather x3 -> x0, blocking collectives: 68.7 us -> none  [merged(): lax.all_gather(a.astype(kind), axis)]
    all_to_all x2, waiting for transfers between devices: 50.2 us -> 6.18 us  [the longest x1 5.3 us: body(): lax.all_to_all(column.reshape(8, 4, HALF), ALL, 0, 0, axis_index_groups=C...]
    unnamed x15 -> x14, local copies, waits for them, and re-layouts: 0.04 us -> 30.8 us
    all_to_all x2, starting transfers between devices: 33.4 us -> 11.2 us  [the longest x1 6.81 us: body(): lax.all_to_all(sent, ALL, 0, 0, axis_index_groups=COLUMNS, tiled=True)]
    ppermute x0 -> x17, starting transfers between devices: none -> 21.3 us  [move(): return lax.ppermute(a, ALL, shifted(axes, k % 4 if axes is not CORE else 1))]
    ppermute x0 -> x17, waiting for transfers between devices: none -> 17.8 us  [move(): return lax.ppermute(a, ALL, shifted(axes, k % 4 if axes is not CORE else 1))]
    pallas_call x0 -> x3, Pallas kernels: none -> 17.7 us  [the longest x1 12.2 us: gate_up(): pl.pallas_call(gate_up_kernel, grid_spec=pltpu.PrefetchScalarGridSpec(num...]
    all_to_all x0 -> x1, blocking collectives: none -> 16.9 us  [body(): head_parts = lax.all_to_all(packed, 'ctx', 0, 0, tiled=True)]
  transfers between devices with their start and end apart: 3 -> 19, of which waited for: 2 -> 11; matrix products, arithmetic and copies ran while one was open for 3% -> 29% of each run, Pallas kernels for 0% -> 2%
where the time goes in v1:
time: 155 us; the launch traced here: 153 us
  local copies, waits for them, and re-layouts  39.6 us (26%)
  starting transfers between devices  32.6 us (21%)
  waiting for transfers between devices  24 us (15%)
  Pallas kernels  17.7 us (11%)
  blocking collectives  16.9 us (11%)
  matrix products  10.7 us (7%)
  other arithmetic  10.5 us (7%)
    unnamed x14, local copies, waits for them, and re-layouts  30.8 us
    ppermute x17, starting transfers between devices, move(): return lax.ppermute(a, ALL, shifted(axes, k % 4 if axes is not CORE else 1))  21.3 us
    ppermute x17, waiting for transfers between devices, move(): return lax.ppermute(a, ALL, shifted(axes, k % 4 if axes is not CORE else 1))  17.8 us
    all_to_all x1, blocking collectives, body(): head_parts = lax.all_to_all(packed, 'ctx', 0, 0, tiled=True)  16.9 us
    pallas_call x1, Pallas kernels, gate_up(): pl.pallas_call(gate_up_kernel, grid_spec=pltpu.PrefetchScalarGridSpec(num...  12.2 us
    all_to_all x1, starting transfers between devices, body(): lax.all_to_all(sent, ALL, 0, 0, axis_index_groups=COLUMNS, tiled=True)  6.81 us
    pallas_call x2, Pallas kernels, down(): pl.pallas_call(functools.partial(down_kernel, turn), grid_spec=pltpu.Pref...  5.46 us
    all_to_all x1, waiting for transfers between devices, body(): lax.all_to_all(column.reshape(8, 4, HALF), ALL, 0, 0, axis_index_groups=C...  5.3 us
  transfers between devices with their start and end apart: 19, of which 11 were waited for; matrix products, arithmetic and copies ran while one was open for 29% of the time, Pallas kernels for 2%

profile of v1, /device:TPU:1, one launch (start us, length us, event | category | flops | bytes accessed | tf_op | source)
XLA Modules:
  0.0 153.1 jit_solution(12114040766132530031)
XLA Ops:
  0.7 1.2 convert_reduce_fusion
  1.9 0.7 convert_convert_fusion
  2.6 0.8 reduce_sum.204
  3.4 0.8 fusion.54
  4.1 0.8 reshape.197
  5.2 0.7 broadcast_in_dim.138
  5.9 6.8 %all-to-all-start = ((bf16[8,4,3200]{2,1,0:T(4,128)(2,1)}), bf16[8,4,3200]{2,1,0:T(4,128)(2,1)S(1)}, u32[]{:S(2)}, u32[]{:S(2)}) async-start(bf16[8,4,3200]{2,1,0:T(4,128)(2,1)} %bitcast.1), calls=%async_computation | async-start | bytes 409600 | tf_op jit(solution)/shard_map/all_to_all | solution.py:230
  12.7 0.8 reshape.200
  13.5 0.7 reshape.213
  14.2 0.7 broadcast_compare_fusion
  15.0 1.5 select_reduce_fusion.8
  17.8 0.9 all-to-all-done
  18.7 2.5 %collective-permute-start.2 = (bf16[32,3200]{1,0:T(8,128)(2,1)S(1)}, bf16[32,3200]{1,0:T(8,128)(2,1)S(1)}, u32[]{:S(2)}, u32[]{:S(2)}) collective-permute-start(bf16[32,3200]{1,0:T(8,128)(2,1)S(1)} %reshape.199), channel_id=1, source_target_pairs={{0,48},{1,7},{2,50},{3,1},{4,52},{5,3},{6,54},{7,5},{8,56},{9,15},... | collective-permute-start | bytes 614408 | tf_op jit(solution)/shard_map/ppermute | solution.py:53
  21.3 0.5 collective-permute-start.1
  21.8 0.6 collective-permute-start
  22.6 11.9 %copy.145 = bf16[1,6144,672]{2,1,0:T(8,128)(2,1)} copy(bf16[1,6144,672]{1,2,0:T(8,128)(2,1)} %param.21) | data formatting | bytes 16515072 | tf_op args[9]
  34.5 11.8 %copy.146 = bf16[1,6144,672]{2,1,0:T(8,128)(2,1)} copy(bf16[1,6144,672]{1,2,0:T(8,128)(2,1)} %param.22) | data formatting | bytes 16515072 | tf_op args[10]
  46.4 1.4 collective-permute-start.4
  47.7 2.6 %collective-permute-start.3 = (bf16[128,3200]{1,0:T(8,128)(2,1)S(1)}, bf16[128,3200]{1,0:T(8,128)(2,1)}, u32[]{:S(2)}, u32[]{:S(2)}) collective-permute-start(bf16[128,3200]{1,0:T(8,128)(2,1)S(1)} %pad_maximum_fusion), channel_id=1, source_target_pairs={{0,4},{1,33},{2,6},{3,35},{4,0},{5,37},{6,2},{7,39},{8,12},{9,41},... | collective-permute-start | bytes 2457608 | tf_op jit(solution)/shard_map/ppermute | solution.py:53
  50.3 1.1 collective-permute-start.5
  51.5 0.3 fusion.33
  52.0 0.4 convolution_convert_fusion.7
  52.3 0.8 fusion.80
  53.1 2.6 %collective-permute-start.6 = (bf16[64,3072]{1,0:T(8,128)(2,1)}, bf16[64,3072]{1,0:T(8,128)(2,1)S(1)}, u32[]{:S(2)}, u32[]{:S(2)}) collective-permute-start(bf16[64,3072]{1,0:T(8,128)(2,1)} %get-tuple-element.53), channel_id=1, source_target_pairs={{0,1},{1,0},{2,3},{3,2},{4,5},{5,4},{6,7},{7,6},{8,9},{9,8},{10,11... | collective-permute-start | bytes 1179656 | tf_op jit(solution)/shard_map/ppermute | solution.py:53
  55.9 3.4 %collective-permute-done.4 = bf16[128,3200]{1,0:T(8,128)(2,1)} collective-permute-done((bf16[128,3200]{1,0:T(8,128)(2,1)S(1)}, bf16[128,3200]{1,0:T(8,128)(2,1)}, u32[]{:S(2)}, u32[]{:S(2)}) %collective-permute-start.4) | collective-permute-done | bytes 819232 | tf_op jit(solution)/shard_map/ppermute | solution.py:53
  59.3 0.8 slice_convert_fusion.1
  60.6 1.5 convolution_convert_fusion.6
  62.1 0.8 fusion.79
  62.9 6.3 %collective-permute-done.3 = bf16[128,3200]{1,0:T(8,128)(2,1)} collective-permute-done((bf16[128,3200]{1,0:T(8,128)(2,1)S(1)}, bf16[128,3200]{1,0:T(8,128)(2,1)}, u32[]{:S(2)}, u32[]{:S(2)}) %collective-permute-start.3) | collective-permute-done | bytes 819232 | tf_op jit(solution)/shard_map/ppermute | solution.py:53
  69.2 0.8 slice_convert_fusion.2
  70.6 1.5 convolution_convert_fusion.5
  72.1 0.8 fusion.78
  73.4 0.4 convolution_convert_fusion.4
  73.8 0.8 fusion.77
  74.6 2.6 %collective-permute-start.7 = (bf16[64,3072]{1,0:T(8,128)(2,1)}, bf16[64,3072]{1,0:T(8,128)(2,1)S(1)}, u32[]{:S(2)}, u32[]{:S(2)}) collective-permute-start(bf16[64,3072]{1,0:T(8,128)(2,1)} %get-tuple-element.51), channel_id=1, source_target_pairs={{0,1},{1,0},{2,3},{3,2},{4,5},{5,4},{6,7},{7,6},{8,9},{9,8},{10,11... | collective-permute-start | bytes 1179656 | tf_op jit(solution)/shard_map/ppermute | solution.py:53
  77.2 0.5 collective-permute-start.9
  78.3 0.5 collective-permute-done.7.refs_5_
  78.7 0.6 collective-permute-done.8.refs_6_
  79.3 0.6 collective-permute-done.9.refs_7_
  79.9 3.7 %copy-done.2 = bf16[1,6144,672]{2,1,0:T(8,128)(2,1)S(1)} copy-done((bf16[1,6144,672]{2,1,0:T(8,128)(2,1)S(1)}, bf16[1,6144,672]{2,1,0:T(8,128)(2,1)}, u32[]{:S(2)}) %copy-start.2) | copy-done | bytes 8257560
  83.5 12.2 %gate_up.1.hidden = bf16[256,672]{1,0:T(8,128)(2,1)S(1)} custom-call(s32[1]{0:T(128)} %bitcast.12.core_ref.half_ref, bf16[64,3072]{1,0:T(8,128)(2,1)S(1)} %get-tuple-element.54.refs_0_, bf16[64,3072]{1,0:T(8,128)(2,1)S(1)} %get-tuple-element.52.refs_1_, bf16[64,3072]{1,0:T(8,128)(2,1)S(1)} %get-tuple-element.50.refs_2_, ...), custom_call_target="tpu_custom_call" | custom-call | flops 4227858432 | bytes 19660800 | tf_op jit(solution)/shard_map/gate_up/pallas_call | solution.py:92
  95.8 3.3 %copy-done.3 = bf16[1,672,6144]{2,1,0:T(8,128)(2,1)S(1)} copy-done((bf16[1,672,6144]{2,1,0:T(8,128)(2,1)S(1)}, bf16[1,672,6144]{2,1,0:T(8,128)(2,1)}, u32[]{:S(2)}) %copy-start.3) | copy-done | bytes 8257560
  99.1 2.7 %down.3 = bf16[256,3072]{1,0:T(8,128)(2,1)S(1)} custom-call(s32[1]{0:T(128)S(6)} %sub.86.half_ref, bf16[256,672]{1,0:T(8,128)(2,1)S(1)} %gate_up.1.hidden, bf16[672,6144]{1,0:T(8,128)(2,1)S(1)} %bitcast.70, f32[256,1]{1,0:T(8,128)S(1)} %copy.151.share), custom_call_target="tpu_custom_call" | custom-call | flops 1056964608 | bytes 5701632 | tf_op jit(solution)/shard_map/down/pallas_call | solution.py:117
  101.8 0.5 collective-permute-start.10
  102.3 2.7 %down.2 = bf16[256,3072]{1,0:T(8,128)(2,1)S(1)} custom-call(s32[1]{0:T(128)} %bitcast.12.core_ref.half_ref, bf16[256,672]{1,0:T(8,128)(2,1)S(1)} %gate_up.1.hidden, bf16[672,6144]{1,0:T(8,128)(2,1)S(1)} %bitcast.71, f32[256,1]{1,0:T(8,128)S(1)} %copy.151.share), custom_call_target="tpu_custom_call" | custom-call | flops 1056964608 | bytes 5701632 | tf_op jit(solution)/shard_map/down/pallas_call | solution.py:117
  105.4 0.4 convolution_convert_fusion.1
  105.9 1.9 %collective-permute-start.13 = (bf16[128,3072]{1,0:T(8,128)(2,1)S(1)}, bf16[128,3072]{1,0:T(8,128)(2,1)}, u32[]{:S(2)}, u32[]{:S(2)}) collective-permute-start(bf16[128,3072]{1,0:T(8,128)(2,1)S(1)} %convolution_convert_fusion.1), channel_id=1, source_target_pairs={{0,2},{1,17},{2,4},{3,19},{4,6},{5,21},{6,0},{7,23},{8,10},{9,25},... | collective-permute-start | bytes 2359304 | tf_op jit(solution)/shard_map/ppermute | solution.py:53
  107.7 1.3 convolution_convert_fusion.2
  109.0 1.1 collective-permute-start.12
  110.1 1.3 convolution_convert_fusion.3
  111.4 0.7 collective-permute-start.11
  112.1 16.9 %all_to_all.15 = bf16[8,12,256]{2,1,0:T(8,128)(2,1)S(1)} all-to-all(bf16[8,12,256]{2,1,0:T(8,128)(2,1)S(1)} %copy.126), channel_id=1, replica_groups=mesh['ctx'=8,'grp'=16] {'ctx'}, dimensions={0} | all-to-all | bytes 98304 | tf_op jit(solution)/shard_map/all_to_all | solution.py:237
  129.0 0.4 copy.127
  129.9 2.2 %add_convert_fusion = bf16[128,3072]{1,0:T(8,128)(2,1)S(1)} fusion(bf16[128,3072]{1,0:T(8,128)(2,1)} %collective-permute-done.13, bf16[128,3072]{1,0:T(8,128)(2,1)} %collective-permute-done.12, bf16[128,3072]{1,0:T(8,128)(2,1)} %collective-permute-done.11, bf16[64,3072]{1,0:T(8,128)(2,1)S(1)} %get-tuple-element.40, ...), kind=kOutput, calls=%fused_computation.9 | convolution fusion | flops 105791488 | bytes 3948544 | tf_op jit(solution)/shard_map/dot_general | solution.py:260
  132.1 0.6 collective-permute-start.16
  132.7 2.1 %collective-permute-start.15 = (bf16[32,3072]{1,0:T(8,128)(2,1)S(1)}, bf16[32,3072]{1,0:T(8,128)(2,1)S(1)}, u32[]{:S(2)}, u32[]{:S(2)}) collective-permute-start(bf16[32,3072]{1,0:T(8,128)(2,1)S(1)} %get-tuple-element.46), channel_id=1, source_target_pairs={{0,48},{1,7},{2,50},{3,1},{4,52},{5,3},{6,54},{7,5},{8,56},{9,15},... | collective-permute-start | bytes 589832 | tf_op jit(solution)/shard_map/ppermute | solution.py:53
  134.9 3.2 %collective-permute-done.16 = bf16[32,3072]{1,0:T(8,128)(2,1)S(1)} collective-permute-done((bf16[32,3072]{1,0:T(8,128)(2,1)S(1)}, bf16[32,3072]{1,0:T(8,128)(2,1)S(1)}, u32[]{:S(2)}, u32[]{:S(2)}) %collective-permute-start.16) | collective-permute-done | bytes 196640 | tf_op jit(solution)/shard_map/ppermute | solution.py:53
  138.1 1.5 collective-permute-done.15
  139.6 1.6 %collective-permute-done.14 = bf16[32,3072]{1,0:T(8,128)(2,1)S(1)} collective-permute-done((bf16[32,3072]{1,0:T(8,128)(2,1)S(1)}, bf16[32,3072]{1,0:T(8,128)(2,1)S(1)}, u32[]{:S(2)}, u32[]{:S(2)}) %collective-permute-start.14) | collective-permute-done | bytes 196640 | tf_op jit(solution)/shard_map/ppermute | solution.py:53
  141.3 0.8 reshape.206
  142.0 4.4 %all-to-all-start.2 = ((bf16[8,4,3072]{2,1,0:T(4,128)(2,1)}), bf16[8,4,3072]{2,1,0:T(4,128)(2,1)S(1)}, u32[]{:S(2)}, u32[]{:S(2)}) async-start(bf16[8,4,3072]{2,1,0:T(4,128)(2,1)} %reshape.206), calls=%async_computation.2 | async-start | bytes 393216 | tf_op jit(solution)/shard_map/all_to_all | solution.py:271
  146.5 0.6 fusion.47
  147.1 5.3 %all-to-all-done.2 = bf16[8,4,3072]{2,1,0:T(4,128)(2,1)S(1)} async-done(((bf16[8,4,3072]{2,1,0:T(4,128)(2,1)}), bf16[8,4,3072]{2,1,0:T(4,128)(2,1)S(1)}, u32[]{:S(2)}, u32[]{:S(2)}) %all-to-all-start.2) | async-done | bytes 196640 | tf_op jit(solution)/shard_map/all_to_all | solution.py:271
  152.4 0.7 reduce_sum.225
  (93 shorter events, 5.4 us)
Async XLA Ops:
  0.6 16.8 %copy-start = (bf16[2,128,1024]{2,1,0:T(8,128)(2,1)S(1)}, bf16[2,128,1024]{2,1,0:T(8,128)(2,1)}, u32[]{:S(2)}) copy-start(bf16[2,128,1024]{2,1,0:T(8,128)(2,1)} %param.14) | copy-start | bytes 1572868
  0.6 16.8 %copy-start.4 = (bf16[2,1024]{1,0:T(2,128)(2,1)S(1)}, bf16[2,1024]{1,0:T(2,128)(2,1)}, u32[]{:S(2)}) copy-start(bf16[2,1024]{1,0:T(2,128)(2,1)} %param.16) | copy-start | bytes 12292
  5.9 12.8 %all-to-all-start = ((bf16[8,4,3200]{2,1,0:T(4,128)(2,1)}), bf16[8,4,3200]{2,1,0:T(4,128)(2,1)S(1)}, u32[]{:S(2)}, u32[]{:S(2)}) async-start(bf16[8,4,3200]{2,1,0:T(4,128)(2,1)} %bitcast.1), calls=%async_computation | async-start | bytes 409600 | tf_op jit(solution)/shard_map/all_to_all | solution.py:230
  18.7 27.5 %collective-permute-start.2 = (bf16[32,3200]{1,0:T(8,128)(2,1)S(1)}, bf16[32,3200]{1,0:T(8,128)(2,1)S(1)}, u32[]{:S(2)}, u32[]{:S(2)}) collective-permute-start(bf16[32,3200]{1,0:T(8,128)(2,1)S(1)} %reshape.199), channel_id=1, source_target_pairs={{0,48},{1,7},{2,50},{3,1},{4,52},{5,3},{6,54},{7,5},{8,56},{9,15},... | collective-permute-start | bytes 614408 | tf_op jit(solution)/shard_map/ppermute | solution.py:53
  21.3 25.0 %collective-permute-start.1 = (bf16[32,3200]{1,0:T(8,128)(2,1)S(1)}, bf16[32,3200]{1,0:T(8,128)(2,1)S(1)}, u32[]{:S(2)}, u32[]{:S(2)}) collective-permute-start(bf16[32,3200]{1,0:T(8,128)(2,1)S(1)} %reshape.199), channel_id=1, source_target_pairs={{0,32},{1,5},{2,34},{3,7},{4,36},{5,1},{6,38},{7,3},{8,40},{9,13},... | collective-permute-start | bytes 614408 | tf_op jit(solution)/shard_map/ppermute | solution.py:53
  21.8 24.5 %collective-permute-start = (bf16[32,3200]{1,0:T(8,128)(2,1)S(1)}, bf16[32,3200]{1,0:T(8,128)(2,1)S(1)}, u32[]{:S(2)}, u32[]{:S(2)}) collective-permute-start(bf16[32,3200]{1,0:T(8,128)(2,1)S(1)} %reshape.199), channel_id=1, source_target_pairs={{0,16},{1,3},{2,18},{3,5},{4,20},{5,7},{6,22},{7,1},{8,24},{9,11},... | collective-permute-start | bytes 614408 | tf_op jit(solution)/shard_map/ppermute | solution.py:53
  46.4 12.9 %collective-permute-start.4 = (bf16[128,3200]{1,0:T(8,128)(2,1)S(1)}, bf16[128,3200]{1,0:T(8,128)(2,1)}, u32[]{:S(2)}, u32[]{:S(2)}) collective-permute-start(bf16[128,3200]{1,0:T(8,128)(2,1)S(1)} %pad_maximum_fusion), channel_id=1, source_target_pairs={{0,2},{1,17},{2,4},{3,19},{4,6},{5,21},{6,0},{7,23},{8,10},{9,25},... | collective-permute-start | bytes 2457608 | tf_op jit(solution)/shard_map/ppermute | solution.py:53
  47.7 21.5 %collective-permute-start.3 = (bf16[128,3200]{1,0:T(8,128)(2,1)S(1)}, bf16[128,3200]{1,0:T(8,128)(2,1)}, u32[]{:S(2)}, u32[]{:S(2)}) collective-permute-start(bf16[128,3200]{1,0:T(8,128)(2,1)S(1)} %pad_maximum_fusion), channel_id=1, source_target_pairs={{0,4},{1,33},{2,6},{3,35},{4,0},{5,37},{6,2},{7,39},{8,12},{9,41},... | collective-permute-start | bytes 2457608 | tf_op jit(solution)/shard_map/ppermute | solution.py:53
  50.3 22.5 %collective-permute-start.5 = (bf16[128,3200]{1,0:T(8,128)(2,1)S(1)}, bf16[128,3200]{1,0:T(8,128)(2,1)S(1)}, u32[]{:S(2)}, u32[]{:S(2)}) collective-permute-start(bf16[128,3200]{1,0:T(8,128)(2,1)S(1)} %pad_maximum_fusion), channel_id=1, source_target_pairs={{0,6},{1,49},{2,0},{3,51},{4,2},{5,53},{6,4},{7,55},{8,14},{9,57},... | collective-permute-start | bytes 2457608 | tf_op jit(solution)/shard_map/ppermute | solution.py:53
  53.1 25.1 %collective-permute-start.6 = (bf16[64,3072]{1,0:T(8,128)(2,1)}, bf16[64,3072]{1,0:T(8,128)(2,1)S(1)}, u32[]{:S(2)}, u32[]{:S(2)}) collective-permute-start(bf16[64,3072]{1,0:T(8,128)(2,1)} %get-tuple-element.53), channel_id=1, source_target_pairs={{0,1},{1,0},{2,3},{3,2},{4,5},{5,4},{6,7},{7,6},{8,9},{9,8},{10,11... | collective-permute-start | bytes 1179656 | tf_op jit(solution)/shard_map/ppermute | solution.py:53
  74.6 4.1 %collective-permute-start.7 = (bf16[64,3072]{1,0:T(8,128)(2,1)}, bf16[64,3072]{1,0:T(8,128)(2,1)S(1)}, u32[]{:S(2)}, u32[]{:S(2)}) collective-permute-start(bf16[64,3072]{1,0:T(8,128)(2,1)} %get-tuple-element.51), channel_id=1, source_target_pairs={{0,1},{1,0},{2,3},{3,2},{4,5},{5,4},{6,7},{7,6},{8,9},{9,8},{10,11... | collective-permute-start | bytes 1179656 | tf_op jit(solution)/shard_map/ppermute | solution.py:53
  77.2 2.1 %collective-permute-start.8 = (bf16[64,3072]{1,0:T(8,128)(2,1)}, bf16[64,3072]{1,0:T(8,128)(2,1)S(1)}, u32[]{:S(2)}, u32[]{:S(2)}) collective-permute-start(bf16[64,3072]{1,0:T(8,128)(2,1)} %get-tuple-element.49), channel_id=1, source_target_pairs={{0,1},{1,0},{2,3},{3,2},{4,5},{5,4},{6,7},{7,6},{8,9},{9,8},{10,11... | collective-permute-start | bytes 1179656 | tf_op jit(solution)/shard_map/ppermute | solution.py:53
  77.2 2.7 %collective-permute-start.9 = (bf16[64,3072]{1,0:T(8,128)(2,1)}, bf16[64,3072]{1,0:T(8,128)(2,1)S(1)}, u32[]{:S(2)}, u32[]{:S(2)}) collective-permute-start(bf16[64,3072]{1,0:T(8,128)(2,1)} %get-tuple-element.47), channel_id=1, source_target_pairs={{0,1},{1,0},{2,3},{3,2},{4,5},{5,4},{6,7},{7,6},{8,9},{9,8},{10,11... | collective-permute-start | bytes 1179656 | tf_op jit(solution)/shard_map/ppermute | solution.py:53
  79.8 3.7 %copy-start.2 = (bf16[1,6144,672]{2,1,0:T(8,128)(2,1)S(1)}, bf16[1,6144,672]{2,1,0:T(8,128)(2,1)}, u32[]{:S(2)}) copy-start(bf16[1,6144,672]{2,1,0:T(8,128)(2,1)} %copy.145) | copy-start | bytes 24772612
  95.7 3.3 %copy-start.3 = (bf16[1,672,6144]{2,1,0:T(8,128)(2,1)S(1)}, bf16[1,672,6144]{2,1,0:T(8,128)(2,1)}, u32[]{:S(2)}) copy-start(bf16[1,672,6144]{2,1,0:T(8,128)(2,1)} %param.23) | copy-start | bytes 24772612
  101.8 3.5 %collective-permute-start.10 = (bf16[256,3072]{1,0:T(8,128)(2,1)S(1)}, bf16[256,3072]{1,0:T(8,128)(2,1)S(1)}, u32[]{:S(2)}, u32[]{:S(2)}) collective-permute-start(bf16[256,3072]{1,0:T(8,128)(2,1)S(1)} %down.3), channel_id=1, source_target_pairs={{0,1},{1,0},{2,3},{3,2},{4,5},{5,4},{6,7},{7,6},{8,9},{9,8},{10,11... | collective-permute-start | bytes 4718600 | tf_op jit(solution)/shard_map/ppermute | solution.py:53
  105.9 24.0 %collective-permute-start.13 = (bf16[128,3072]{1,0:T(8,128)(2,1)S(1)}, bf16[128,3072]{1,0:T(8,128)(2,1)}, u32[]{:S(2)}, u32[]{:S(2)}) collective-permute-start(bf16[128,3072]{1,0:T(8,128)(2,1)S(1)} %convolution_convert_fusion.1), channel_id=1, source_target_pairs={{0,2},{1,17},{2,4},{3,19},{4,6},{5,21},{6,0},{7,23},{8,10},{9,25},... | collective-permute-start | bytes 2359304 | tf_op jit(solution)/shard_map/ppermute | solution.py:53
  109.0 20.9 %collective-permute-start.12 = (bf16[128,3072]{1,0:T(8,128)(2,1)}, bf16[128,3072]{1,0:T(8,128)(2,1)}, u32[]{:S(2)}, u32[]{:S(2)}) collective-permute-start(bf16[128,3072]{1,0:T(8,128)(2,1)} %convolution_convert_fusion.2), channel_id=1, source_target_pairs={{0,6},{1,49},{2,0},{3,51},{4,2},{5,53},{6,4},{7,55},{8,14},{9,57},... | collective-permute-start | bytes 2359304 | tf_op jit(solution)/shard_map/ppermute | solution.py:53
  111.4 18.5 %collective-permute-start.11 = (bf16[128,3072]{1,0:T(8,128)(2,1)}, bf16[128,3072]{1,0:T(8,128)(2,1)}, u32[]{:S(2)}, u32[]{:S(2)}) collective-permute-start(bf16[128,3072]{1,0:T(8,128)(2,1)} %convolution_convert_fusion.3), channel_id=1, source_target_pairs={{0,4},{1,33},{2,6},{3,35},{4,0},{5,37},{6,2},{7,39},{8,12},{9,41},... | collective-permute-start | bytes 2359304 | tf_op jit(solution)/shard_map/ppermute | solution.py:53
  129.9 23.2 %copy-start.1 = (bf16[2,128,1024]{2,1,0:T(8,128)(2,1)S(1)}, bf16[2,128,1024]{2,1,0:T(8,128)(2,1)}, u32[]{:S(2)}) copy-start(bf16[2,128,1024]{2,1,0:T(8,128)(2,1)} %param.14) | copy-start | bytes 1572868
  132.1 6.0 %collective-permute-start.16 = (bf16[32,3072]{1,0:T(8,128)(2,1)S(1)}, bf16[32,3072]{1,0:T(8,128)(2,1)S(1)}, u32[]{:S(2)}, u32[]{:S(2)}) collective-permute-start(bf16[32,3072]{1,0:T(8,128)(2,1)S(1)} %get-tuple-element.45), channel_id=1, source_target_pairs={{0,16},{1,3},{2,18},{3,5},{4,20},{5,7},{6,22},{7,1},{8,24},{9,11},... | collective-permute-start | bytes 589832 | tf_op jit(solution)/shard_map/ppermute | solution.py:53
  132.7 6.8 %collective-permute-start.15 = (bf16[32,3072]{1,0:T(8,128)(2,1)S(1)}, bf16[32,3072]{1,0:T(8,128)(2,1)S(1)}, u32[]{:S(2)}, u32[]{:S(2)}) collective-permute-start(bf16[32,3072]{1,0:T(8,128)(2,1)S(1)} %get-tuple-element.46), channel_id=1, source_target_pairs={{0,48},{1,7},{2,50},{3,1},{4,52},{5,3},{6,54},{7,5},{8,56},{9,15},... | collective-permute-start | bytes 589832 | tf_op jit(solution)/shard_map/ppermute | solution.py:53
  134.9 6.3 %collective-permute-start.14 = (bf16[32,3072]{1,0:T(8,128)(2,1)S(1)}, bf16[32,3072]{1,0:T(8,128)(2,1)S(1)}, u32[]{:S(2)}, u32[]{:S(2)}) collective-permute-start(bf16[32,3072]{1,0:T(8,128)(2,1)S(1)} %get-tuple-element.44), channel_id=1, source_target_pairs={{0,32},{1,5},{2,34},{3,7},{4,36},{5,1},{6,38},{7,3},{8,40},{9,13},... | collective-permute-start | bytes 589832 | tf_op jit(solution)/shard_map/ppermute | solution.py:53
  142.0 10.3 %all-to-all-start.2 = ((bf16[8,4,3072]{2,1,0:T(4,128)(2,1)}), bf16[8,4,3072]{2,1,0:T(4,128)(2,1)S(1)}, u32[]{:S(2)}, u32[]{:S(2)}) async-start(bf16[8,4,3072]{2,1,0:T(4,128)(2,1)} %reshape.206), calls=%async_computation.2 | async-start | bytes 393216 | tf_op jit(solution)/shard_map/all_to_all | solution.py:271

commit v2 on v0

v2 whole, which is shorter than its diff:
```python
import functools

import jax
import jax.numpy as jnp
from jax import lax
from jax.experimental import pallas as pl
from jax.experimental.pallas import tpu as pltpu
from jax.sharding import PartitionSpec as P

QH = 48
KVH = 8
HD = 128
TOPK = 4
D = 6144
HALF = D // 2
FF = 672
META = 128
OUT = 1
BACK = 2
OUT_WIDE = HALF // OUT
BACK_WIDE = HALF // BACK
KB = 512
OUT_STEPS = OUT_WIDE // KB
BACK_STEPS = BACK_WIDE // KB
ALL = ("ctx", "grp")
BF = jnp.bfloat16
F32 = jnp.float32


def coords(i):
    c, g = divmod(i, 16)
    return {"x": (g >> 1) & 3, "y": c & 3, "z": ((g >> 3) << 1) | (c >> 2), "core": g & 1}


def index(x, y, z, core):
    return (((z & 1) << 2) | y) * 16 + (((z >> 1) << 3) | (x << 1) | core)


def shifted(axes, k):
    pairs = []
    for i in range(128):
        at = coords(i)
        axis = axes[at["core"]]
        at[axis] = (at[axis] + k) % (2 if axis == "core" else 4)
        pairs.append((i, index(**at)))
    return pairs


OUTER = ("x", "y")
INNER = ("y", "x")
CORE = ("core", "core")
COLUMNS = [
    [index(x, y, z, core) for z in range(4) for core in range(2)] for x in range(4) for y in range(4)
]


def move(a, axes, k):
    return lax.ppermute(a, ALL, shifted(axes, k % 4 if axes is not CORE else 1))


def turned(a):
    return a.reshape(4, 4, 16, a.shape[-1]).swapaxes(0, 1).reshape(a.shape)


def call(kernel, outs, *args, name, limit=8, **kw):
    return pl.pallas_call(
        kernel,
        out_shape=outs,
        compiler_params=pltpu.CompilerParams(vmem_limit_bytes=limit << 20),
        cost_estimate=pl.CostEstimate(flops=0, bytes_accessed=0, transcendentals=0),
        name=name,
        **kw,
    )(*args)


VMEM = pl.BlockSpec(memory_space=pltpu.VMEM)
SMEM = pl.BlockSpec(memory_space=pltpu.SMEM)
HBM = pl.BlockSpec(memory_space=pltpu.HBM)


def in_hbm(*arrays):
    return [pltpu.with_memory_space_constraint(a, pltpu.HBM) for a in arrays]


def shape(*dims, dtype=BF):
    return jax.ShapeDtypeStruct(dims, dtype)


def pack_kernel(x_at, routes_at, weights_at, out, x, routes, weights, sems):
    copies = [
        pltpu.make_async_copy(a, b, sems.at[i])
        for i, (a, b) in enumerate(((x_at, x), (routes_at, routes), (weights_at, weights)))
    ]
    for copy in copies:
        copy.start()
    for copy in copies:
        copy.wait()
    row = lax.broadcasted_iota(jnp.int32, (4, TOPK), 0)
    place = lax.broadcasted_iota(jnp.int32, (4, TOPK), 1)
    named = jnp.zeros((4, TOPK), jnp.int32)
    for r in range(4):
        for k in range(TOPK):
            named = jnp.where((row == r) & (place == k), routes[r, k], named)
    code = 2 * named
    for r in range(3):
        for k in range(TOPK):
            code += jnp.where((named == routes[r, k]) & (row > r), 1, 0)
    share = weights[...] / jnp.sum(weights[...], axis=1, keepdims=True)
    high = share.astype(BF).astype(F32)
    middle = (share - high).astype(BF).astype(F32)
    lane = lax.broadcasted_iota(jnp.int32, (4, META), 1)
    meta = jnp.zeros((4, META), F32)
    for j, part in enumerate((code.astype(F32), high, middle, share - high - middle)):
        for k in range(TOPK):
            meta = jnp.where(lane == j * TOPK + k, part[:, k : k + 1], meta)
    meta = meta.astype(BF)
    for target in range(8):
        at = (target % 2) * HALF
        out[target, :, :OUT_WIDE] = x[:, at : at + OUT_WIDE]
        out[target, :, OUT_WIDE : OUT_WIDE + META] = meta
        if OUT > 1:
            out[target, :, OUT_WIDE + META :] = x[:, at + OUT_WIDE : at + HALF]


def pack(x, routes, weights):
    return call(
        pack_kernel,
        shape(8, 4, HALF + META),
        *in_hbm(x, routes, weights),
        name="pack",
        in_specs=[HBM] * 3,
        out_specs=VMEM,
        scratch_shapes=[
            pltpu.VMEM((4, D), BF),
            pltpu.SMEM((4, TOPK), jnp.int32),
            pltpu.VMEM((4, TOPK), F32),
            pltpu.SemaphoreType.DMA((3,)),
        ],
    )


def load_kernel(gate_at, up_at, down_at, gate, up, down, sems):
    parts = 3
    copies = []
    for i, (a, b) in enumerate(((gate_at, gate), (up_at, up), (down_at, down))):
        for p in range(parts):
            rows = pl.ds(p * (FF // parts), FF // parts)
            copies.append(pltpu.make_async_copy(a.at[rows], b.at[rows], sems.at[i, p]))
    for copy in copies:
        copy.start()
    for copy in copies:
        copy.wait()


def load(gate_w, up_w, down_w):
    return call(
        load_kernel,
        [pltpu.VMEM((FF, D), BF)] * 3,
        *in_hbm(gate_w, up_w, down_w),
        name="load",
        in_specs=[HBM] * 3,
        out_specs=[VMEM] * 3,
        scratch_shapes=[pltpu.SemaphoreType.DMA((3, 3))],
    )


def picked(chosen, rows, mine, theirs):
    for at in range(0, OUT_WIDE, KB):
        found = lax.dot_general(
            chosen, rows[:, at : at + KB], (((0,), (0,)), ((), ())), preferred_element_type=F32
        ).astype(BF)
        mine[:, at : at + KB] = found[:64]
        theirs[:, at : at + KB] = found[64:]


def choose_kernel(expert, rows, mine, theirs, chosen, shares):
    meta = rows[:, OUT_WIDE : OUT_WIDE + META].astype(F32)
    row = lax.broadcasted_iota(jnp.int32, (128, 128), 0)
    lane = lax.broadcasted_iota(jnp.int32, (128, 128), 1)
    wanted = 2 * jnp.where(lane < 64, expert[0], expert[0] ^ 1) + lane % 2
    wanted = jnp.where(row // 4 == (lane % 64) // 2, wanted, -1).astype(F32)
    ones = jnp.zeros((128, 128), F32)
    weighted = jnp.zeros((128, 128), F32)
    for k in range(TOPK):
        hit = meta[:, k : k + 1] == wanted
        share = sum(meta[:, j * TOPK + k : j * TOPK + k + 1] for j in (1, 2, 3))
        ones += jnp.where(hit, 1.0, 0.0)
        weighted += jnp.where(hit, share, 0.0)
    chosen[...] = ones.astype(BF)
    shares[...] = jnp.sum(weighted, axis=0, keepdims=True)
    picked(chosen[...], rows, mine, theirs)


def choose(expert, rows):
    return call(
        choose_kernel,
        [shape(64, OUT_WIDE), shape(64, OUT_WIDE), shape(128, 128), shape(1, 128, dtype=F32)],
        expert,
        rows,
        name="choose",
        in_specs=[SMEM, VMEM],
        out_specs=[VMEM] * 4,
    )


def pick_kernel(chosen, rows, mine, theirs):
    picked(chosen[...], rows, mine, theirs)


def pick(chosen, rows):
    return call(
        pick_kernel,
        [shape(64, OUT_WIDE), shape(64, OUT_WIDE)],
        chosen,
        rows,
        name="pick",
    )


def across(weights, rows):
    return lax.dot_general(weights, rows, (((1,), (1,)), ((), ())), preferred_element_type=F32)


def columns_of(half, chunk, wide):
    return pl.ds(pl.multiple_of(half * HALF + chunk * wide, wide), wide)


def own_kernel(chunk, core, *refs):
    own, gate_w, up_w, before, (gate, up) = refs[:4], refs[4], refs[5], refs[6:-2], refs[-2:]
    rows = jnp.concatenate([r[...] for r in own], axis=0)
    here = columns_of(core[0], chunk, OUT_WIDE)
    for out, weights, at in ((gate, gate_w, 0), (up, up_w, 1)):
        found = across(weights[:, here], rows)
        out[...] = found + before[at][...] if before else found


def other_kernel(chunk, peer, *refs):
    rows = turned(jnp.concatenate([r[...] for r in refs[:4]], axis=0))
    gate_w, up_w, gate_at, up_at, share, *outs = refs[4:]
    here = columns_of(peer[0], chunk, OUT_WIDE)
    gate = gate_at[...] + across(gate_w[:, here], rows)
    up = up_at[...] + across(up_w[:, here], rows)
    if chunk < OUT - 1:
        outs[0][...] = gate
        outs[1][...] = up
    else:
        hidden = gate / (1.0 + jnp.exp(-gate)) * up * share[...]
        outs[0][...] = hidden.T.astype(BF)


def gate_up(core, peer, chunk, own, other, gate_w, up_w, before, share):
    sums = [shape(FF, 256, dtype=F32)] * 2
    args = [core, *own, gate_w, up_w, *before]
    sums = call(
        functools.partial(own_kernel, chunk),
        sums,
        *args,
        name="gate_up_own",
        in_specs=[SMEM] + [VMEM] * (len(args) - 1),
        out_specs=[VMEM] * 2,
    )
    args = [peer, *other, gate_w, up_w, *sums, share]
    last = chunk == OUT - 1
    return call(
        functools.partial(other_kernel, chunk),
        shape(256, FF) if last else [shape(FF, 256, dtype=F32)] * 2,
        *args,
        name="gate_up_other",
        in_specs=[SMEM] + [VMEM] * (len(args) - 1),
        out_specs=VMEM if last else [VMEM] * 2,
    )


def down_kernel(chunk, turn, half, hidden, weights, out):
    here = columns_of(half[0], chunk, BACK_WIDE)
    rows = jnp.dot(hidden[...], weights[:, here], preferred_element_type=F32).astype(BF)
    out[...] = turned(rows) if turn else rows


def down(half, chunk, hidden, weights, turn):
    return call(
        functools.partial(down_kernel, chunk, turn),
        shape(256, BACK_WIDE),
        half,
        hidden,
        weights,
        name="down",
        in_specs=[SMEM, VMEM, VMEM],
        out_specs=VMEM,
    )


def give_kernel(chosen, mine, theirs, out):
    for at in range(0, BACK_WIDE, KB):
        rows = jnp.concatenate([mine[:, at : at + KB], theirs[:, at : at + KB]], axis=0)
        out[:, at : at + KB] = jnp.dot(chosen[...], rows, preferred_element_type=F32).astype(BF)


def give(chosen, mine, theirs, k):
    slots = pl.BlockSpec((64, BACK_WIDE), lambda i: (k, 0))
    return call(
        give_kernel,
        shape(128, BACK_WIDE),
        chosen,
        mine,
        theirs,
        name="give",
        grid=(1,),
        in_specs=[pl.BlockSpec((128, 128), lambda i: (0, 0)), slots, slots],
        out_specs=pl.BlockSpec((128, BACK_WIDE), lambda i: (0, 0)),
    )


def join_kernel(chosen, *refs):
    parts, outs = refs[:-4], refs[-4:]
    for c in range(BACK):
        mine, theirs, *arrived = parts[5 * c : 5 * c + 5]
        for at in range(0, BACK_WIDE, KB):
            here = slice(at, at + KB)
            rows = jnp.concatenate([mine[:, here], theirs[:, here]], axis=0)
            rows = jnp.dot(chosen[...], rows, preferred_element_type=F32)
            for part in arrived:
                rows += part[:, here].astype(F32)
            rows = rows.astype(BF)
            there = slice(c * BACK_WIDE + at, c * BACK_WIDE + at + KB)
            for k in range(4):
                outs[k][:, there] = rows[32 * k : 32 * k + 32]


def join(chosen, parts):
    slots = pl.BlockSpec((64, BACK_WIDE), lambda i: (0, 0))
    rows = pl.BlockSpec((128, BACK_WIDE), lambda i: (0, 0))
    return call(
        join_kernel,
        [shape(32, HALF)] * 4,
        chosen,
        *parts,
        name="join",
        grid=(1,),
        in_specs=[pl.BlockSpec((128, 128), lambda i: (0, 0))] + [slots, slots, rows, rows, rows] * BACK,
        out_specs=[pl.BlockSpec((32, HALF), lambda i: (0, 0))] * 4,
    )


def column_kernel(*refs):
    parts, out = refs[:-1], refs[-1]
    rows = sum(p[...].astype(F32) for p in parts).astype(BF)
    for target in range(8):
        out[target] = rows[4 * target : 4 * target + 4]


def last_kernel(parts, out):
    for core in range(2):
        rows = sum(parts[2 * z + core].astype(F32) for z in range(4))
        out[:, core * HALF : (core + 1) * HALF] = rows.astype(BF)


def attend_kernel(place, lengths_at, *refs):
    given, out, held, sems = refs[:5], refs[5], refs[6:12], refs[12]
    copies = [
        pltpu.make_async_copy(a, b, sems.at[i]) for i, (a, b) in enumerate(zip((lengths_at,) + given, held))
    ]
    for copy in copies:
        copy.start()
    for copy in copies:
        copy.wait()
    lengths, queries, keys, values, new_key, new_value = held
    group = QH // KVH
    local = keys.shape[1]
    leader = place[0] == 0
    position = place[0] * local + lax.broadcasted_iota(jnp.int32, (group, local), 1)
    lane = lax.broadcasted_iota(jnp.int32, (group, HD), 1)
    out[...] = jnp.zeros_like(out)
    for r in range(2):
        live = position < lengths[r]
        for j in range(KVH):
            head = slice(j * HD, (j + 1) * HD)
            q = queries[r, j]
            scores = across(q, keys[r, :, head]) * HD ** (-0.5)
            own = jnp.sum(
                q.astype(F32) * new_key[r : r + 1, head].astype(F32), axis=1, keepdims=True
            ) * HD ** (-0.5)
            top = jnp.max(jnp.where(live, scores, -1e30), axis=1, keepdims=True)
            top = jnp.where(leader, jnp.maximum(top, own), top)
            top = top.astype(BF).astype(F32)
            weights = jnp.where(live, jnp.exp(scores - top), 0.0)
            own = jnp.where(leader, jnp.exp(own - top), 0.0)
            total = jnp.sum(weights, axis=1, keepdims=True) + own
            high = weights.astype(BF)
            low = (weights - high.astype(F32)).astype(BF)
            value = values[r, :, head]
            mixed = jnp.dot(high, value, preferred_element_type=F32)
            mixed += jnp.dot(low, value, preferred_element_type=F32)
            mixed += own * new_value[r : r + 1, head].astype(F32)
            total_high = total.astype(BF).astype(F32)
            stats = jnp.where(lane == 0, top, jnp.where(lane == 1, total_high, total - total_high))
            out[j, 8 * r : 8 * r + group, :HD] = mixed.astype(BF)
            out[j, 8 * r : 8 * r + group, HD:] = stats.astype(BF)


def attend(queries, key_cache, value_cache, new_key, new_value, lengths):
    place = lax.axis_index("ctx").astype(jnp.int32).reshape(1)
    queries = queries.reshape(2, KVH, QH // KVH, HD)
    return call(
        attend_kernel,
        shape(KVH, 16, 2 * HD),
        place,
        *in_hbm(lengths, queries, key_cache, value_cache, new_key, new_value),
        name="attend",
        in_specs=[SMEM] + [HBM] * 6,
        out_specs=VMEM,
        scratch_shapes=[pltpu.SMEM((2,), jnp.int32)]
        + [pltpu.VMEM(a.shape, a.dtype) for a in (queries, key_cache, value_cache, new_key, new_value)]
        + [pltpu.SemaphoreType.DMA((6,))],
    )


def heads_kernel(parts, out):
    group = QH // KVH
    tops = [parts[s, :, HD : HD + 1].astype(F32) for s in range(KVH)]
    peak = functools.reduce(jnp.maximum, tops)
    mixed = jnp.zeros((16, HD), F32)
    total = jnp.zeros((16, 1), F32)
    for s in range(KVH):
        scale = jnp.exp(tops[s] - peak)
        mixed += scale * parts[s, :, :HD].astype(F32)
        total += scale * sum(parts[s, :, HD + i : HD + i + 1].astype(F32) for i in (1, 2))
    mixed = (mixed / total).astype(BF)
    for r in range(2):
        for g in range(group):
            out[r : r + 1, g * HD : (g + 1) * HD] = mixed[8 * r + g : 8 * r + g + 1]


def body(
    queries,
    key_cache,
    value_cache,
    new_key,
    new_value,
    lengths,
    moe_input,
    routes,
    route_weights,
    w_gate,
    w_up,
    w_down,
):
    expert = (lax.axis_index("grp") & 15).astype(jnp.int32)
    core = (expert & 1).reshape(1)
    expert = expert.reshape(1)

    packed = attend(queries, key_cache, value_cache, new_key, new_value, lengths)
    sent = pack(moe_input, routes, route_weights)
    column = lax.all_to_all(sent, ALL, 0, 0, axis_index_groups=COLUMNS, tiled=True)
    column, packed = lax.optimization_barrier((column, packed))
    column = column.reshape(32, HALF + META)
    head_parts = lax.all_to_all(packed, "ctx", 0, 0, tiled=True)
    plane = jnp.concatenate([column] + [move(column, INNER, k) for k in (1, 2, 3)], axis=0)
    cuts = [0] + [OUT_WIDE * (c + 1) + META for c in range(OUT)]
    planes = [plane[:, cuts[c] : cuts[c + 1]] for c in range(OUT)]

    weights = (w_gate[0].T, w_up[0].T, w_down[0])
    planes[0], head_parts, weights, expert, core, peer = lax.optimization_barrier(
        (planes[0], head_parts, weights, expert, core, 1 - core)
    )
    shards = [[p] + [move(p, OUTER, k) for k in (1, 2, 3)] for p in planes]
    gate_w, up_w, down_w = load(*weights)
    head_outputs = call(heads_kernel, shape(2, HD * QH // KVH), head_parts, name="heads")
    shards[-1][2], head_outputs, gate_w = lax.optimization_barrier(
        (shards[-1][2], head_outputs, gate_w)
    )

    chosen, shares, sums = [None] * 4, [None] * 4, ()
    for c in range(OUT):
        own, other = [None] * 4, [None] * 4
        for k in (0, 1, 3, 2):
            if c == 0:
                own[k], theirs, chosen[k], shares[k] = choose(expert, shards[c][k])
            else:
                own[k], theirs = pick(chosen[k], shards[c][k])
            other[k] = move(theirs, CORE, 1)
        share = jnp.concatenate([s[:, :64] for s in shares], axis=1)
        sums = gate_up(core, peer, c, own, other, gate_w, up_w, sums, share)
    hidden = sums

    parts = []
    for c in range(BACK):
        theirs = move(down(peer, c, hidden, down_w, True), CORE, 1)
        mine = down(core, c, hidden, down_w, False)
        parts += [mine, theirs]
        parts += [move(give(chosen[k], mine, theirs, k), OUTER, -k) for k in (2, 1, 3)]
    pieces = join(chosen[0], parts)
    pieces = [pieces[0]] + [move(pieces[k], INNER, -k) for k in (2, 1, 3)]
    column = call(column_kernel, shape(8, 4, HALF), *pieces, name="column")
    parts = lax.all_to_all(column, ALL, 0, 0, axis_index_groups=COLUMNS, tiled=True)
    return head_outputs, call(last_kernel, shape(4, D), parts, name="last")


def solution(mesh):
    placed = (
        P("grp", None),
        P("grp", "ctx", None),
        P("grp", "ctx", None),
        P("grp", None),
        P("grp", None),
        P("grp"),
        P(ALL, None),
        P(ALL, None),
        P(ALL, None),
        P("grp", None, "ctx"),
        P("grp", None, "ctx"),
        P("grp", "ctx", None),
    )
    return jax.shard_map(
        body,
        mesh=mesh,
        in_specs=placed,
        out_specs=(P("grp", "ctx"), P(ALL, None)),
        check_vma=False,
    )
```

time: 220 us -> 109 us (0.50)
  blocking collectives: 68.7 us -> 12.5 us
  matrix products: 27.5 us -> 0 us
  Pallas kernels: 0 us -> 26.4 us
  waiting for transfers between devices: 50.3 us -> 26.5 us
  local copies, waits for them, and re-layouts: 22.1 us -> 1.43 us
  between operations: 14.2 us -> 0.87 us
  starting transfers between devices: 33.6 us -> 41 us
  other arithmetic: 2.71 us -> 0.14 us
    all_gather x3 -> x0, blocking collectives: 68.7 us -> none  [merged(): lax.all_gather(a.astype(kind), axis)]
    all_to_all x2, waiting for transfers between devices: 50.2 us -> 3.75 us  [the longest x1 1.95 us: body(): head_parts = lax.all_to_all(packed, 'ctx', 0, 0, tiled=True)]
    ppermute x0 -> x21, starting transfers between devices: none -> 30 us  [move(): return lax.ppermute(a, ALL, shifted(axes, k % 4 if axes is not CORE else 1))]
    dot_general x8 -> x0, matrix products: 27.5 us -> none  [the longest x1 17.5 us: body(): jnp.dot(hidden, down_w, preferred_element_type=jnp.float32)]
    pallas_call x0 -> x23, Pallas kernels: none -> 26.4 us  [call(): pl.pallas_call(kernel, out_shape=outs, compiler_params=pltpu.CompilerPara...]
    ppermute x0 -> x21, waiting for transfers between devices: none -> 22.8 us  [move(): return lax.ppermute(a, ALL, shifted(axes, k % 4 if axes is not CORE else 1))]
    all_to_all x2, starting transfers between devices: 33.4 us -> 11 us  [the longest x1 6.83 us: body(): lax.all_to_all(sent, ALL, 0, 0, axis_index_groups=COLUMNS, tiled=True)]
    all_to_all x4 -> x0, local copies, waits for them, and re-layouts: 16.5 us -> none  [the longest x2 14.4 us: body(): lax.all_to_all(widened, ('ctx', 'grp'), split_axis=0, concat_axis=0, tile...]
  transfers between devices with their start and end apart: 3 -> 23, of which waited for: 2 -> 14; matrix products, arithmetic and copies ran while one was open for 3% -> 1% of each run, Pallas kernels for 0% -> 18%
where the time goes in v2:
time: 109 us
  starting transfers between devices  41 us (38%)
  waiting for transfers between devices  26.5 us (24%)
  Pallas kernels  26.4 us (24%)
  blocking collectives  12.5 us (11%)
  local copies, waits for them, and re-layouts  1.43 us (1%)
    ppermute x21, starting transfers between devices, move(): return lax.ppermute(a, ALL, shifted(axes, k % 4 if axes is not CORE else 1))  30 us
    pallas_call x23, Pallas kernels, call(): pl.pallas_call(kernel, out_shape=outs, compiler_params=pltpu.CompilerPara...  26.4 us
    ppermute x21, waiting for transfers between devices, move(): return lax.ppermute(a, ALL, shifted(axes, k % 4 if axes is not CORE else 1))  22.8 us
    all_to_all x1, blocking collectives, body(): lax.all_to_all(column, ALL, 0, 0, axis_index_groups=COLUMNS, tiled=True)  12.5 us
    all_to_all x1, starting transfers between devices, body(): lax.all_to_all(sent, ALL, 0, 0, axis_index_groups=COLUMNS, tiled=True)  6.83 us
    all_to_all x1, starting transfers between devices, body(): head_parts = lax.all_to_all(packed, 'ctx', 0, 0, tiled=True)  4.19 us
  transfers between devices with their start and end apart: 23, of which 14 were waited for; matrix products, arithmetic and copies ran while one was open for 1% of the time, Pallas kernels for 18%

profile of v2, /device:TPU:1, one launch (start us, length us, event | category | flops | bytes accessed | tf_op | source)
XLA Modules:
  0.0 108.9 jit_solution(5178871026596431909)
XLA Ops:
  0.6 1.7 %pack.1 = bf16[8,4,3200]{2,1,0:T(4,128)(2,1)} custom-call(bf16[4,6144]{1,0:T(4,128)(2,1)} %x_at.1, s32[4,4]{1,0:T(4,128)} %routes_at.1, f32[4,4]{1,0:T(4,128)} %weights_at.1), custom_call_target="tpu_custom_call" | custom-call | tf_op jit(solution)/shard_map/pack/pallas_call | solution.py:66
  2.3 6.8 %all-to-all-start = ((bf16[8,4,3200]{2,1,0:T(4,128)(2,1)}), bf16[8,4,3200]{2,1,0:T(4,128)(2,1)S(1)}, u32[]{:S(2)}, u32[]{:S(2)}) async-start(bf16[8,4,3200]{2,1,0:T(4,128)(2,1)} %pack.1), calls=%async_computation | async-start | bytes 409600 | tf_op jit(solution)/shard_map/all_to_all | solution.py:454
  9.2 1.4 %reshape.20.refs_0_ = bf16[2,8,6,128]{3,2,1,0:T(8,128)(2,1)} reshape(bf16[2,6144]{1,0:T(2,128)(2,1)} %param.12) | data formatting | bytes 49152 | tf_op jit(solution)/shard_map/reshape | solution.py:403
  10.5 2.8 %attend.1 = bf16[8,16,256]{2,1,0:T(8,128)(2,1)} custom-call(s32[1]{0:T(128)} %bitcast.place, s32[2]{0:T(128)} %lengths_at.1, bf16[2,8,6,128]{3,2,1,0:T(8,128)(2,1)} %reshape.20.refs_0_, bf16[2,128,1024]{2,1,0:T(8,128)(2,1)} %refs_1_.1, bf16[2,128,1024]{2,1,0:T(8,128)(2,1)} %refs_2_.1, bf16[2,1024]{1,0:T(2,128)(2,1)} %refs_3_.1, bf16[2,1024]{1,0:T(2,128)(2,1)} %refs_4_.1), custom_call_target="tpu_custom_call" | custom-call | tf_op jit(solution)/shard_map/attend/pallas_call | solution.py:66
  13.3 1.8 %all-to-all-done = bf16[8,4,3200]{2,1,0:T(4,128)(2,1)S(1)} async-done(((bf16[8,4,3200]{2,1,0:T(4,128)(2,1)}), bf16[8,4,3200]{2,1,0:T(4,128)(2,1)S(1)}, u32[]{:S(2)}, u32[]{:S(2)}) %all-to-all-start) | async-done | bytes 204832 | tf_op jit(solution)/shard_map/all_to_all | solution.py:454
  15.2 2.5 %collective-permute-start.2 = (bf16[32,3200]{1,0:T(8,128)(2,1)S(1)}, bf16[32,3200]{1,0:T(8,128)(2,1)S(1)}, u32[]{:S(2)}, u32[]{:S(2)}) collective-permute-start(bf16[32,3200]{1,0:T(8,128)(2,1)S(1)} %reshape.21), channel_id=1, source_target_pairs={{0,48},{1,7},{2,50},{3,1},{4,52},{5,3},{6,54},{7,5},{8,56},{9,15},... | collective-permute-start | bytes 614408 | tf_op jit(solution)/shard_map/ppermute | solution.py:58
  17.7 0.5 collective-permute-start.1
  18.3 0.6 collective-permute-start
  18.9 4.2 %all-to-all-start.1 = ((bf16[8,16,256]{2,1,0:T(8,128)(2,1)}), bf16[8,16,256]{2,1,0:T(8,128)(2,1)S(1)}, u32[]{:S(2)}, u32[]{:S(2)}) async-start(bf16[8,16,256]{2,1,0:T(8,128)(2,1)} %attend.1), calls=%async_computation.1 | async-start | bytes 131072 | tf_op jit(solution)/shard_map/all_to_all | solution.py:457
  23.1 1.1 %collective-permute-done.1 = bf16[32,3200]{1,0:T(8,128)(2,1)S(1)} collective-permute-done((bf16[32,3200]{1,0:T(8,128)(2,1)S(1)}, bf16[32,3200]{1,0:T(8,128)(2,1)S(1)}, u32[]{:S(2)}, u32[]{:S(2)}) %collective-permute-start.1) | collective-permute-done | bytes 204832 | tf_op jit(solution)/shard_map/ppermute | solution.py:58
  24.2 2.2 %collective-permute-done = bf16[32,3200]{1,0:T(8,128)(2,1)S(1)} collective-permute-done((bf16[32,3200]{1,0:T(8,128)(2,1)S(1)}, bf16[32,3200]{1,0:T(8,128)(2,1)S(1)}, u32[]{:S(2)}, u32[]{:S(2)}) %collective-permute-start) | collective-permute-done | bytes 204832 | tf_op jit(solution)/shard_map/ppermute | solution.py:58
  26.3 0.1 pad_maximum_fusion.rows
  26.4 2.0 %all-to-all-done.1.parts = bf16[8,16,256]{2,1,0:T(8,128)(2,1)S(1)} async-done(((bf16[8,16,256]{2,1,0:T(8,128)(2,1)}), bf16[8,16,256]{2,1,0:T(8,128)(2,1)S(1)}, u32[]{:S(2)}, u32[]{:S(2)}) %all-to-all-start.1) | async-done | bytes 65568 | tf_op jit(solution)/shard_map/all_to_all | solution.py:457
  28.4 0.9 collective-permute-start.8
  29.2 0.6 collective-permute-start.5
  29.8 0.9 collective-permute-start.3
  30.7 0.8 heads.1
  31.5 0.5 choose.4
  32.1 5.1 %collective-permute-start.4 = (bf16[64,3072]{1,0:T(8,128)(2,1)S(1)}, bf16[64,3072]{1,0:T(8,128)(2,1)S(1)}, u32[]{:S(2)}, u32[]{:S(2)}) collective-permute-start(bf16[64,3072]{1,0:T(8,128)(2,1)S(1)} %get-tuple-element.53), channel_id=1, source_target_pairs={{0,1},{1,0},{2,3},{3,2},{4,5},{5,4},{6,7},{7,6},{8,9},{9,8},{10,11... | collective-permute-start | bytes 1179656 | tf_op jit(solution)/shard_map/ppermute | solution.py:58
  37.2 8.2 %load.1 = (bf16[672,6144]{1,0:T(8,128)(2,1)S(1)}, bf16[672,6144]{1,0:T(8,128)(2,1)S(1)}, bf16[672,6144]{1,0:T(8,128)(2,1)S(1)}) custom-call(bf16[672,6144]{1,0:T(8,128)(2,1)} %bitcast.18, bf16[672,6144]{1,0:T(8,128)(2,1)} %bitcast.19, bf16[672,6144]{1,0:T(8,128)(2,1)} %bitcast.20), custom_call_target="tpu_custom_call" | custom-call | tf_op jit(solution)/shard_map/load/pallas_call | solution.py:66
  45.4 0.5 choose.7
  46.0 6.8 %collective-permute-start.9 = (bf16[64,3072]{1,0:T(8,128)(2,1)S(1)}, bf16[64,3072]{1,0:T(8,128)(2,1)S(1)}, u32[]{:S(2)}, u32[]{:S(2)}) collective-permute-start(bf16[64,3072]{1,0:T(8,128)(2,1)S(1)} %get-tuple-element.57), channel_id=1, source_target_pairs={{0,1},{1,0},{2,3},{3,2},{4,5},{5,4},{6,7},{7,6},{8,9},{9,8},{10,11... | collective-permute-start | bytes 1179656 | tf_op jit(solution)/shard_map/ppermute | solution.py:58
  52.8 0.5 choose.5
  53.3 3.1 %collective-permute-start.6 = (bf16[64,3072]{1,0:T(8,128)(2,1)S(1)}, bf16[64,3072]{1,0:T(8,128)(2,1)S(1)}, u32[]{:S(2)}, u32[]{:S(2)}) collective-permute-start(bf16[64,3072]{1,0:T(8,128)(2,1)S(1)} %get-tuple-element.54), channel_id=1, source_target_pairs={{0,1},{1,0},{2,3},{3,2},{4,5},{5,4},{6,7},{7,6},{8,9},{9,8},{10,11... | collective-permute-start | bytes 1179656 | tf_op jit(solution)/shard_map/ppermute | solution.py:58
  56.4 0.5 choose.6
  57.0 0.1 collective-permute-start.7
  57.1 2.3 %gate_up_own.1 = (f32[672,256]{1,0:T(8,128)S(1)}, f32[672,256]{1,0:T(8,128)S(1)}) custom-call(s32[1]{0:T(128)} %bitcast.7.core.half, bf16[64,3072]{1,0:T(8,128)(2,1)S(1)} %get-tuple-element.60.refs_0_, bf16[64,3072]{1,0:T(8,128)(2,1)S(1)} %get-tuple-element.61.refs_1_, bf16[64,3072]{1,0:T(8,128)(2,1)S(1)} %get-tuple-element.62.refs_2_, ...), custom_call_target="tpu_custom_call" | custom-call | tf_op jit(solution)/shard_map/gate_up_own/pallas_call | solution.py:66
  59.4 0.1 pad_maximum_fusion.1.refs_8_
  59.5 2.5 %gate_up_other.1.hidden = bf16[256,672]{1,0:T(8,128)(2,1)S(1)} custom-call(s32[1]{0:T(128)S(6)} %sub.3.peer.half, bf16[64,3072]{1,0:T(8,128)(2,1)S(1)} %collective-permute-done.4.refs_0_, bf16[64,3072]{1,0:T(8,128)(2,1)S(1)} %collective-permute-done.6.refs_1_, bf16[64,3072]{1,0:T(8,128)(2,1)S(1)} %collective-permute-done.7.refs_2_, ...), custom_call_target="tpu_custom_call" | custom-call | tf_op jit(solution)/shard_map/gate_up_other/pallas_call | solution.py:66
  62.0 0.8 down.5
  62.8 0.6 collective-permute-start.10
  63.4 0.8 down.7
  64.2 0.1 collective-permute-start.14
  64.3 0.8 down.4.mine.refs_0_
  65.1 0.2 collective-permute-done.10.theirs.refs_1_
  65.3 0.2 give.6
  65.6 1.1 %collective-permute-start.11 = (bf16[128,1536]{1,0:T(8,128)(2,1)S(1)}, bf16[128,1536]{1,0:T(8,128)(2,1)S(1)}, u32[]{:S(2)}, u32[]{:S(2)}) collective-permute-start(bf16[128,1536]{1,0:T(8,128)(2,1)S(1)} %give.6), channel_id=1, source_target_pairs={{0,4},{1,33},{2,6},{3,35},{4,0},{5,37},{6,2},{7,39},{8,12},{9,41},... | collective-permute-start | bytes 1179656 | tf_op jit(solution)/shard_map/ppermute | solution.py:58
  66.7 0.8 down.6.mine.refs_5_
  67.5 0.2 give.7
  67.8 2.0 %collective-permute-start.12 = (bf16[128,1536]{1,0:T(8,128)(2,1)S(1)}, bf16[128,1536]{1,0:T(8,128)(2,1)S(1)}, u32[]{:S(2)}, u32[]{:S(2)}) collective-permute-start(bf16[128,1536]{1,0:T(8,128)(2,1)S(1)} %give.7), channel_id=1, source_target_pairs={{0,6},{1,49},{2,0},{3,51},{4,2},{5,53},{6,4},{7,55},{8,14},{9,57},... | collective-permute-start | bytes 1179656 | tf_op jit(solution)/shard_map/ppermute | solution.py:58
  69.8 0.2 give.8
  70.1 0.1 collective-permute-start.13
  70.1 0.2 give.9
  70.4 1.7 %collective-permute-start.15 = (bf16[128,1536]{1,0:T(8,128)(2,1)S(1)}, bf16[128,1536]{1,0:T(8,128)(2,1)S(1)}, u32[]{:S(2)}, u32[]{:S(2)}) collective-permute-start(bf16[128,1536]{1,0:T(8,128)(2,1)S(1)} %give.9), channel_id=1, source_target_pairs={{0,4},{1,33},{2,6},{3,35},{4,0},{5,37},{6,2},{7,39},{8,12},{9,41},... | collective-permute-start | bytes 1179656 | tf_op jit(solution)/shard_map/ppermute | solution.py:58
  72.1 0.2 give.10
  72.3 1.2 %collective-permute-start.16 = (bf16[128,1536]{1,0:T(8,128)(2,1)S(1)}, bf16[128,1536]{1,0:T(8,128)(2,1)S(1)}, u32[]{:S(2)}, u32[]{:S(2)}) collective-permute-start(bf16[128,1536]{1,0:T(8,128)(2,1)S(1)} %give.10), channel_id=1, source_target_pairs={{0,6},{1,49},{2,0},{3,51},{4,2},{5,53},{6,4},{7,55},{8,14},{9,57},... | collective-permute-start | bytes 1179656 | tf_op jit(solution)/shard_map/ppermute | solution.py:58
  73.5 0.2 give.11
  73.7 0.5 collective-permute-done.11.refs_2_
  74.3 0.5 collective-permute-start.17
  74.8 2.3 %collective-permute-done.12.refs_3_ = bf16[128,1536]{1,0:T(8,128)(2,1)S(1)} collective-permute-done((bf16[128,1536]{1,0:T(8,128)(2,1)S(1)}, bf16[128,1536]{1,0:T(8,128)(2,1)S(1)}, u32[]{:S(2)}, u32[]{:S(2)}) %collective-permute-start.12) | collective-permute-done | bytes 393248 | tf_op jit(solution)/shard_map/ppermute | solution.py:58
  77.1 1.4 %collective-permute-done.13.refs_4_ = bf16[128,1536]{1,0:T(8,128)(2,1)S(1)} collective-permute-done((bf16[128,1536]{1,0:T(8,128)(2,1)S(1)}, bf16[128,1536]{1,0:T(8,128)(2,1)S(1)}, u32[]{:S(2)}, u32[]{:S(2)}) %collective-permute-start.13) | collective-permute-done | bytes 393248 | tf_op jit(solution)/shard_map/ppermute | solution.py:58
  78.5 4.3 %collective-permute-done.15.refs_7_ = bf16[128,1536]{1,0:T(8,128)(2,1)S(1)} collective-permute-done((bf16[128,1536]{1,0:T(8,128)(2,1)S(1)}, bf16[128,1536]{1,0:T(8,128)(2,1)S(1)}, u32[]{:S(2)}, u32[]{:S(2)}) %collective-permute-start.15) | collective-permute-done | bytes 393248 | tf_op jit(solution)/shard_map/ppermute | solution.py:58
  82.7 2.8 %collective-permute-done.16.refs_8_ = bf16[128,1536]{1,0:T(8,128)(2,1)S(1)} collective-permute-done((bf16[128,1536]{1,0:T(8,128)(2,1)S(1)}, bf16[128,1536]{1,0:T(8,128)(2,1)S(1)}, u32[]{:S(2)}, u32[]{:S(2)}) %collective-permute-start.16) | collective-permute-done | bytes 393248 | tf_op jit(solution)/shard_map/ppermute | solution.py:58
  85.5 1.4 %collective-permute-done.17.refs_9_ = bf16[128,1536]{1,0:T(8,128)(2,1)S(1)} collective-permute-done((bf16[128,1536]{1,0:T(8,128)(2,1)S(1)}, bf16[128,1536]{1,0:T(8,128)(2,1)S(1)}, u32[]{:S(2)}, u32[]{:S(2)}) %collective-permute-start.17) | collective-permute-done | bytes 393248 | tf_op jit(solution)/shard_map/ppermute | solution.py:58
  86.9 0.5 join.1
  87.4 0.1 collective-permute-start.18
  87.5 0.8 collective-permute-start.19
  88.3 0.8 collective-permute-start.20
  89.0 4.8 %collective-permute-done.18.refs_1_ = bf16[32,3072]{1,0:T(8,128)(2,1)S(1)} collective-permute-done((bf16[32,3072]{1,0:T(8,128)(2,1)S(1)}, bf16[32,3072]{1,0:T(8,128)(2,1)S(1)}, u32[]{:S(2)}, u32[]{:S(2)}) %collective-permute-start.18) | collective-permute-done | bytes 196640 | tf_op jit(solution)/shard_map/ppermute | solution.py:58
  93.8 0.4 collective-permute-done.19.refs_2_
  94.3 1.4 %collective-permute-done.20.refs_3_ = bf16[32,3072]{1,0:T(8,128)(2,1)S(1)} collective-permute-done((bf16[32,3072]{1,0:T(8,128)(2,1)S(1)}, bf16[32,3072]{1,0:T(8,128)(2,1)S(1)}, u32[]{:S(2)}, u32[]{:S(2)}) %collective-permute-start.20) | collective-permute-done | bytes 196640 | tf_op jit(solution)/shard_map/ppermute | solution.py:58
  95.6 0.1 column.1
  95.7 12.5 %all_to_all.15.parts = bf16[8,4,3072]{2,1,0:T(4,128)(2,1)S(1)} all-to-all(bf16[8,4,3072]{2,1,0:T(4,128)(2,1)S(1)} %column.1), channel_id=1, replica_groups={{0,1,64,65,8,9,72,73},{16,17,80,81,24,25,88,89},{32,33,96,97,40,41,104,..., dimensions={0} | all-to-all | bytes 393216 | tf_op jit(solution)/shard_map/all_to_all | solution.py:495
  108.2 0.7 last.1
  (10 shorter events, 0.1 us)
Async XLA Ops:
  2.3 12.8 %all-to-all-start = ((bf16[8,4,3200]{2,1,0:T(4,128)(2,1)}), bf16[8,4,3200]{2,1,0:T(4,128)(2,1)S(1)}, u32[]{:S(2)}, u32[]{:S(2)}) async-start(bf16[8,4,3200]{2,1,0:T(4,128)(2,1)} %pack.1), calls=%async_computation | async-start | bytes 409600 | tf_op jit(solution)/shard_map/all_to_all | solution.py:454
  15.2 7.9 %collective-permute-start.2 = (bf16[32,3200]{1,0:T(8,128)(2,1)S(1)}, bf16[32,3200]{1,0:T(8,128)(2,1)S(1)}, u32[]{:S(2)}, u32[]{:S(2)}) collective-permute-start(bf16[32,3200]{1,0:T(8,128)(2,1)S(1)} %reshape.21), channel_id=1, source_target_pairs={{0,48},{1,7},{2,50},{3,1},{4,52},{5,3},{6,54},{7,5},{8,56},{9,15},... | collective-permute-start | bytes 614408 | tf_op jit(solution)/shard_map/ppermute | solution.py:58
  17.7 6.5 %collective-permute-start.1 = (bf16[32,3200]{1,0:T(8,128)(2,1)S(1)}, bf16[32,3200]{1,0:T(8,128)(2,1)S(1)}, u32[]{:S(2)}, u32[]{:S(2)}) collective-permute-start(bf16[32,3200]{1,0:T(8,128)(2,1)S(1)} %reshape.21), channel_id=1, source_target_pairs={{0,32},{1,5},{2,34},{3,7},{4,36},{5,1},{6,38},{7,3},{8,40},{9,13},... | collective-permute-start | bytes 614408 | tf_op jit(solution)/shard_map/ppermute | solution.py:58
  18.3 8.1 %collective-permute-start = (bf16[32,3200]{1,0:T(8,128)(2,1)S(1)}, bf16[32,3200]{1,0:T(8,128)(2,1)S(1)}, u32[]{:S(2)}, u32[]{:S(2)}) collective-permute-start(bf16[32,3200]{1,0:T(8,128)(2,1)S(1)} %reshape.21), channel_id=1, source_target_pairs={{0,16},{1,3},{2,18},{3,5},{4,20},{5,7},{6,22},{7,1},{8,24},{9,11},... | collective-permute-start | bytes 614408 | tf_op jit(solution)/shard_map/ppermute | solution.py:58
  18.9 9.5 %all-to-all-start.1 = ((bf16[8,16,256]{2,1,0:T(8,128)(2,1)}), bf16[8,16,256]{2,1,0:T(8,128)(2,1)S(1)}, u32[]{:S(2)}, u32[]{:S(2)}) async-start(bf16[8,16,256]{2,1,0:T(8,128)(2,1)} %attend.1), calls=%async_computation.1 | async-start | bytes 131072 | tf_op jit(solution)/shard_map/all_to_all | solution.py:457
  28.4 17.1 %collective-permute-start.8 = (bf16[128,3200]{1,0:T(8,128)(2,1)S(1)}, bf16[128,3200]{1,0:T(8,128)(2,1)S(1)}, u32[]{:S(2)}, u32[]{:S(2)}) collective-permute-start(bf16[128,3200]{1,0:T(8,128)(2,1)S(1)} %pad_maximum_fusion.rows), channel_id=1, source_target_pairs={{0,6},{1,49},{2,0},{3,51},{4,2},{5,53},{6,4},{7,55},{8,14},{9,57},... | collective-permute-start | bytes 2457608 | tf_op jit(solution)/shard_map/ppermute | solution.py:58
  29.2 23.5 %collective-permute-start.5 = (bf16[128,3200]{1,0:T(8,128)(2,1)S(1)}, bf16[128,3200]{1,0:T(8,128)(2,1)S(1)}, u32[]{:S(2)}, u32[]{:S(2)}) collective-permute-start(bf16[128,3200]{1,0:T(8,128)(2,1)S(1)} %pad_maximum_fusion.rows), channel_id=1, source_target_pairs={{0,2},{1,17},{2,4},{3,19},{4,6},{5,21},{6,0},{7,23},{8,10},{9,25},... | collective-permute-start | bytes 2457608 | tf_op jit(solution)/shard_map/ppermute | solution.py:58
  29.8 26.6 %collective-permute-start.3 = (bf16[128,3200]{1,0:T(8,128)(2,1)S(1)}, bf16[128,3200]{1,0:T(8,128)(2,1)S(1)}, u32[]{:S(2)}, u32[]{:S(2)}) collective-permute-start(bf16[128,3200]{1,0:T(8,128)(2,1)S(1)} %pad_maximum_fusion.rows), channel_id=1, source_target_pairs={{0,4},{1,33},{2,6},{3,35},{4,0},{5,37},{6,2},{7,39},{8,12},{9,41},... | collective-permute-start | bytes 2457608 | tf_op jit(solution)/shard_map/ppermute | solution.py:58
  32.1 27.4 %collective-permute-start.4 = (bf16[64,3072]{1,0:T(8,128)(2,1)S(1)}, bf16[64,3072]{1,0:T(8,128)(2,1)S(1)}, u32[]{:S(2)}, u32[]{:S(2)}) collective-permute-start(bf16[64,3072]{1,0:T(8,128)(2,1)S(1)} %get-tuple-element.53), channel_id=1, source_target_pairs={{0,1},{1,0},{2,3},{3,2},{4,5},{5,4},{6,7},{7,6},{8,9},{9,8},{10,11... | collective-permute-start | bytes 1179656 | tf_op jit(solution)/shard_map/ppermute | solution.py:58
  46.0 13.5 %collective-permute-start.9 = (bf16[64,3072]{1,0:T(8,128)(2,1)S(1)}, bf16[64,3072]{1,0:T(8,128)(2,1)S(1)}, u32[]{:S(2)}, u32[]{:S(2)}) collective-permute-start(bf16[64,3072]{1,0:T(8,128)(2,1)S(1)} %get-tuple-element.57), channel_id=1, source_target_pairs={{0,1},{1,0},{2,3},{3,2},{4,5},{5,4},{6,7},{7,6},{8,9},{9,8},{10,11... | collective-permute-start | bytes 1179656 | tf_op jit(solution)/shard_map/ppermute | solution.py:58
  53.3 6.2 %collective-permute-start.6 = (bf16[64,3072]{1,0:T(8,128)(2,1)S(1)}, bf16[64,3072]{1,0:T(8,128)(2,1)S(1)}, u32[]{:S(2)}, u32[]{:S(2)}) collective-permute-start(bf16[64,3072]{1,0:T(8,128)(2,1)S(1)} %get-tuple-element.54), channel_id=1, source_target_pairs={{0,1},{1,0},{2,3},{3,2},{4,5},{5,4},{6,7},{7,6},{8,9},{9,8},{10,11... | collective-permute-start | bytes 1179656 | tf_op jit(solution)/shard_map/ppermute | solution.py:58
  57.0 2.5 %collective-permute-start.7 = (bf16[64,3072]{1,0:T(8,128)(2,1)S(1)}, bf16[64,3072]{1,0:T(8,128)(2,1)S(1)}, u32[]{:S(2)}, u32[]{:S(2)}) collective-permute-start(bf16[64,3072]{1,0:T(8,128)(2,1)S(1)} %get-tuple-element.56), channel_id=1, source_target_pairs={{0,1},{1,0},{2,3},{3,2},{4,5},{5,4},{6,7},{7,6},{8,9},{9,8},{10,11... | collective-permute-start | bytes 1179656 | tf_op jit(solution)/shard_map/ppermute | solution.py:58
  62.8 2.5 %collective-permute-start.10 = (bf16[256,1536]{1,0:T(8,128)(2,1)S(1)}, bf16[256,1536]{1,0:T(8,128)(2,1)S(1)}, u32[]{:S(2)}, u32[]{:S(2)}) collective-permute-start(bf16[256,1536]{1,0:T(8,128)(2,1)S(1)} %down.5), channel_id=1, source_target_pairs={{0,1},{1,0},{2,3},{3,2},{4,5},{5,4},{6,7},{7,6},{8,9},{9,8},{10,11... | collective-permute-start | bytes 2359304 | tf_op jit(solution)/shard_map/ppermute | solution.py:58
  64.2 5.9 %collective-permute-start.14 = (bf16[256,1536]{1,0:T(8,128)(2,1)S(1)}, bf16[256,1536]{1,0:T(8,128)(2,1)S(1)}, u32[]{:S(2)}, u32[]{:S(2)}) collective-permute-start(bf16[256,1536]{1,0:T(8,128)(2,1)S(1)} %down.7), channel_id=1, source_target_pairs={{0,1},{1,0},{2,3},{3,2},{4,5},{5,4},{6,7},{7,6},{8,9},{9,8},{10,11... | collective-permute-start | bytes 2359304 | tf_op jit(solution)/shard_map/ppermute | solution.py:58
  65.6 8.7 %collective-permute-start.11 = (bf16[128,1536]{1,0:T(8,128)(2,1)S(1)}, bf16[128,1536]{1,0:T(8,128)(2,1)S(1)}, u32[]{:S(2)}, u32[]{:S(2)}) collective-permute-start(bf16[128,1536]{1,0:T(8,128)(2,1)S(1)} %give.6), channel_id=1, source_target_pairs={{0,4},{1,33},{2,6},{3,35},{4,0},{5,37},{6,2},{7,39},{8,12},{9,41},... | collective-permute-start | bytes 1179656 | tf_op jit(solution)/shard_map/ppermute | solution.py:58
  67.8 9.3 %collective-permute-start.12 = (bf16[128,1536]{1,0:T(8,128)(2,1)S(1)}, bf16[128,1536]{1,0:T(8,128)(2,1)S(1)}, u32[]{:S(2)}, u32[]{:S(2)}) collective-permute-start(bf16[128,1536]{1,0:T(8,128)(2,1)S(1)} %give.7), channel_id=1, source_target_pairs={{0,6},{1,49},{2,0},{3,51},{4,2},{5,53},{6,4},{7,55},{8,14},{9,57},... | collective-permute-start | bytes 1179656 | tf_op jit(solution)/shard_map/ppermute | solution.py:58
  70.1 8.4 %collective-permute-start.13 = (bf16[128,1536]{1,0:T(8,128)(2,1)S(1)}, bf16[128,1536]{1,0:T(8,128)(2,1)S(1)}, u32[]{:S(2)}, u32[]{:S(2)}) collective-permute-start(bf16[128,1536]{1,0:T(8,128)(2,1)S(1)} %give.8), channel_id=1, source_target_pairs={{0,2},{1,17},{2,4},{3,19},{4,6},{5,21},{6,0},{7,23},{8,10},{9,25},... | collective-permute-start | bytes 1179656 | tf_op jit(solution)/shard_map/ppermute | solution.py:58
  70.4 12.3 %collective-permute-start.15 = (bf16[128,1536]{1,0:T(8,128)(2,1)S(1)}, bf16[128,1536]{1,0:T(8,128)(2,1)S(1)}, u32[]{:S(2)}, u32[]{:S(2)}) collective-permute-start(bf16[128,1536]{1,0:T(8,128)(2,1)S(1)} %give.9), channel_id=1, source_target_pairs={{0,4},{1,33},{2,6},{3,35},{4,0},{5,37},{6,2},{7,39},{8,12},{9,41},... | collective-permute-start | bytes 1179656 | tf_op jit(solution)/shard_map/ppermute | solution.py:58
  72.3 13.2 %collective-permute-start.16 = (bf16[128,1536]{1,0:T(8,128)(2,1)S(1)}, bf16[128,1536]{1,0:T(8,128)(2,1)S(1)}, u32[]{:S(2)}, u32[]{:S(2)}) collective-permute-start(bf16[128,1536]{1,0:T(8,128)(2,1)S(1)} %give.10), channel_id=1, source_target_pairs={{0,6},{1,49},{2,0},{3,51},{4,2},{5,53},{6,4},{7,55},{8,14},{9,57},... | collective-permute-start | bytes 1179656 | tf_op jit(solution)/shard_map/ppermute | solution.py:58
  74.3 12.6 %collective-permute-start.17 = (bf16[128,1536]{1,0:T(8,128)(2,1)S(1)}, bf16[128,1536]{1,0:T(8,128)(2,1)S(1)}, u32[]{:S(2)}, u32[]{:S(2)}) collective-permute-start(bf16[128,1536]{1,0:T(8,128)(2,1)S(1)} %give.11), channel_id=1, source_target_pairs={{0,2},{1,17},{2,4},{3,19},{4,6},{5,21},{6,0},{7,23},{8,10},{9,25},... | collective-permute-start | bytes 1179656 | tf_op jit(solution)/shard_map/ppermute | solution.py:58
  87.4 6.4 %collective-permute-start.18 = (bf16[32,3072]{1,0:T(8,128)(2,1)S(1)}, bf16[32,3072]{1,0:T(8,128)(2,1)S(1)}, u32[]{:S(2)}, u32[]{:S(2)}) collective-permute-start(bf16[32,3072]{1,0:T(8,128)(2,1)S(1)} %get-tuple-element.75), channel_id=1, source_target_pairs={{0,32},{1,5},{2,34},{3,7},{4,36},{5,1},{6,38},{7,3},{8,40},{9,13},... | collective-permute-start | bytes 589832 | tf_op jit(solution)/shard_map/ppermute | solution.py:58
  87.5 6.8 %collective-permute-start.19 = (bf16[32,3072]{1,0:T(8,128)(2,1)S(1)}, bf16[32,3072]{1,0:T(8,128)(2,1)S(1)}, u32[]{:S(2)}, u32[]{:S(2)}) collective-permute-start(bf16[32,3072]{1,0:T(8,128)(2,1)S(1)} %get-tuple-element.76), channel_id=1, source_target_pairs={{0,48},{1,7},{2,50},{3,1},{4,52},{5,3},{6,54},{7,5},{8,56},{9,15},... | collective-permute-start | bytes 589832 | tf_op jit(solution)/shard_map/ppermute | solution.py:58
  88.3 7.4 %collective-permute-start.20 = (bf16[32,3072]{1,0:T(8,128)(2,1)S(1)}, bf16[32,3072]{1,0:T(8,128)(2,1)S(1)}, u32[]{:S(2)}, u32[]{:S(2)}) collective-permute-start(bf16[32,3072]{1,0:T(8,128)(2,1)S(1)} %get-tuple-element.77), channel_id=1, source_target_pairs={{0,16},{1,3},{2,18},{3,5},{4,20},{5,7},{6,22},{7,1},{8,24},{9,11},... | collective-permute-start | bytes 589832 | tf_op jit(solution)/shard_map/ppermute | solution.py:58

commit v3 on v2

--- a/solution.py
+++ b/solution.py
@@ -17,6 +17,7 @@
 META = 128
 OUT = 1
 BACK = 2
+TIE = False
 OUT_WIDE = HALF // OUT
 BACK_WIDE = HALF // BACK
 KB = 512
@@ -49,8 +50,10 @@
 OUTER = ("x", "y")
 INNER = ("y", "x")
 CORE = ("core", "core")
-COLUMNS = [
-    [index(x, y, z, core) for z in range(4) for core in range(2)] for x in range(4) for y in range(4)
+PLANES = [
+    [index(**{INNER[core]: i, OUTER[core]: o, "z": z, "core": core}) for i in range(4) for z in range(4)]
+    for core in range(2)
+    for o in range(4)
 ]
 
 
@@ -86,7 +89,7 @@
     return jax.ShapeDtypeStruct(dims, dtype)
 
 
-def pack_kernel(x_at, routes_at, weights_at, out, x, routes, weights, sems):
+def pack_kernel(core, x_at, routes_at, weights_at, keep, give, x, routes, weights, sems):
     copies = [
         pltpu.make_async_copy(a, b, sems.at[i])
         for i, (a, b) in enumerate(((x_at, x), (routes_at, routes), (weights_at, weights)))
@@ -114,28 +117,51 @@
         for k in range(TOPK):
             meta = jnp.where(lane == j * TOPK + k, part[:, k : k + 1], meta)
     meta = meta.astype(BF)
-    for target in range(8):
-        at = (target % 2) * HALF
-        out[target, :, :OUT_WIDE] = x[:, at : at + OUT_WIDE]
-        out[target, :, OUT_WIDE : OUT_WIDE + META] = meta
+    own = jnp.where(core[0] == 0, x[:, :HALF], x[:, HALF:])
+    other = jnp.where(core[0] == 0, x[:, HALF:], x[:, :HALF])
+    for out, columns in ((keep, own), (give, other)):
+        out[:, :OUT_WIDE] = columns[:, :OUT_WIDE]
+        out[:, OUT_WIDE : OUT_WIDE + META] = meta
         if OUT > 1:
-            out[target, :, OUT_WIDE + META :] = x[:, at + OUT_WIDE : at + HALF]
-
-
-def pack(x, routes, weights):
+            out[:, OUT_WIDE + META :] = columns[:, OUT_WIDE:]
+
+
+def pack(core, x, routes, weights):
     return call(
         pack_kernel,
-        shape(8, 4, HALF + META),
+        [shape(4, HALF + META)] * 2,
+        core,
         *in_hbm(x, routes, weights),
         name="pack",
-        in_specs=[HBM] * 3,
-        out_specs=VMEM,
+        in_specs=[SMEM] + [HBM] * 3,
+        out_specs=[VMEM] * 2,
         scratch_shapes=[
             pltpu.VMEM((4, D), BF),
             pltpu.SMEM((4, TOPK), jnp.int32),
             pltpu.VMEM((4, TOPK), F32),
             pltpu.SemaphoreType.DMA((3,)),
         ],
+    )
+
+
+def spread_kernel(core, keep, got, out):
+    first = jnp.where(core[0] == 0, keep[...], got[...])
+    second = jnp.where(core[0] == 0, got[...], keep[...])
+    rows = jnp.concatenate([first, second], axis=0)
+    for target in range(16):
+        out[target] = rows
+
+
+def spread(core, keep, got):
+    return call(
+        spread_kernel,
+        shape(16, 8, HALF + META),
+        core,
+        keep,
+        got,
+        name="spread",
+        in_specs=[SMEM, VMEM, VMEM],
+        out_specs=VMEM,
     )
 
 
@@ -173,12 +199,13 @@
         theirs[:, at : at + KB] = found[64:]
 
 
-def choose_kernel(expert, rows, mine, theirs, chosen, shares):
+def choose_kernel(expert, place, rows, mine, theirs, chosen, shares):
     meta = rows[:, OUT_WIDE : OUT_WIDE + META].astype(F32)
     row = lax.broadcasted_iota(jnp.int32, (128, 128), 0)
     lane = lax.broadcasted_iota(jnp.int32, (128, 128), 1)
     wanted = 2 * jnp.where(lane < 64, expert[0], expert[0] ^ 1) + lane % 2
-    wanted = jnp.where(row // 4 == (lane % 64) // 2, wanted, -1).astype(F32)
+    block = ((place[0] - row // 32) & 3) * 8 + (row // 4) % 8
+    wanted = jnp.where(block == (lane % 64) // 2, wanted, -1).astype(F32)
     ones = jnp.zeros((128, 128), F32)
     weighted = jnp.zeros((128, 128), F32)
     for k in range(TOPK):
@@ -191,14 +218,15 @@
     picked(chosen[...], rows, mine, theirs)
 
 
-def choose(expert, rows):
+def choose(expert, place, rows):
     return call(
         choose_kernel,
         [shape(64, OUT_WIDE), shape(64, OUT_WIDE), shape(128, 128), shape(1, 128, dtype=F32)],
         expert,
+        place,
         rows,
         name="choose",
-        in_specs=[SMEM, VMEM],
+        in_specs=[SMEM, SMEM, VMEM],
         out_specs=[VMEM] * 4,
     )
 
@@ -226,67 +254,73 @@
 
 
 def own_kernel(chunk, core, *refs):
-    own, gate_w, up_w, before, (gate, up) = refs[:4], refs[4], refs[5], refs[6:-2], refs[-2:]
-    rows = jnp.concatenate([r[...] for r in own], axis=0)
+    gate_w, up_w, gate, up = refs[4:]
+    rows = jnp.concatenate([r[...] for r in refs[:4]], axis=0)
     here = columns_of(core[0], chunk, OUT_WIDE)
-    for out, weights, at in ((gate, gate_w, 0), (up, up_w, 1)):
-        found = across(weights[:, here], rows)
-        out[...] = found + before[at][...] if before else found
-
-
-def other_kernel(chunk, peer, *refs):
-    rows = turned(jnp.concatenate([r[...] for r in refs[:4]], axis=0))
-    gate_w, up_w, gate_at, up_at, share, *outs = refs[4:]
-    here = columns_of(peer[0], chunk, OUT_WIDE)
-    gate = gate_at[...] + across(gate_w[:, here], rows)
-    up = up_at[...] + across(up_w[:, here], rows)
-    if chunk < OUT - 1:
-        outs[0][...] = gate
-        outs[1][...] = up
-    else:
-        hidden = gate / (1.0 + jnp.exp(-gate)) * up * share[...]
-        outs[0][...] = hidden.T.astype(BF)
-
-
-def gate_up(core, peer, chunk, own, other, gate_w, up_w, before, share):
-    sums = [shape(FF, 256, dtype=F32)] * 2
-    args = [core, *own, gate_w, up_w, *before]
-    sums = call(
+    gate[...] = across(gate_w[:, here], rows)
+    up[...] = across(up_w[:, here], rows)
+
+
+def gate_up_own(core, chunk, own, gate_w, up_w):
+    return call(
         functools.partial(own_kernel, chunk),
-        sums,
+        [shape(FF, 256, dtype=F32)] * 2,
+        core,
+        *own,
+        gate_w,
+        up_w,
+        name="gate_up_own",
+        in_specs=[SMEM] + [VMEM] * 6,
+        out_specs=[VMEM] * 2,
+    )
+
+
+def hidden_kernel(peer, *refs):
+    other, refs = refs[: 4 * OUT], refs[4 * OUT :]
+    sums, refs = refs[: 2 * OUT], refs[2 * OUT :]
+    gate_w, up_w, down_w, share, hidden, *theirs = refs
+    gate = sum(r[...] for r in sums[0::2])
+    up = sum(r[...] for r in sums[1::2])
+    for c in range(OUT):
+        rows = turned(jnp.concatenate([r[...] for r in other[4 * c : 4 * c + 4]], axis=0))
+        here = columns_of(peer[0], c, OUT_WIDE)
+        gate += across(gate_w[:, here], rows)
+        up += across(up_w[:, here], rows)
+    hidden[...] = (gate / (1.0 + jnp.exp(-gate)) * up * share[...]).T.astype(BF)
+    for c in range(BACK):
+        here = columns_of(peer[0], c, BACK_WIDE)
+        rows = jnp.dot(hidden[...], down_w[:, here], preferred_element_type=F32)
+        theirs[c][...] = turned(rows.astype(BF))
+
+
+def hidden_rows(peer, other, sums, gate_w, up_w, down_w, share):
+    args = [peer, *other, *sums, gate_w, up_w, down_w, share]
+    return call(
+        hidden_kernel,
+        [shape(256, FF)] + [shape(256, BACK_WIDE)] * BACK,
         *args,
-        name="gate_up_own",
+        name="hidden",
         in_specs=[SMEM] + [VMEM] * (len(args) - 1),
-        out_specs=[VMEM] * 2,
-    )
-    args = [peer, *other, gate_w, up_w, *sums, share]
-    last = chunk == OUT - 1
-    return call(
-        functools.partial(other_kernel, chunk),
-        shape(256, FF) if last else [shape(FF, 256, dtype=F32)] * 2,
-        *args,
-        name="gate_up_other",
-        in_specs=[SMEM] + [VMEM] * (len(args) - 1),
-        out_specs=VMEM if last else [VMEM] * 2,
-    )
-
-
-def down_kernel(chunk, turn, half, hidden, weights, out):
-    here = columns_of(half[0], chunk, BACK_WIDE)
-    rows = jnp.dot(hidden[...], weights[:, here], preferred_element_type=F32).astype(BF)
-    out[...] = turned(rows) if turn else rows
-
-
-def down(half, chunk, hidden, weights, turn):
-    return call(
-        functools.partial(down_kernel, chunk, turn),
-        shape(256, BACK_WIDE),
-        half,
+        out_specs=[VMEM] * (1 + BACK),
+    )
+
+
+def down_kernel(core, hidden, weights, *outs):
+    for c in range(BACK):
+        here = columns_of(core[0], c, BACK_WIDE)
+        outs[c][...] = jnp.dot(hidden[...], weights[:, here], preferred_element_type=F32).astype(BF)
+
+
+def down(core, hidden, weights):
+    return call(
+        down_kernel,
+        [shape(256, BACK_WIDE)] * BACK,
+        core,
         hidden,
         weights,
         name="down",
         in_specs=[SMEM, VMEM, VMEM],
-        out_specs=VMEM,
+        out_specs=[VMEM] * BACK,
     )
 
 
@@ -312,7 +346,7 @@
 
 
 def join_kernel(chosen, *refs):
-    parts, outs = refs[:-4], refs[-4:]
+    parts, out = refs[:-1], refs[-1]
     for c in range(BACK):
         mine, theirs, *arrived = parts[5 * c : 5 * c + 5]
         for at in range(0, BACK_WIDE, KB):
@@ -321,10 +355,7 @@
             rows = jnp.dot(chosen[...], rows, preferred_element_type=F32)
             for part in arrived:
                 rows += part[:, here].astype(F32)
-            rows = rows.astype(BF)
-            there = slice(c * BACK_WIDE + at, c * BACK_WIDE + at + KB)
-            for k in range(4):
-                outs[k][:, there] = rows[32 * k : 32 * k + 32]
+            out[:, c * BACK_WIDE + at : c * BACK_WIDE + at + KB] = rows.astype(BF)
 
 
 def join(chosen, parts):
@@ -332,27 +363,37 @@
     rows = pl.BlockSpec((128, BACK_WIDE), lambda i: (0, 0))
     return call(
         join_kernel,
-        [shape(32, HALF)] * 4,
+        shape(128, HALF),
         chosen,
         *parts,
         name="join",
         grid=(1,),
         in_specs=[pl.BlockSpec((128, 128), lambda i: (0, 0))] + [slots, slots, rows, rows, rows] * BACK,
-        out_specs=[pl.BlockSpec((32, HALF), lambda i: (0, 0))] * 4,
-    )
-
-
-def column_kernel(*refs):
-    parts, out = refs[:-1], refs[-1]
-    rows = sum(p[...].astype(F32) for p in parts).astype(BF)
-    for target in range(8):
-        out[target] = rows[4 * target : 4 * target + 4]
-
-
-def last_kernel(parts, out):
-    for core in range(2):
-        rows = sum(parts[2 * z + core].astype(F32) for z in range(4))
-        out[:, core * HALF : (core + 1) * HALF] = rows.astype(BF)
+        out_specs=pl.BlockSpec((128, HALF), lambda i: (0, 0)),
+    )
+
+
+def fold_kernel(core, parts, keep, give):
+    rows = sum(parts[s].astype(F32) for s in range(16)).astype(BF)
+    keep[...] = jnp.where(core[0] == 0, rows[:4], rows[4:])
+    give[...] = jnp.where(core[0] == 0, rows[4:], rows[:4])
+
+
+def fold(core, parts):
+    return call(
+        fold_kernel,
+        [shape(4, HALF)] * 2,
+        core,
+        parts,
+        name="fold",
+        in_specs=[SMEM, VMEM],
+        out_specs=[VMEM] * 2,
+    )
+
+
+def last_kernel(core, keep, got, out):
+    out[:, :HALF] = jnp.where(core[0] == 0, keep[...], got[...])
+    out[:, HALF:] = jnp.where(core[0] == 0, got[...], keep[...])
 
 
 def attend_kernel(place, lengths_at, *refs):
@@ -446,54 +487,67 @@
     w_down,
 ):
     expert = (lax.axis_index("grp") & 15).astype(jnp.int32)
-    core = (expert & 1).reshape(1)
-    expert = expert.reshape(1)
-
+    core, peer = expert & 1, 1 - (expert & 1)
+    place = jnp.where(core == 0, lax.axis_index("ctx") & 3, (expert >> 1) & 3).astype(jnp.int32)
+    expert, core, peer, place = (a.reshape(1) for a in (expert, core, peer, place))
+
+    keep, sent = pack(core, moe_input, routes, route_weights)
+    column = spread(core, keep, move(sent, CORE, 1))
+    plane = lax.all_to_all(column, ALL, 0, 0, axis_index_groups=PLANES, tiled=True)
     packed = attend(queries, key_cache, value_cache, new_key, new_value, lengths)
-    sent = pack(moe_input, routes, route_weights)
-    column = lax.all_to_all(sent, ALL, 0, 0, axis_index_groups=COLUMNS, tiled=True)
-    column, packed = lax.optimization_barrier((column, packed))
-    column = column.reshape(32, HALF + META)
-    head_parts = lax.all_to_all(packed, "ctx", 0, 0, tiled=True)
-    plane = jnp.concatenate([column] + [move(column, INNER, k) for k in (1, 2, 3)], axis=0)
+    weights = (w_gate[0].T, w_up[0].T, w_down[0])
+    plane, packed, weights, expert, core, peer, place = lax.optimization_barrier(
+        (plane, packed, weights, expert, core, peer, place)
+    )
+    plane = plane.reshape(128, HALF + META)
     cuts = [0] + [OUT_WIDE * (c + 1) + META for c in range(OUT)]
     planes = [plane[:, cuts[c] : cuts[c + 1]] for c in range(OUT)]
-
-    weights = (w_gate[0].T, w_up[0].T, w_down[0])
-    planes[0], head_parts, weights, expert, core, peer = lax.optimization_barrier(
-        (planes[0], head_parts, weights, expert, core, 1 - core)
-    )
     shards = [[p] + [move(p, OUTER, k) for k in (1, 2, 3)] for p in planes]
+
     gate_w, up_w, down_w = load(*weights)
-    head_outputs = call(heads_kernel, shape(2, HD * QH // KVH), head_parts, name="heads")
-    shards[-1][2], head_outputs, gate_w = lax.optimization_barrier(
-        (shards[-1][2], head_outputs, gate_w)
-    )
-
-    chosen, shares, sums = [None] * 4, [None] * 4, ()
+    shards[0][1], gate_w = lax.optimization_barrier((shards[0][1], gate_w))
+
+    chosen, shares, others, sums = [None] * 4, [None] * 4, [], []
     for c in range(OUT):
         own, other = [None] * 4, [None] * 4
         for k in (0, 1, 3, 2):
             if c == 0:
-                own[k], theirs, chosen[k], shares[k] = choose(expert, shards[c][k])
+                own[k], theirs, chosen[k], shares[k] = choose(expert, place, shards[c][k])
             else:
                 own[k], theirs = pick(chosen[k], shards[c][k])
             other[k] = move(theirs, CORE, 1)
-        share = jnp.concatenate([s[:, :64] for s in shares], axis=1)
-        sums = gate_up(core, peer, c, own, other, gate_w, up_w, sums, share)
-    hidden = sums
-
+        others += other
+        sums += gate_up_own(core, c, own, gate_w, up_w)
+        if TIE and c < OUT - 1:
+            sums, chosen = lax.optimization_barrier((sums, chosen))
+    share = jnp.concatenate([s[:, :64] for s in shares], axis=1)
+    hidden, *theirs = hidden_rows(peer, others, sums, gate_w, up_w, down_w, share)
+
+    theirs = [move(t, CORE, 1) for t in theirs]
+    mine = down(core, hidden, down_w)
     parts = []
     for c in range(BACK):
-        theirs = move(down(peer, c, hidden, down_w, True), CORE, 1)
-        mine = down(core, c, hidden, down_w, False)
-        parts += [mine, theirs]
-        parts += [move(give(chosen[k], mine, theirs, k), OUTER, -k) for k in (2, 1, 3)]
-    pieces = join(chosen[0], parts)
-    pieces = [pieces[0]] + [move(pieces[k], INNER, -k) for k in (2, 1, 3)]
-    column = call(column_kernel, shape(8, 4, HALF), *pieces, name="column")
-    parts = lax.all_to_all(column, ALL, 0, 0, axis_index_groups=COLUMNS, tiled=True)
-    return head_outputs, call(last_kernel, shape(4, D), parts, name="last")
+        given = [give(chosen[k], mine[c], theirs[c], k) for k in (1, 3, 2)]
+        if c == BACK - 1:
+            given[-1], packed = lax.optimization_barrier((given[-1], packed))
+        parts += [mine[c], theirs[c]] + [move(g, OUTER, -k) for g, k in zip(given, (1, 3, 2))]
+
+    head_parts = lax.all_to_all(packed, "ctx", 0, 0, tiled=True)
+    parts[-1], head_parts = lax.optimization_barrier((parts[-1], head_parts))
+    head_outputs = call(heads_kernel, shape(2, HD * QH // KVH), head_parts, name="heads")
+    rows = join(chosen[0], parts).reshape(16, 8, HALF)
+    keep, sent = fold(core, lax.all_to_all(rows, ALL, 0, 0, axis_index_groups=PLANES, tiled=True))
+    mixed = call(
+        last_kernel,
+        shape(4, D),
+        core,
+        keep,
+        move(sent, CORE, 1),
+        name="last",
+        in_specs=[SMEM, VMEM, VMEM],
+        out_specs=VMEM,
+    )
+    return head_outputs, mixed
 
 
 def solution(mesh):

time: 109 us -> 103 us (0.945)
  blocking collectives: 12.5 us -> 26 us
  starting transfers between devices: 41 us -> 30.9 us
  waiting for transfers between devices: 26.5 us -> 17.8 us
    ppermute x21 -> x17, waiting for transfers between devices: 22.8 us -> 8.84 us  [move(): return lax.ppermute(a, ALL, shifted(axes, k % 4 if axes is not CORE else 1))]
    all_to_all x1 -> x2, blocking collectives: 12.5 us -> 26 us  [the longest x1 15.7 us: body(): lax.all_to_all(rows, ALL, 0, 0, axis_index_groups=PLANES, tiled=True)]
    ppermute x21 -> x17, starting transfers between devices: 30 us -> 23.2 us  [move(): return lax.ppermute(a, ALL, shifted(axes, k % 4 if axes is not CORE else 1))]
    all_to_all x2 -> x1, waiting for transfers between devices: 3.75 us -> 8.98 us  [body(): lax.all_to_all(column, ALL, 0, 0, axis_index_groups=PLANES, tiled=True)]
    all_to_all x2 -> x1, starting transfers between devices: 11 us -> 7.68 us  [body(): lax.all_to_all(column, ALL, 0, 0, axis_index_groups=PLANES, tiled=True)]
    pallas_call x23 -> x21, Pallas kernels: 26.4 us -> 25.6 us  [call(): pl.pallas_call(kernel, out_shape=outs, compiler_params=pltpu.CompilerPara...]
  transfers between devices with their start and end apart: 23 -> 18, of which waited for: 14 -> 6; matrix products, arithmetic and copies ran while one was open for 1% -> 1% of each run, Pallas kernels for 18% -> 18%
where the time goes in v3:
time: 103 us
  starting transfers between devices  30.9 us (30%)
  blocking collectives  26 us (25%)
  Pallas kernels  25.6 us (25%)
  waiting for transfers between devices  17.8 us (17%)
  local copies, waits for them, and re-layouts  1.38 us (1%)
    pallas_call x21, Pallas kernels, call(): pl.pallas_call(kernel, out_shape=outs, compiler_params=pltpu.CompilerPara...  25.6 us
    ppermute x17, starting transfers between devices, move(): return lax.ppermute(a, ALL, shifted(axes, k % 4 if axes is not CORE else 1))  23.2 us
    all_to_all x1, blocking collectives, body(): lax.all_to_all(rows, ALL, 0, 0, axis_index_groups=PLANES, tiled=True)  15.7 us
    all_to_all x1, blocking collectives, body(): head_parts = lax.all_to_all(packed, 'ctx', 0, 0, tiled=True)  10.3 us
    all_to_all x1, waiting for transfers between devices, body(): lax.all_to_all(column, ALL, 0, 0, axis_index_groups=PLANES, tiled=True)  8.98 us
    ppermute x17, waiting for transfers between devices, move(): return lax.ppermute(a, ALL, shifted(axes, k % 4 if axes is not CORE else 1))  8.84 us
    all_to_all x1, starting transfers between devices, body(): lax.all_to_all(column, ALL, 0, 0, axis_index_groups=PLANES, tiled=True)  7.68 us
  transfers between devices with their start and end apart: 18, of which 6 were waited for; matrix products, arithmetic and copies ran while one was open for 1% of the time, Pallas kernels for 18%

profile of v3, /device:TPU:1, one launch (start us, length us, event | category | flops | bytes accessed | tf_op | source)
XLA Modules:
  0.0 102.7 jit_solution(6666741096072117435)
XLA Ops:
  0.6 1.0 %pack.1 = (bf16[4,3200]{1,0:T(4,128)(2,1)S(1)}, bf16[4,3200]{1,0:T(4,128)(2,1)S(1)}) custom-call(s32[1]{0:T(128)} %bitcast.core, bf16[4,6144]{1,0:T(4,128)(2,1)} %x_at.1, s32[4,4]{1,0:T(4,128)} %routes_at.1, f32[4,4]{1,0:T(4,128)} %weights_at.1), custom_call_target="tpu_custom_call" | custom-call | tf_op jit(solution)/shard_map/pack/pallas_call | solution.py:69
  1.7 1.5 %collective-permute-start = (bf16[4,3200]{1,0:T(4,128)(2,1)S(1)}, bf16[4,3200]{1,0:T(4,128)(2,1)S(1)}, u32[]{:S(2)}, u32[]{:S(2)}) collective-permute-start(bf16[4,3200]{1,0:T(4,128)(2,1)S(1)} %get-tuple-element.48), channel_id=1, source_target_pairs={{0,1},{1,0},{2,3},{3,2},{4,5},{5,4},{6,7},{7,6},{8,9},{9,8},{10,11... | collective-permute-start | bytes 76808 | tf_op jit(solution)/shard_map/ppermute | solution.py:61
  3.2 0.9 collective-permute-done.got
  4.0 1.0 spread.1
  5.0 7.7 %all-to-all-start = ((bf16[16,8,3200]{2,1,0:T(8,128)(2,1)}), bf16[16,8,3200]{2,1,0:T(8,128)(2,1)S(1)}, u32[]{:S(2)}, u32[]{:S(2)}) async-start(bf16[16,8,3200]{2,1,0:T(8,128)(2,1)} %spread.1), calls=%async_computation | async-start | bytes 1638400 | tf_op jit(solution)/shard_map/all_to_all | solution.py:496
  12.7 1.4 %reshape.30.refs_0_ = bf16[2,8,6,128]{3,2,1,0:T(8,128)(2,1)} reshape(bf16[2,6144]{1,0:T(2,128)(2,1)} %param.12) | data formatting | bytes 49152 | tf_op jit(solution)/shard_map/reshape | solution.py:444
  14.1 2.2 %attend.1 = bf16[8,16,256]{2,1,0:T(8,128)(2,1)S(1)} custom-call(s32[1]{0:T(128)} %bitcast.1.place, s32[2]{0:T(128)} %lengths_at.1, bf16[2,8,6,128]{3,2,1,0:T(8,128)(2,1)} %reshape.30.refs_0_, bf16[2,128,1024]{2,1,0:T(8,128)(2,1)} %refs_1_.1, bf16[2,128,1024]{2,1,0:T(8,128)(2,1)} %refs_2_.1, bf16[2,1024]{1,0:T(2,128)(2,1)} %refs_3_.1, bf16[2,1024]{1,0:T(2,128)(2,1)} %refs_4_.1), custom_call_target="tpu_custom_call" | custom-call | tf_op jit(solution)/shard_map/attend/pallas_call | solution.py:69
  16.3 9.0 %all-to-all-done = bf16[16,8,3200]{2,1,0:T(8,128)(2,1)S(1)} async-done(((bf16[16,8,3200]{2,1,0:T(8,128)(2,1)}), bf16[16,8,3200]{2,1,0:T(8,128)(2,1)S(1)}, u32[]{:S(2)}, u32[]{:S(2)}) %all-to-all-start) | async-done | bytes 819232 | tf_op jit(solution)/shard_map/all_to_all | solution.py:496
  25.3 2.3 %collective-permute-start.6 = (bf16[128,3200]{1,0:T(8,128)(2,1)S(1)}, bf16[128,3200]{1,0:T(8,128)(2,1)S(1)}, u32[]{:S(2)}, u32[]{:S(2)}) collective-permute-start(bf16[128,3200]{1,0:T(8,128)(2,1)S(1)} %bitcast.18), channel_id=1, source_target_pairs={{0,6},{1,49},{2,0},{3,51},{4,2},{5,53},{6,4},{7,55},{8,14},{9,57},... | collective-permute-start | bytes 2457608 | tf_op jit(solution)/shard_map/ppermute | solution.py:61
  27.5 1.1 %collective-permute-start.1 = (bf16[128,3200]{1,0:T(8,128)(2,1)S(1)}, bf16[128,3200]{1,0:T(8,128)(2,1)S(1)}, u32[]{:S(2)}, u32[]{:S(2)}) collective-permute-start(bf16[128,3200]{1,0:T(8,128)(2,1)S(1)} %bitcast.19), channel_id=1, source_target_pairs={{0,4},{1,33},{2,6},{3,35},{4,0},{5,37},{6,2},{7,39},{8,12},{9,41},... | collective-permute-start | bytes 2457608 | tf_op jit(solution)/shard_map/ppermute | solution.py:61
  28.7 0.3 collective-permute-start.3
  29.0 0.5 choose.5
  29.5 1.4 %collective-permute-start.2 = (bf16[64,3072]{1,0:T(8,128)(2,1)S(1)}, bf16[64,3072]{1,0:T(8,128)(2,1)S(1)}, u32[]{:S(2)}, u32[]{:S(2)}) collective-permute-start(bf16[64,3072]{1,0:T(8,128)(2,1)S(1)} %get-tuple-element.55), channel_id=1, source_target_pairs={{0,1},{1,0},{2,3},{3,2},{4,5},{5,4},{6,7},{7,6},{8,9},{9,8},{10,11... | collective-permute-start | bytes 1179656 | tf_op jit(solution)/shard_map/ppermute | solution.py:61
  30.9 8.2 %load.1 = (bf16[672,6144]{1,0:T(8,128)(2,1)S(1)}, bf16[672,6144]{1,0:T(8,128)(2,1)S(1)}, bf16[672,6144]{1,0:T(8,128)(2,1)S(1)}) custom-call(bf16[672,6144]{1,0:T(8,128)(2,1)} %bitcast.27, bf16[672,6144]{1,0:T(8,128)(2,1)} %bitcast.28, bf16[672,6144]{1,0:T(8,128)(2,1)} %bitcast.29), custom_call_target="tpu_custom_call" | custom-call | tf_op jit(solution)/shard_map/load/pallas_call | solution.py:69
  39.1 6.5 %collective-permute-done.6.rows = bf16[128,3200]{1,0:T(8,128)(2,1)S(1)} collective-permute-done((bf16[128,3200]{1,0:T(8,128)(2,1)S(1)}, bf16[128,3200]{1,0:T(8,128)(2,1)S(1)}, u32[]{:S(2)}, u32[]{:S(2)}) %collective-permute-start.6) | collective-permute-done | bytes 819232 | tf_op jit(solution)/shard_map/ppermute | solution.py:61
  45.6 0.5 choose.7
  46.1 1.8 %collective-permute-start.7 = (bf16[64,3072]{1,0:T(8,128)(2,1)S(1)}, bf16[64,3072]{1,0:T(8,128)(2,1)S(1)}, u32[]{:S(2)}, u32[]{:S(2)}) collective-permute-start(bf16[64,3072]{1,0:T(8,128)(2,1)S(1)} %get-tuple-element.63), channel_id=1, source_target_pairs={{0,1},{1,0},{2,3},{3,2},{4,5},{5,4},{6,7},{7,6},{8,9},{9,8},{10,11... | collective-permute-start | bytes 1179656 | tf_op jit(solution)/shard_map/ppermute | solution.py:61
  47.9 0.0 collective-permute-done.1.rows
  47.9 0.5 choose.4
  48.4 0.1 collective-permute-start.5
  48.5 0.8 collective-permute-done.3.rows
  49.3 0.5 choose.6
  49.8 2.0 %collective-permute-start.4 = (bf16[64,3072]{1,0:T(8,128)(2,1)S(1)}, bf16[64,3072]{1,0:T(8,128)(2,1)S(1)}, u32[]{:S(2)}, u32[]{:S(2)}) collective-permute-start(bf16[64,3072]{1,0:T(8,128)(2,1)S(1)} %get-tuple-element.61), channel_id=1, source_target_pairs={{0,1},{1,0},{2,3},{3,2},{4,5},{5,4},{6,7},{7,6},{8,9},{9,8},{10,11... | collective-permute-start | bytes 1179656 | tf_op jit(solution)/shard_map/ppermute | solution.py:61
  51.8 2.3 %gate_up_own.1 = (f32[672,256]{1,0:T(8,128)S(1)}, f32[672,256]{1,0:T(8,128)S(1)}) custom-call(s32[1]{0:T(128)} %bitcast.core, bf16[64,3072]{1,0:T(8,128)(2,1)S(1)} %get-tuple-element.64.refs_0_, bf16[64,3072]{1,0:T(8,128)(2,1)S(1)} %get-tuple-element.65.refs_1_, bf16[64,3072]{1,0:T(8,128)(2,1)S(1)} %get-tuple-element.66.refs_2_, ...), custom_call_target="tpu_custom_call" | custom-call | tf_op jit(solution)/shard_map/gate_up_own/pallas_call | solution.py:69
  54.2 0.1 pad_maximum_fusion.refs_9_
  54.2 0.0 collective-permute-done.2.refs_0_
  54.2 0.0 collective-permute-done.7.refs_3_
  54.2 0.0 collective-permute-done.5.refs_2_
  54.3 0.0 collective-permute-done.4.refs_1_
  54.3 3.8 %hidden.1 = (bf16[256,672]{1,0:T(8,128)(2,1)S(1)}, bf16[256,1536]{1,0:T(8,128)(2,1)S(1)}, bf16[256,1536]{1,0:T(8,128)(2,1)S(1)}) custom-call(s32[1]{0:T(128)} %bitcast.8.peer, bf16[64,3072]{1,0:T(8,128)(2,1)S(1)} %collective-permute-done.2.refs_0_, bf16[64,3072]{1,0:T(8,128)(2,1)S(1)} %collective-permute-done.4.refs_1_, ...), custom_call_target="tpu_custom_call" | custom-call | tf_op jit(solution)/shard_map/hidden/pallas_call | solution.py:69
  58.1 0.1 collective-permute-start.8
  58.2 0.5 collective-permute-start.10
  58.7 1.4 %down.1 = (bf16[256,1536]{1,0:T(8,128)(2,1)S(1)}, bf16[256,1536]{1,0:T(8,128)(2,1)S(1)}) custom-call(s32[1]{0:T(128)} %bitcast.core, bf16[256,672]{1,0:T(8,128)(2,1)S(1)} %get-tuple-element.77.hidden, bf16[672,6144]{1,0:T(8,128)(2,1)S(1)} %get-tuple-element.72.refs_8_.weights), custom_call_target="tpu_custom_call" | custom-call | tf_op jit(solution)/shard_map/down/pallas_call | solution.py:69
  60.1 0.4 collective-permute-done.8.theirs.refs_6_
  60.5 0.2 give.6
  60.7 3.0 %collective-permute-start.9 = (bf16[128,1536]{1,0:T(8,128)(2,1)S(1)}, bf16[128,1536]{1,0:T(8,128)(2,1)S(1)}, u32[]{:S(2)}, u32[]{:S(2)}) collective-permute-start(bf16[128,1536]{1,0:T(8,128)(2,1)S(1)} %give.6), channel_id=1, source_target_pairs={{0,4},{1,33},{2,6},{3,35},{4,0},{5,37},{6,2},{7,39},{8,12},{9,41},... | collective-permute-start | bytes 1179656 | tf_op jit(solution)/shard_map/ppermute | solution.py:61
  63.7 0.2 give.10
  64.0 1.0 collective-permute-start.14
  65.0 0.2 give.11
  65.2 0.8 collective-permute-start.15
  66.0 0.0 collective-permute-done.10.theirs.refs_1_
  66.0 0.2 give.7
  66.3 2.1 %collective-permute-start.11 = (bf16[128,1536]{1,0:T(8,128)(2,1)S(1)}, bf16[128,1536]{1,0:T(8,128)(2,1)S(1)}, u32[]{:S(2)}, u32[]{:S(2)}) collective-permute-start(bf16[128,1536]{1,0:T(8,128)(2,1)S(1)} %give.7), channel_id=1, source_target_pairs={{0,6},{1,49},{2,0},{3,51},{4,2},{5,53},{6,4},{7,55},{8,14},{9,57},... | collective-permute-start | bytes 1179656 | tf_op jit(solution)/shard_map/ppermute | solution.py:61
  68.3 0.2 give.8
  68.6 0.1 collective-permute-start.12
  68.7 0.2 give.9
  68.9 0.3 collective-permute-done.9.refs_9_
  69.2 2.9 %collective-permute-start.13 = (bf16[128,1536]{1,0:T(8,128)(2,1)S(1)}, bf16[128,1536]{1,0:T(8,128)(2,1)S(1)}, u32[]{:S(2)}, u32[]{:S(2)}) collective-permute-start(bf16[128,1536]{1,0:T(8,128)(2,1)S(1)} %give.9), channel_id=1, source_target_pairs={{0,4},{1,33},{2,6},{3,35},{4,0},{5,37},{6,2},{7,39},{8,12},{9,41},... | collective-permute-start | bytes 1179656 | tf_op jit(solution)/shard_map/ppermute | solution.py:61
  72.2 10.3 %all_to_all.15.parts = bf16[8,16,256]{2,1,0:T(8,128)(2,1)S(1)} all-to-all(bf16[8,16,256]{2,1,0:T(8,128)(2,1)S(1)} %attend.1), channel_id=1, replica_groups=mesh['ctx'=8,'grp'=16] {'ctx'}, dimensions={0} | all-to-all | bytes 131072 | tf_op jit(solution)/shard_map/all_to_all | solution.py:535
  82.5 0.0 collective-permute-done.14.refs_7_
  82.5 0.0 collective-permute-done.15.refs_8_
  82.5 0.0 collective-permute-done.11.refs_2_
  82.5 0.0 collective-permute-done.12.refs_3_
  82.5 0.0 collective-permute-done.13.refs_4_
  82.5 0.5 join.1
  83.0 15.7 %all_to_all.16.parts = bf16[16,8,3072]{2,1,0:T(8,128)(2,1)S(1)} all-to-all(bf16[16,8,3072]{2,1,0:T(8,128)(2,1)S(1)} %bitcast.22), channel_id=1, replica_groups={{0,64,8,72,16,80,24,88,32,96,40,104,48,112,56,120},{2,66,10,74,18,82,26..., dimensions={0} | all-to-all | bytes 1572864 | tf_op jit(solution)/shard_map/all_to_all | solution.py:539
  98.7 0.1 fold.1
  98.8 2.3 %collective-permute-start.16 = (bf16[4,3072]{1,0:T(4,128)(2,1)S(1)}, bf16[4,3072]{1,0:T(4,128)(2,1)S(1)}, u32[]{:S(2)}, u32[]{:S(2)}) collective-permute-start(bf16[4,3072]{1,0:T(4,128)(2,1)S(1)} %get-tuple-element.91), channel_id=1, source_target_pairs={{0,1},{1,0},{2,3},{3,2},{4,5},{5,4},{6,7},{7,6},{8,9},{9,8},{10,11... | collective-permute-start | bytes 73736 | tf_op jit(solution)/shard_map/ppermute | solution.py:61
  101.2 0.8 heads.1
  102.0 0.0 collective-permute-done.16.got
  102.0 0.6 last.1
Async XLA Ops:
  1.7 2.4 %collective-permute-start = (bf16[4,3200]{1,0:T(4,128)(2,1)S(1)}, bf16[4,3200]{1,0:T(4,128)(2,1)S(1)}, u32[]{:S(2)}, u32[]{:S(2)}) collective-permute-start(bf16[4,3200]{1,0:T(4,128)(2,1)S(1)} %get-tuple-element.48), channel_id=1, source_target_pairs={{0,1},{1,0},{2,3},{3,2},{4,5},{5,4},{6,7},{7,6},{8,9},{9,8},{10,11... | collective-permute-start | bytes 76808 | tf_op jit(solution)/shard_map/ppermute | solution.py:61
  5.0 20.2 %all-to-all-start = ((bf16[16,8,3200]{2,1,0:T(8,128)(2,1)}), bf16[16,8,3200]{2,1,0:T(8,128)(2,1)S(1)}, u32[]{:S(2)}, u32[]{:S(2)}) async-start(bf16[16,8,3200]{2,1,0:T(8,128)(2,1)} %spread.1), calls=%async_computation | async-start | bytes 1638400 | tf_op jit(solution)/shard_map/all_to_all | solution.py:496
  25.3 20.3 %collective-permute-start.6 = (bf16[128,3200]{1,0:T(8,128)(2,1)S(1)}, bf16[128,3200]{1,0:T(8,128)(2,1)S(1)}, u32[]{:S(2)}, u32[]{:S(2)}) collective-permute-start(bf16[128,3200]{1,0:T(8,128)(2,1)S(1)} %bitcast.18), channel_id=1, source_target_pairs={{0,6},{1,49},{2,0},{3,51},{4,2},{5,53},{6,4},{7,55},{8,14},{9,57},... | collective-permute-start | bytes 2457608 | tf_op jit(solution)/shard_map/ppermute | solution.py:61
  27.5 20.4 %collective-permute-start.1 = (bf16[128,3200]{1,0:T(8,128)(2,1)S(1)}, bf16[128,3200]{1,0:T(8,128)(2,1)S(1)}, u32[]{:S(2)}, u32[]{:S(2)}) collective-permute-start(bf16[128,3200]{1,0:T(8,128)(2,1)S(1)} %bitcast.19), channel_id=1, source_target_pairs={{0,4},{1,33},{2,6},{3,35},{4,0},{5,37},{6,2},{7,39},{8,12},{9,41},... | collective-permute-start | bytes 2457608 | tf_op jit(solution)/shard_map/ppermute | solution.py:61
  28.7 20.6 %collective-permute-start.3 = (bf16[128,3200]{1,0:T(8,128)(2,1)S(1)}, bf16[128,3200]{1,0:T(8,128)(2,1)S(1)}, u32[]{:S(2)}, u32[]{:S(2)}) collective-permute-start(bf16[128,3200]{1,0:T(8,128)(2,1)S(1)} %bitcast.20), channel_id=1, source_target_pairs={{0,2},{1,17},{2,4},{3,19},{4,6},{5,21},{6,0},{7,23},{8,10},{9,25},... | collective-permute-start | bytes 2457608 | tf_op jit(solution)/shard_map/ppermute | solution.py:61
  29.5 24.7 %collective-permute-start.2 = (bf16[64,3072]{1,0:T(8,128)(2,1)S(1)}, bf16[64,3072]{1,0:T(8,128)(2,1)S(1)}, u32[]{:S(2)}, u32[]{:S(2)}) collective-permute-start(bf16[64,3072]{1,0:T(8,128)(2,1)S(1)} %get-tuple-element.55), channel_id=1, source_target_pairs={{0,1},{1,0},{2,3},{3,2},{4,5},{5,4},{6,7},{7,6},{8,9},{9,8},{10,11... | collective-permute-start | bytes 1179656 | tf_op jit(solution)/shard_map/ppermute | solution.py:61
  46.1 8.1 %collective-permute-start.7 = (bf16[64,3072]{1,0:T(8,128)(2,1)S(1)}, bf16[64,3072]{1,0:T(8,128)(2,1)S(1)}, u32[]{:S(2)}, u32[]{:S(2)}) collective-permute-start(bf16[64,3072]{1,0:T(8,128)(2,1)S(1)} %get-tuple-element.63), channel_id=1, source_target_pairs={{0,1},{1,0},{2,3},{3,2},{4,5},{5,4},{6,7},{7,6},{8,9},{9,8},{10,11... | collective-permute-start | bytes 1179656 | tf_op jit(solution)/shard_map/ppermute | solution.py:61
  48.4 5.8 %collective-permute-start.5 = (bf16[64,3072]{1,0:T(8,128)(2,1)S(1)}, bf16[64,3072]{1,0:T(8,128)(2,1)S(1)}, u32[]{:S(2)}, u32[]{:S(2)}) collective-permute-start(bf16[64,3072]{1,0:T(8,128)(2,1)S(1)} %get-tuple-element.62), channel_id=1, source_target_pairs={{0,1},{1,0},{2,3},{3,2},{4,5},{5,4},{6,7},{7,6},{8,9},{9,8},{10,11... | collective-permute-start | bytes 1179656 | tf_op jit(solution)/shard_map/ppermute | solution.py:61
  49.8 4.4 %collective-permute-start.4 = (bf16[64,3072]{1,0:T(8,128)(2,1)S(1)}, bf16[64,3072]{1,0:T(8,128)(2,1)S(1)}, u32[]{:S(2)}, u32[]{:S(2)}) collective-permute-start(bf16[64,3072]{1,0:T(8,128)(2,1)S(1)} %get-tuple-element.61), channel_id=1, source_target_pairs={{0,1},{1,0},{2,3},{3,2},{4,5},{5,4},{6,7},{7,6},{8,9},{9,8},{10,11... | collective-permute-start | bytes 1179656 | tf_op jit(solution)/shard_map/ppermute | solution.py:61
  58.1 2.4 %collective-permute-start.8 = (bf16[256,1536]{1,0:T(8,128)(2,1)S(1)}, bf16[256,1536]{1,0:T(8,128)(2,1)S(1)}, u32[]{:S(2)}, u32[]{:S(2)}) collective-permute-start(bf16[256,1536]{1,0:T(8,128)(2,1)S(1)} %get-tuple-element.79), channel_id=1, source_target_pairs={{0,1},{1,0},{2,3},{3,2},{4,5},{5,4},{6,7},{7,6},{8,9},{9,8},{10,11... | collective-permute-start | bytes 2359304 | tf_op jit(solution)/shard_map/ppermute | solution.py:61
  58.2 7.8 %collective-permute-start.10 = (bf16[256,1536]{1,0:T(8,128)(2,1)S(1)}, bf16[256,1536]{1,0:T(8,128)(2,1)S(1)}, u32[]{:S(2)}, u32[]{:S(2)}) collective-permute-start(bf16[256,1536]{1,0:T(8,128)(2,1)S(1)} %get-tuple-element.86), channel_id=1, source_target_pairs={{0,1},{1,0},{2,3},{3,2},{4,5},{5,4},{6,7},{7,6},{8,9},{9,8},{10,11... | collective-permute-start | bytes 2359304 | tf_op jit(solution)/shard_map/ppermute | solution.py:61
  60.7 8.5 %collective-permute-start.9 = (bf16[128,1536]{1,0:T(8,128)(2,1)S(1)}, bf16[128,1536]{1,0:T(8,128)(2,1)S(1)}, u32[]{:S(2)}, u32[]{:S(2)}) collective-permute-start(bf16[128,1536]{1,0:T(8,128)(2,1)S(1)} %give.6), channel_id=1, source_target_pairs={{0,4},{1,33},{2,6},{3,35},{4,0},{5,37},{6,2},{7,39},{8,12},{9,41},... | collective-permute-start | bytes 1179656 | tf_op jit(solution)/shard_map/ppermute | solution.py:61
  64.0 18.5 %collective-permute-start.14 = (bf16[128,1536]{1,0:T(8,128)(2,1)S(1)}, bf16[128,1536]{1,0:T(8,128)(2,1)S(1)}, u32[]{:S(2)}, u32[]{:S(2)}) collective-permute-start(bf16[128,1536]{1,0:T(8,128)(2,1)S(1)} %give.10), channel_id=1, source_target_pairs={{0,6},{1,49},{2,0},{3,51},{4,2},{5,53},{6,4},{7,55},{8,14},{9,57},... | collective-permute-start | bytes 1179656 | tf_op jit(solution)/shard_map/ppermute | solution.py:61
  65.2 17.3 %collective-permute-start.15 = (bf16[128,1536]{1,0:T(8,128)(2,1)S(1)}, bf16[128,1536]{1,0:T(8,128)(2,1)S(1)}, u32[]{:S(2)}, u32[]{:S(2)}) collective-permute-start(bf16[128,1536]{1,0:T(8,128)(2,1)S(1)} %give.11), channel_id=1, source_target_pairs={{0,2},{1,17},{2,4},{3,19},{4,6},{5,21},{6,0},{7,23},{8,10},{9,25},... | collective-permute-start | bytes 1179656 | tf_op jit(solution)/shard_map/ppermute | solution.py:61
  66.3 16.2 %collective-permute-start.11 = (bf16[128,1536]{1,0:T(8,128)(2,1)S(1)}, bf16[128,1536]{1,0:T(8,128)(2,1)S(1)}, u32[]{:S(2)}, u32[]{:S(2)}) collective-permute-start(bf16[128,1536]{1,0:T(8,128)(2,1)S(1)} %give.7), channel_id=1, source_target_pairs={{0,6},{1,49},{2,0},{3,51},{4,2},{5,53},{6,4},{7,55},{8,14},{9,57},... | collective-permute-start | bytes 1179656 | tf_op jit(solution)/shard_map/ppermute | solution.py:61
  68.6 13.9 %collective-permute-start.12 = (bf16[128,1536]{1,0:T(8,128)(2,1)S(1)}, bf16[128,1536]{1,0:T(8,128)(2,1)S(1)}, u32[]{:S(2)}, u32[]{:S(2)}) collective-permute-start(bf16[128,1536]{1,0:T(8,128)(2,1)S(1)} %give.8), channel_id=1, source_target_pairs={{0,2},{1,17},{2,4},{3,19},{4,6},{5,21},{6,0},{7,23},{8,10},{9,25},... | collective-permute-start | bytes 1179656 | tf_op jit(solution)/shard_map/ppermute | solution.py:61
  69.2 13.3 %collective-permute-start.13 = (bf16[128,1536]{1,0:T(8,128)(2,1)S(1)}, bf16[128,1536]{1,0:T(8,128)(2,1)S(1)}, u32[]{:S(2)}, u32[]{:S(2)}) collective-permute-start(bf16[128,1536]{1,0:T(8,128)(2,1)S(1)} %give.9), channel_id=1, source_target_pairs={{0,4},{1,33},{2,6},{3,35},{4,0},{5,37},{6,2},{7,39},{8,12},{9,41},... | collective-permute-start | bytes 1179656 | tf_op jit(solution)/shard_map/ppermute | solution.py:61
  98.8 3.2 %collective-permute-start.16 = (bf16[4,3072]{1,0:T(4,128)(2,1)S(1)}, bf16[4,3072]{1,0:T(4,128)(2,1)S(1)}, u32[]{:S(2)}, u32[]{:S(2)}) collective-permute-start(bf16[4,3072]{1,0:T(4,128)(2,1)S(1)} %get-tuple-element.91), channel_id=1, source_target_pairs={{0,1},{1,0},{2,3},{3,2},{4,5},{5,4},{6,7},{7,6},{8,9},{9,8},{10,11... | collective-permute-start | bytes 73736 | tf_op jit(solution)/shard_map/ppermute | solution.py:61

commit v4 on v2

v4 whole, which is shorter than its diff:
```python
import functools

import jax
import jax.numpy as jnp
from jax import lax
from jax.experimental import pallas as pl
from jax.experimental.pallas import tpu as pltpu
from jax.sharding import PartitionSpec as P

QH = 48
KVH = 8
HD = 128
TOPK = 4
D = 6144
HALF = D // 2
FF = 672
META = 128
KB = 512
ALL = ("ctx", "grp")
BF = jnp.bfloat16
F32 = jnp.float32


def coords(i):
    c, g = divmod(i, 16)
    return {"x": (g >> 1) & 3, "y": c & 3, "z": ((g >> 3) << 1) | (c >> 2), "core": g & 1}


def index(x, y, z, core):
    return (((z & 1) << 2) | y) * 16 + (((z >> 1) << 3) | (x << 1) | core)


def shifted(axes, k):
    pairs = []
    for i in range(128):
        at = coords(i)
        axis = axes[at["core"]]
        at[axis] = (at[axis] + k) % (2 if axis == "core" else 4)
        pairs.append((i, index(**at)))
    return pairs


OUTER = ("x", "y")
INNER = ("y", "x")
CORE = ("core", "core")
PLANES = [
    [index(**{INNER[core]: i, OUTER[core]: o, "z": z, "core": core}) for i in range(4) for z in range(4)]
    for core in range(2)
    for o in range(4)
]


def move(a, axes, k):
    return lax.ppermute(a, ALL, shifted(axes, k % 4 if axes is not CORE else 1))


def call(kernel, outs, *args, name, limit=8, **kw):
    return pl.pallas_call(
        kernel,
        out_shape=outs,
        compiler_params=pltpu.CompilerParams(vmem_limit_bytes=limit << 20),
        cost_estimate=pl.CostEstimate(flops=0, bytes_accessed=0, transcendentals=0),
        name=name,
        **kw,
    )(*args)


VMEM = pl.BlockSpec(memory_space=pltpu.VMEM)
SMEM = pl.BlockSpec(memory_space=pltpu.SMEM)
HBM = pl.BlockSpec(memory_space=pltpu.HBM)


def in_hbm(*arrays):
    return [pltpu.with_memory_space_constraint(a, pltpu.HBM) for a in arrays]


def shape(*dims, dtype=BF):
    return jax.ShapeDtypeStruct(dims, dtype)


def pack_kernel(x_at, routes_at, weights_at, out, x, routes, weights, sems):
    copies = [
        pltpu.make_async_copy(a, b, sems.at[i])
        for i, (a, b) in enumerate(((x_at, x), (routes_at, routes), (weights_at, weights)))
    ]
    for copy in copies:
        copy.start()
    for copy in copies:
        copy.wait()
    row = lax.broadcasted_iota(jnp.int32, (4, TOPK), 0)
    place = lax.broadcasted_iota(jnp.int32, (4, TOPK), 1)
    named = jnp.zeros((4, TOPK), jnp.int32)
    for r in range(4):
        for k in range(TOPK):
            named = jnp.where((row == r) & (place == k), routes[r, k], named)
    code = 2 * named
    for r in range(3):
        for k in range(TOPK):
            code += jnp.where((named == routes[r, k]) & (row > r), 1, 0)
    share = weights[...] / jnp.sum(weights[...], axis=1, keepdims=True)
    high = share.astype(BF).astype(F32)
    middle = (share - high).astype(BF).astype(F32)
    lane = lax.broadcasted_iota(jnp.int32, (4, META), 1)
    meta = jnp.zeros((4, META), F32)
    for j, part in enumerate((code.astype(F32), high, middle, share - high - middle)):
        for k in range(TOPK):
            meta = jnp.where(lane == j * TOPK + k, part[:, k : k + 1], meta)
    meta = meta.astype(BF)
    for target in range(16):
        out[target, :, :D] = x[...]
        out[target, :, D:] = meta


def pack(x, routes, weights):
    return call(
        pack_kernel,
        shape(16, 4, D + META),
        *in_hbm(x, routes, weights),
        name="pack",
        in_specs=[HBM] * 3,
        out_specs=VMEM,
        scratch_shapes=[
            pltpu.VMEM((4, D), BF),
            pltpu.SMEM((4, TOPK), jnp.int32),
            pltpu.VMEM((4, TOPK), F32),
            pltpu.SemaphoreType.DMA((3,)),
        ],
    )


def load_kernel(gate_at, up_at, down_at, gate, up, down, sems):
    parts = 3
    copies = []
    for i, (a, b) in enumerate(((gate_at, gate), (up_at, up), (down_at, down))):
        for p in range(parts):
            rows = pl.ds(p * (FF // parts), FF // parts)
            copies.append(pltpu.make_async_copy(a.at[rows], b.at[rows], sems.at[i, p]))
    for copy in copies:
        copy.start()
    for copy in copies:
        copy.wait()


def load(gate_w, up_w, down_w):
    return call(
        load_kernel,
        [pltpu.VMEM((FF, D), BF)] * 3,
        *in_hbm(gate_w, up_w, down_w),
        name="load",
        in_specs=[HBM] * 3,
        out_specs=[VMEM] * 3,
        scratch_shapes=[pltpu.SemaphoreType.DMA((3, 3))],
    )


def choose_kernel(expert, rows, mine, theirs, chosen):
    meta = rows[:, D:].astype(F32)
    row = lax.broadcasted_iota(jnp.int32, (64, 64), 0)
    lane = lax.broadcasted_iota(jnp.int32, (64, 64), 1)
    wanted = 2 * jnp.where(lane < 32, expert[0], expert[0] ^ 1) + lane % 2
    wanted = jnp.where(row // 4 == (lane % 32) // 2, wanted, -1).astype(F32)
    ones = jnp.zeros((64, 64), F32)
    for k in range(TOPK):
        ones += jnp.where(meta[:, k : k + 1] == wanted, 1.0, 0.0)
    chosen[...] = ones.astype(BF)
    for at in range(0, D + META, KB):
        here = slice(at, min(at + KB, D + META))
        found = lax.dot_general(
            chosen[...], rows[:, here], (((0,), (0,)), ((), ())), preferred_element_type=F32
        ).astype(BF)
        mine[:, here] = found[:32]
        theirs[:, here] = found[32:]


def choose(expert, rows):
    return call(
        choose_kernel,
        [shape(32, D + META), shape(32, D + META), shape(64, 64)],
        expert,
        rows,
        name="choose",
        in_specs=[SMEM, VMEM],
        out_specs=[VMEM] * 3,
    )


def across(weights, rows):
    return lax.dot_general(weights, rows, (((1,), (1,)), ((), ())), preferred_element_type=F32)


def expert_kernel(expert, *refs):
    picked, (gate_w, up_w, down_w, *outs) = refs[:8], refs[8:]
    rows = jnp.concatenate([r[:, :D] for r in picked], axis=0)
    meta = jnp.concatenate([r[:, D:] for r in picked], axis=0).astype(F32)
    share = jnp.zeros((256, 1), F32)
    for k in range(TOPK):
        of_row = sum(meta[:, j * TOPK + k : j * TOPK + k + 1] for j in (1, 2, 3))
        slot = meta[:, k : k + 1] - (2 * expert[0]).astype(F32)
        share += jnp.where((slot == 0.0) | (slot == 1.0), of_row, 0.0)
    gate, up = across(gate_w[...], rows), across(up_w[...], rows)
    hidden = ((gate / (1.0 + jnp.exp(-gate)) * up).T * share).astype(BF)
    for c in range(2):
        here = slice(c * HALF, (c + 1) * HALF)
        rows = jnp.dot(hidden, down_w[:, here], preferred_element_type=F32).astype(BF)
        outs[2 * c][...] = rows[:128]
        outs[2 * c + 1][...] = rows[128:]


def expert_rows(expert, own, other, gate_w, up_w, down_w):
    return call(
        expert_kernel,
        [shape(128, HALF)] * 4,
        expert,
        *own,
        *other,
        gate_w,
        up_w,
        down_w,
        name="expert",
        limit=16,
        in_specs=[SMEM] + [VMEM] * 11,
        out_specs=[VMEM] * 4,
    )


def given(chosen, mine, theirs, at):
    here = slice(at, at + KB)
    rows = jnp.concatenate([mine[:, here], theirs[:, here]], axis=0)
    return jnp.dot(chosen[...], rows, preferred_element_type=F32)


def give_kernel(chosen, mine, theirs, out):
    for at in range(0, HALF, KB):
        out[:, at : at + KB] = given(chosen, mine, theirs, at).astype(BF)


def give(chosen, mine, theirs, k):
    slots = pl.BlockSpec((32, HALF), lambda i: (k, 0))
    return call(
        give_kernel,
        shape(64, HALF),
        chosen,
        mine,
        theirs,
        name="give",
        grid=(1,),
        in_specs=[pl.BlockSpec((64, 64), lambda i: (0, 0)), slots, slots],
        out_specs=pl.BlockSpec((64, HALF), lambda i: (0, 0)),
    )


def join_kernel(chosen, *refs):
    parts, out = refs[:-1], refs[-1]
    for c in range(2):
        mine, theirs, *arrived = parts[5 * c : 5 * c + 5]
        for at in range(0, HALF, KB):
            rows = given(chosen, mine, theirs, at)
            for part in arrived:
                rows += part[:, at : at + KB].astype(F32)
            rows = rows.astype(BF)
            for block in range(16):
                out[block, :, c * HALF + at : c * HALF + at + KB] = rows[4 * block : 4 * block + 4]


def join(chosen, parts):
    slots = pl.BlockSpec((32, HALF), lambda i: (0, 0))
    rows = pl.BlockSpec((64, HALF), lambda i: (0, 0))
    return call(
        join_kernel,
        shape(16, 4, D),
        chosen,
        *parts,
        name="join",
        grid=(1,),
        in_specs=[pl.BlockSpec((64, 64), lambda i: (0, 0))] + [slots, slots, rows, rows, rows] * 2,
        out_specs=pl.BlockSpec((16, 4, D), lambda i: (0, 0, 0)),
    )


def fold_kernel(parts, out):
    out[...] = sum(parts[s].astype(F32) for s in range(16)).astype(BF)


def attend_kernel(place, lengths_at, *refs):
    given, out, held, sems = refs[:5], refs[5], refs[6:12], refs[12]
    copies = [
        pltpu.make_async_copy(a, b, sems.at[i]) for i, (a, b) in enumerate(zip((lengths_at,) + given, held))
    ]
    for copy in copies:
        copy.start()
    for copy in copies:
        copy.wait()
    lengths, queries, keys, values, new_key, new_value = held
    group = QH // KVH
    local = keys.shape[1]
    leader = place[0] == 0
    position = place[0] * local + lax.broadcasted_iota(jnp.int32, (group, local), 1)
    lane = lax.broadcasted_iota(jnp.int32, (group, HD), 1)
    out[...] = jnp.zeros_like(out)
    for r in range(2):
        live = position < lengths[r]
        for j in range(KVH):
            head = slice(j * HD, (j + 1) * HD)
            q = queries[r, j]
            scores = across(q, keys[r, :, head]) * HD ** (-0.5)
            own = jnp.sum(
                q.astype(F32) * new_key[r : r + 1, head].astype(F32), axis=1, keepdims=True
            ) * HD ** (-0.5)
            top = jnp.max(jnp.where(live, scores, -1e30), axis=1, keepdims=True)
            top = jnp.where(leader, jnp.maximum(top, own), top)
            top = top.astype(BF).astype(F32)
            weights = jnp.where(live, jnp.exp(scores - top), 0.0)
            own = jnp.where(leader, jnp.exp(own - top), 0.0)
            total = jnp.sum(weights, axis=1, keepdims=True) + own
            high = weights.astype(BF)
            low = (weights - high.astype(F32)).astype(BF)
            value = values[r, :, head]
            mixed = jnp.dot(high, value, preferred_element_type=F32)
            mixed += jnp.dot(low, value, preferred_element_type=F32)
            mixed += own * new_value[r : r + 1, head].astype(F32)
            total_high = total.astype(BF).astype(F32)
            stats = jnp.where(lane == 0, top, jnp.where(lane == 1, total_high, total - total_high))
            out[j, 8 * r : 8 * r + group, :HD] = mixed.astype(BF)
            out[j, 8 * r : 8 * r + group, HD:] = stats.astype(BF)


def attend(queries, key_cache, value_cache, new_key, new_value, lengths):
    place = lax.axis_index("ctx").astype(jnp.int32).reshape(1)
    queries = queries.reshape(2, KVH, QH // KVH, HD)
    return call(
        attend_kernel,
        shape(KVH, 16, 2 * HD),
        place,
        *in_hbm(lengths, queries, key_cache, value_cache, new_key, new_value),
        name="attend",
        in_specs=[SMEM] + [HBM] * 6,
        out_specs=VMEM,
        scratch_shapes=[pltpu.SMEM((2,), jnp.int32)]
        + [pltpu.VMEM(a.shape, a.dtype) for a in (queries, key_cache, value_cache, new_key, new_value)]
        + [pltpu.SemaphoreType.DMA((6,))],
    )


def heads_kernel(parts, out):
    group = QH // KVH
    tops = [parts[s, :, HD : HD + 1].astype(F32) for s in range(KVH)]
    peak = functools.reduce(jnp.maximum, tops)
    mixed = jnp.zeros((16, HD), F32)
    total = jnp.zeros((16, 1), F32)
    for s in range(KVH):
        scale = jnp.exp(tops[s] - peak)
        mixed += scale * parts[s, :, :HD].astype(F32)
        total += scale * sum(parts[s, :, HD + i : HD + i + 1].astype(F32) for i in (1, 2))
    mixed = (mixed / total).astype(BF)
    for r in range(2):
        for g in range(group):
            out[r : r + 1, g * HD : (g + 1) * HD] = mixed[8 * r + g : 8 * r + g + 1]


def body(
    queries,
    key_cache,
    value_cache,
    new_key,
    new_value,
    lengths,
    moe_input,
    routes,
    route_weights,
    w_gate,
    w_up,
    w_down,
):
    expert = lax.axis_index("grp").astype(jnp.int32).reshape(1)

    sent = pack(moe_input, routes, route_weights)
    plane = lax.all_to_all(sent, ALL, 0, 0, axis_index_groups=PLANES, tiled=True)
    packed = attend(queries, key_cache, value_cache, new_key, new_value, lengths)
    weights = (w_gate[0].T, w_up[0].T, w_down[0])
    plane, packed, weights, expert = lax.optimization_barrier((plane, packed, weights, expert))
    plane = plane.reshape(64, D + META)
    shards = [plane] + [move(plane, OUTER, k) for k in (1, 2, 3)]

    gate_w, up_w, down_w = load(*weights)
    shards[1], gate_w = lax.optimization_barrier((shards[1], gate_w))

    chosen, own, other = [None] * 4, [None] * 4, [None] * 4
    for k in (0, 1, 3, 2):
        own[k], theirs, chosen[k] = choose(expert, shards[k])
        other[k] = move(theirs, CORE, 1)
    sums = expert_rows(expert, own, other, gate_w, up_w, down_w)

    parts = []
    for c in range(2):
        mine, theirs = sums[2 * c : 2 * c + 2]
        theirs = move(theirs, CORE, 1)
        rows = [give(chosen[k], mine, theirs, k) for k in (1, 3, 2)]
        if c == 1:
            rows[-1], packed = lax.optimization_barrier((rows[-1], packed))
        parts += [mine, theirs] + [move(r, OUTER, -k) for r, k in zip(rows, (1, 3, 2))]

    head_parts = lax.all_to_all(packed, "ctx", 0, 0, tiled=True)
    head_outputs = call(heads_kernel, shape(2, HD * QH // KVH), head_parts, name="heads")
    parts[-1], head_outputs = lax.optimization_barrier((parts[-1], head_outputs))
    sums = lax.all_to_all(
        join(chosen[0], parts), ALL, 0, 0, axis_index_groups=PLANES, tiled=True
    )
    return head_outputs, call(fold_kernel, shape(4, D), sums, name="fold")


def solution(mesh):
    placed = (
        P("grp", None),
        P("grp", "ctx", None),
        P("grp", "ctx", None),
        P("grp", None),
        P("grp", None),
        P("grp"),
        P(ALL, None),
        P(ALL, None),
        P(ALL, None),
        P("grp", None, "ctx"),
        P("grp", None, "ctx"),
        P("grp", "ctx", None),
    )
    return jax.shard_map(
        body,
        mesh=mesh,
        in_specs=placed,
        out_specs=(P("grp", "ctx"), P(ALL, None)),
        check_vma=False,
    )
```

time: 109 us -> 102 us (0.936); the launches traced: 109 us -> 100 us
  blocking collectives: 12.5 us -> 25.9 us
  starting transfers between devices: 41 us -> 27.7 us
  waiting for transfers between devices: 26.5 us -> 19.6 us
  Pallas kernels: 26.4 us -> 24.9 us
    all_to_all x1 -> x2, blocking collectives: 12.5 us -> 25.9 us  [the longest x1 15.4 us: body(): lax.all_to_all(join(chosen[0], parts), ALL, 0, 0, axis_index_groups=PLANE...]
    ppermute x21 -> x15, waiting for transfers between devices: 22.8 us -> 11 us  [move(): return lax.ppermute(a, ALL, shifted(axes, k % 4 if axes is not CORE else 1))]
    ppermute x21 -> x15, starting transfers between devices: 30 us -> 19.2 us  [move(): return lax.ppermute(a, ALL, shifted(axes, k % 4 if axes is not CORE else 1))]
    all_to_all x2 -> x1, waiting for transfers between devices: 3.75 us -> 8.64 us  [body(): lax.all_to_all(sent, ALL, 0, 0, axis_index_groups=PLANES, tiled=True)]
    all_to_all x2 -> x1, starting transfers between devices: 11 us -> 8.44 us  [body(): lax.all_to_all(sent, ALL, 0, 0, axis_index_groups=PLANES, tiled=True)]
    pallas_call x23 -> x17, Pallas kernels: 26.4 us -> 24.9 us  [call(): pl.pallas_call(kernel, out_shape=outs, compiler_params=pltpu.CompilerPara...]
  transfers between devices with their start and end apart: 23 -> 16, of which waited for: 14 -> 6; matrix products, arithmetic and copies ran while one was open for 1% -> 1% of each run, Pallas kernels for 18% -> 15%
where the time goes in v4:
time: 102 us; the launch traced here: 100 us
  starting transfers between devices  27.7 us (27%)
  blocking collectives  25.9 us (25%)
  Pallas kernels  24.9 us (24%)
  waiting for transfers between devices  19.6 us (19%)
  local copies, waits for them, and re-layouts  1.56 us (2%)
    pallas_call x17, Pallas kernels, call(): pl.pallas_call(kernel, out_shape=outs, compiler_params=pltpu.CompilerPara...  24.9 us
    ppermute x15, starting transfers between devices, move(): return lax.ppermute(a, ALL, shifted(axes, k % 4 if axes is not CORE else 1))  19.2 us
    all_to_all x1, blocking collectives, body(): lax.all_to_all(join(chosen[0], parts), ALL, 0, 0, axis_index_groups=PLANE...  15.4 us
    ppermute x15, waiting for transfers between devices, move(): return lax.ppermute(a, ALL, shifted(axes, k % 4 if axes is not CORE else 1))  11 us
    all_to_all x1, blocking collectives, body(): head_parts = lax.all_to_all(packed, 'ctx', 0, 0, tiled=True)  10.5 us
    all_to_all x1, waiting for transfers between devices, body(): lax.all_to_all(sent, ALL, 0, 0, axis_index_groups=PLANES, tiled=True)  8.64 us
    all_to_all x1, starting transfers between devices, body(): lax.all_to_all(sent, ALL, 0, 0, axis_index_groups=PLANES, tiled=True)  8.44 us
  transfers between devices with their start and end apart: 16, of which 6 were waited for; matrix products, arithmetic and copies ran while one was open for 1% of the time, Pallas kernels for 15%

profile of v4, /device:TPU:1, one launch (start us, length us, event | category | flops | bytes accessed | tf_op | source)
XLA Modules:
  0.0 100.4 jit_solution(11872041244440091907)
XLA Ops:
  0.6 1.9 %pack.1 = bf16[16,4,6272]{2,1,0:T(4,128)(2,1)} custom-call(bf16[4,6144]{1,0:T(4,128)(2,1)} %x_at.1, s32[4,4]{1,0:T(4,128)} %routes_at.1, f32[4,4]{1,0:T(4,128)} %weights_at.1), custom_call_target="tpu_custom_call" | custom-call | tf_op jit(solution)/shard_map/pack/pallas_call | solution.py:58
  2.6 8.4 %all-to-all-start = ((bf16[16,4,6272]{2,1,0:T(4,128)(2,1)}), bf16[16,4,6272]{2,1,0:T(4,128)(2,1)S(1)}, u32[]{:S(2)}, u32[]{:S(2)}) async-start(bf16[16,4,6272]{2,1,0:T(4,128)(2,1)} %pack.1), calls=%async_computation | async-start | bytes 1605632 | tf_op jit(solution)/shard_map/all_to_all | solution.py:377
  11.0 1.4 %reshape.17.refs_0_ = bf16[2,8,6,128]{3,2,1,0:T(8,128)(2,1)} reshape(bf16[2,6144]{1,0:T(2,128)(2,1)} %param.12) | data formatting | bytes 49152 | tf_op jit(solution)/shard_map/reshape | solution.py:329
  12.4 2.2 %attend.1 = bf16[8,16,256]{2,1,0:T(8,128)(2,1)S(1)} custom-call(s32[1]{0:T(128)} %bitcast.place, s32[2]{0:T(128)} %lengths_at.1, bf16[2,8,6,128]{3,2,1,0:T(8,128)(2,1)} %reshape.17.refs_0_, bf16[2,128,1024]{2,1,0:T(8,128)(2,1)} %refs_1_.1, bf16[2,128,1024]{2,1,0:T(8,128)(2,1)} %refs_2_.1, bf16[2,1024]{1,0:T(2,128)(2,1)} %refs_3_.1, bf16[2,1024]{1,0:T(2,128)(2,1)} %refs_4_.1), custom_call_target="tpu_custom_call" | custom-call | tf_op jit(solution)/shard_map/attend/pallas_call | solution.py:58
  14.6 8.6 %all-to-all-done = bf16[16,4,6272]{2,1,0:T(4,128)(2,1)S(1)} async-done(((bf16[16,4,6272]{2,1,0:T(4,128)(2,1)}), bf16[16,4,6272]{2,1,0:T(4,128)(2,1)S(1)}, u32[]{:S(2)}, u32[]{:S(2)}) %all-to-all-start) | async-done | bytes 802848 | tf_op jit(solution)/shard_map/all_to_all | solution.py:377
  23.2 0.2 reshape.19.rows
  23.4 2.7 %collective-permute-start.2 = (bf16[64,6272]{1,0:T(8,128)(2,1)S(1)}, bf16[64,6272]{1,0:T(8,128)(2,1)S(1)}, u32[]{:S(2)}, u32[]{:S(2)}) collective-permute-start(bf16[64,6272]{1,0:T(8,128)(2,1)S(1)} %reshape.19.rows), channel_id=1, source_target_pairs={{0,6},{1,49},{2,0},{3,51},{4,2},{5,53},{6,4},{7,55},{8,14},{9,57},... | collective-permute-start | bytes 2408456 | tf_op jit(solution)/shard_map/ppermute | solution.py:54
  26.1 0.8 collective-permute-start
  27.0 0.7 collective-permute-start.1
  27.6 0.5 choose.5
  28.1 1.1 %collective-permute-start.3 = (bf16[32,6272]{1,0:T(8,128)(2,1)S(1)}, bf16[32,6272]{1,0:T(8,128)(2,1)S(1)}, u32[]{:S(2)}, u32[]{:S(2)}) collective-permute-start(bf16[32,6272]{1,0:T(8,128)(2,1)S(1)} %get-tuple-element.45), channel_id=1, source_target_pairs={{0,1},{1,0},{2,3},{3,2},{4,5},{5,4},{6,7},{7,6},{8,9},{9,8},{10,11... | collective-permute-start | bytes 1204232 | tf_op jit(solution)/shard_map/ppermute | solution.py:54
  29.3 8.2 %load.1 = (bf16[672,6144]{1,0:T(8,128)(2,1)S(1)}, bf16[672,6144]{1,0:T(8,128)(2,1)S(1)}, bf16[672,6144]{1,0:T(8,128)(2,1)S(1)}) custom-call(bf16[672,6144]{1,0:T(8,128)(2,1)} %bitcast.9, bf16[672,6144]{1,0:T(8,128)(2,1)} %bitcast.10, bf16[672,6144]{1,0:T(8,128)(2,1)} %bitcast.11), custom_call_target="tpu_custom_call" | custom-call | tf_op jit(solution)/shard_map/load/pallas_call | solution.py:58
  37.5 6.4 %collective-permute-done.2.rows = bf16[64,6272]{1,0:T(8,128)(2,1)S(1)} collective-permute-done((bf16[64,6272]{1,0:T(8,128)(2,1)S(1)}, bf16[64,6272]{1,0:T(8,128)(2,1)S(1)}, u32[]{:S(2)}, u32[]{:S(2)}) %collective-permute-start.2) | collective-permute-done | bytes 802848 | tf_op jit(solution)/shard_map/ppermute | solution.py:54
  43.8 0.5 choose.7
  44.3 1.5 %collective-permute-start.6 = (bf16[32,6272]{1,0:T(8,128)(2,1)S(1)}, bf16[32,6272]{1,0:T(8,128)(2,1)S(1)}, u32[]{:S(2)}, u32[]{:S(2)}) collective-permute-start(bf16[32,6272]{1,0:T(8,128)(2,1)S(1)} %get-tuple-element.48), channel_id=1, source_target_pairs={{0,1},{1,0},{2,3},{3,2},{4,5},{5,4},{6,7},{7,6},{8,9},{9,8},{10,11... | collective-permute-start | bytes 1204232 | tf_op jit(solution)/shard_map/ppermute | solution.py:54
  45.9 0.0 collective-permute-done.rows
  45.9 0.5 choose.4
  46.4 0.1 collective-permute-start.5
  46.5 1.1 %collective-permute-done.1.rows = bf16[64,6272]{1,0:T(8,128)(2,1)S(1)} collective-permute-done((bf16[64,6272]{1,0:T(8,128)(2,1)S(1)}, bf16[64,6272]{1,0:T(8,128)(2,1)S(1)}, u32[]{:S(2)}, u32[]{:S(2)}) %collective-permute-start.1) | collective-permute-done | bytes 802848 | tf_op jit(solution)/shard_map/ppermute | solution.py:54
  47.5 0.5 choose.6
  48.0 1.8 %collective-permute-start.4 = (bf16[32,6272]{1,0:T(8,128)(2,1)S(1)}, bf16[32,6272]{1,0:T(8,128)(2,1)S(1)}, u32[]{:S(2)}, u32[]{:S(2)}) collective-permute-start(bf16[32,6272]{1,0:T(8,128)(2,1)S(1)} %get-tuple-element.46), channel_id=1, source_target_pairs={{0,1},{1,0},{2,3},{3,2},{4,5},{5,4},{6,7},{7,6},{8,9},{9,8},{10,11... | collective-permute-start | bytes 1204232 | tf_op jit(solution)/shard_map/ppermute | solution.py:54
  49.8 0.0 collective-permute-done.3.refs_4_
  49.8 0.0 collective-permute-done.6.refs_7_
  49.8 0.0 collective-permute-done.5.refs_6_
  49.8 1.3 %collective-permute-done.4.refs_5_ = bf16[32,6272]{1,0:T(8,128)(2,1)S(1)} collective-permute-done((bf16[32,6272]{1,0:T(8,128)(2,1)S(1)}, bf16[32,6272]{1,0:T(8,128)(2,1)S(1)}, u32[]{:S(2)}, u32[]{:S(2)}) %collective-permute-start.4) | collective-permute-done | bytes 401440 | tf_op jit(solution)/shard_map/ppermute | solution.py:54
  51.2 7.0 %expert.1 = (bf16[128,3072]{1,0:T(8,128)(2,1)S(1)}, bf16[128,3072]{1,0:T(8,128)(2,1)S(1)}, bf16[128,3072]{1,0:T(8,128)(2,1)S(1)}, bf16[128,3072]{1,0:T(8,128)(2,1)S(1)}) custom-call(s32[1]{0:T(128)} %bitcast.6.expert, bf16[32,6272]{1,0:T(8,128)(2,1)S(1)} %get-tuple-element.36.refs_0_, bf16[32,6272]{1,0:T(8,128)(2,1)S(1)} %get-tuple-element.42.refs_1_, ...), custom_call_target="tpu_custom_call" | custom-call | tf_op jit(solution)/shard_map/expert/pallas_call | solution.py:58
  58.2 0.5 collective-permute-start.7
  58.7 0.1 collective-permute-start.9
  58.8 1.8 %collective-permute-done.7.theirs.refs_6_ = bf16[128,3072]{1,0:T(8,128)(2,1)S(1)} collective-permute-done((bf16[128,3072]{1,0:T(8,128)(2,1)S(1)}, bf16[128,3072]{1,0:T(8,128)(2,1)S(1)}, u32[]{:S(2)}, u32[]{:S(2)}) %collective-permute-start.7) | collective-permute-done | bytes 786464 | tf_op jit(solution)/shard_map/ppermute | solution.py:54
  60.6 0.2 give.6
  60.8 3.0 %collective-permute-start.8 = (bf16[64,3072]{1,0:T(8,128)(2,1)S(1)}, bf16[64,3072]{1,0:T(8,128)(2,1)S(1)}, u32[]{:S(2)}, u32[]{:S(2)}) collective-permute-start(bf16[64,3072]{1,0:T(8,128)(2,1)S(1)} %give.6), channel_id=1, source_target_pairs={{0,4},{1,33},{2,6},{3,35},{4,0},{5,37},{6,2},{7,39},{8,12},{9,41},... | collective-permute-start | bytes 1179656 | tf_op jit(solution)/shard_map/ppermute | solution.py:54
  63.8 0.2 give.10
  64.1 0.8 collective-permute-start.13
  64.9 0.2 give.11
  65.2 1.0 collective-permute-start.14
  66.1 0.0 collective-permute-done.9.theirs.refs_1_
  66.1 0.2 give.7
  66.4 2.0 %collective-permute-start.10 = (bf16[64,3072]{1,0:T(8,128)(2,1)S(1)}, bf16[64,3072]{1,0:T(8,128)(2,1)S(1)}, u32[]{:S(2)}, u32[]{:S(2)}) collective-permute-start(bf16[64,3072]{1,0:T(8,128)(2,1)S(1)} %give.7), channel_id=1, source_target_pairs={{0,6},{1,49},{2,0},{3,51},{4,2},{5,53},{6,4},{7,55},{8,14},{9,57},... | collective-permute-start | bytes 1179656 | tf_op jit(solution)/shard_map/ppermute | solution.py:54
  68.4 0.2 give.8
  68.7 0.1 collective-permute-start.11
  68.7 0.2 give.9
  69.0 0.3 collective-permute-done.8.refs_9_
  69.3 3.0 %collective-permute-start.12 = (bf16[64,3072]{1,0:T(8,128)(2,1)S(1)}, bf16[64,3072]{1,0:T(8,128)(2,1)S(1)}, u32[]{:S(2)}, u32[]{:S(2)}) collective-permute-start(bf16[64,3072]{1,0:T(8,128)(2,1)S(1)} %give.9), channel_id=1, source_target_pairs={{0,4},{1,33},{2,6},{3,35},{4,0},{5,37},{6,2},{7,39},{8,12},{9,41},... | collective-permute-start | bytes 1179656 | tf_op jit(solution)/shard_map/ppermute | solution.py:54
  72.3 10.5 %all_to_all.15.parts = bf16[8,16,256]{2,1,0:T(8,128)(2,1)S(1)} all-to-all(bf16[8,16,256]{2,1,0:T(8,128)(2,1)S(1)} %attend.1), channel_id=1, replica_groups=mesh['ctx'=8,'grp'=16] {'ctx'}, dimensions={0} | all-to-all | bytes 131072 | tf_op jit(solution)/shard_map/all_to_all | solution.py:402
  82.8 0.8 heads.1
  83.6 0.0 collective-permute-done.13.refs_7_
  83.7 0.0 collective-permute-done.14.refs_8_
  83.7 0.0 collective-permute-done.10.refs_2_
  83.7 0.0 collective-permute-done.11.refs_3_
  83.7 0.0 collective-permute-done.12.refs_4_
  83.7 0.6 join.1
  84.3 15.4 %all_to_all.16.parts = bf16[16,4,6144]{2,1,0:T(4,128)(2,1)S(1)} all-to-all(bf16[16,4,6144]{2,1,0:T(4,128)(2,1)S(1)} %join.1), channel_id=1, replica_groups={{0,64,8,72,16,80,24,88,32,96,40,104,48,112,56,120},{2,66,10,74,18,82,26..., dimensions={0} | all-to-all | bytes 1572864 | tf_op jit(solution)/shard_map/all_to_all | solution.py:405
  99.7 0.7 fold.1
Async XLA Ops:
  2.6 20.6 %all-to-all-start = ((bf16[16,4,6272]{2,1,0:T(4,128)(2,1)}), bf16[16,4,6272]{2,1,0:T(4,128)(2,1)S(1)}, u32[]{:S(2)}, u32[]{:S(2)}) async-start(bf16[16,4,6272]{2,1,0:T(4,128)(2,1)} %pack.1), calls=%async_computation | async-start | bytes 1605632 | tf_op jit(solution)/shard_map/all_to_all | solution.py:377
  23.4 20.5 %collective-permute-start.2 = (bf16[64,6272]{1,0:T(8,128)(2,1)S(1)}, bf16[64,6272]{1,0:T(8,128)(2,1)S(1)}, u32[]{:S(2)}, u32[]{:S(2)}) collective-permute-start(bf16[64,6272]{1,0:T(8,128)(2,1)S(1)} %reshape.19.rows), channel_id=1, source_target_pairs={{0,6},{1,49},{2,0},{3,51},{4,2},{5,53},{6,4},{7,55},{8,14},{9,57},... | collective-permute-start | bytes 2408456 | tf_op jit(solution)/shard_map/ppermute | solution.py:54
  26.1 19.7 %collective-permute-start = (bf16[64,6272]{1,0:T(8,128)(2,1)S(1)}, bf16[64,6272]{1,0:T(8,128)(2,1)S(1)}, u32[]{:S(2)}, u32[]{:S(2)}) collective-permute-start(bf16[64,6272]{1,0:T(8,128)(2,1)S(1)} %reshape.19.rows), channel_id=1, source_target_pairs={{0,4},{1,33},{2,6},{3,35},{4,0},{5,37},{6,2},{7,39},{8,12},{9,41},... | collective-permute-start | bytes 2408456 | tf_op jit(solution)/shard_map/ppermute | solution.py:54
  27.0 20.6 %collective-permute-start.1 = (bf16[64,6272]{1,0:T(8,128)(2,1)S(1)}, bf16[64,6272]{1,0:T(8,128)(2,1)S(1)}, u32[]{:S(2)}, u32[]{:S(2)}) collective-permute-start(bf16[64,6272]{1,0:T(8,128)(2,1)S(1)} %reshape.19.rows), channel_id=1, source_target_pairs={{0,2},{1,17},{2,4},{3,19},{4,6},{5,21},{6,0},{7,23},{8,10},{9,25},... | collective-permute-start | bytes 2408456 | tf_op jit(solution)/shard_map/ppermute | solution.py:54
  28.1 21.7 %collective-permute-start.3 = (bf16[32,6272]{1,0:T(8,128)(2,1)S(1)}, bf16[32,6272]{1,0:T(8,128)(2,1)S(1)}, u32[]{:S(2)}, u32[]{:S(2)}) collective-permute-start(bf16[32,6272]{1,0:T(8,128)(2,1)S(1)} %get-tuple-element.45), channel_id=1, source_target_pairs={{0,1},{1,0},{2,3},{3,2},{4,5},{5,4},{6,7},{7,6},{8,9},{9,8},{10,11... | collective-permute-start | bytes 1204232 | tf_op jit(solution)/shard_map/ppermute | solution.py:54
  44.3 5.5 %collective-permute-start.6 = (bf16[32,6272]{1,0:T(8,128)(2,1)S(1)}, bf16[32,6272]{1,0:T(8,128)(2,1)S(1)}, u32[]{:S(2)}, u32[]{:S(2)}) collective-permute-start(bf16[32,6272]{1,0:T(8,128)(2,1)S(1)} %get-tuple-element.48), channel_id=1, source_target_pairs={{0,1},{1,0},{2,3},{3,2},{4,5},{5,4},{6,7},{7,6},{8,9},{9,8},{10,11... | collective-permute-start | bytes 1204232 | tf_op jit(solution)/shard_map/ppermute | solution.py:54
  46.4 3.5 %collective-permute-start.5 = (bf16[32,6272]{1,0:T(8,128)(2,1)S(1)}, bf16[32,6272]{1,0:T(8,128)(2,1)S(1)}, u32[]{:S(2)}, u32[]{:S(2)}) collective-permute-start(bf16[32,6272]{1,0:T(8,128)(2,1)S(1)} %get-tuple-element.47), channel_id=1, source_target_pairs={{0,1},{1,0},{2,3},{3,2},{4,5},{5,4},{6,7},{7,6},{8,9},{9,8},{10,11... | collective-permute-start | bytes 1204232 | tf_op jit(solution)/shard_map/ppermute | solution.py:54
  48.0 3.1 %collective-permute-start.4 = (bf16[32,6272]{1,0:T(8,128)(2,1)S(1)}, bf16[32,6272]{1,0:T(8,128)(2,1)S(1)}, u32[]{:S(2)}, u32[]{:S(2)}) collective-permute-start(bf16[32,6272]{1,0:T(8,128)(2,1)S(1)} %get-tuple-element.46), channel_id=1, source_target_pairs={{0,1},{1,0},{2,3},{3,2},{4,5},{5,4},{6,7},{7,6},{8,9},{9,8},{10,11... | collective-permute-start | bytes 1204232 | tf_op jit(solution)/shard_map/ppermute | solution.py:54
  58.2 2.4 %collective-permute-start.7 = (bf16[128,3072]{1,0:T(8,128)(2,1)S(1)}, bf16[128,3072]{1,0:T(8,128)(2,1)S(1)}, u32[]{:S(2)}, u32[]{:S(2)}) collective-permute-start(bf16[128,3072]{1,0:T(8,128)(2,1)S(1)} %get-tuple-element.53), channel_id=1, source_target_pairs={{0,1},{1,0},{2,3},{3,2},{4,5},{5,4},{6,7},{7,6},{8,9},{9,8},{10,11... | collective-permute-start | bytes 2359304 | tf_op jit(solution)/shard_map/ppermute | solution.py:54
  58.7 7.5 %collective-permute-start.9 = (bf16[128,3072]{1,0:T(8,128)(2,1)S(1)}, bf16[128,3072]{1,0:T(8,128)(2,1)S(1)}, u32[]{:S(2)}, u32[]{:S(2)}) collective-permute-start(bf16[128,3072]{1,0:T(8,128)(2,1)S(1)} %get-tuple-element.60), channel_id=1, source_target_pairs={{0,1},{1,0},{2,3},{3,2},{4,5},{5,4},{6,7},{7,6},{8,9},{9,8},{10,11... | collective-permute-start | bytes 2359304 | tf_op jit(solution)/shard_map/ppermute | solution.py:54
  60.8 8.5 %collective-permute-start.8 = (bf16[64,3072]{1,0:T(8,128)(2,1)S(1)}, bf16[64,3072]{1,0:T(8,128)(2,1)S(1)}, u32[]{:S(2)}, u32[]{:S(2)}) collective-permute-start(bf16[64,3072]{1,0:T(8,128)(2,1)S(1)} %give.6), channel_id=1, source_target_pairs={{0,4},{1,33},{2,6},{3,35},{4,0},{5,37},{6,2},{7,39},{8,12},{9,41},... | collective-permute-start | bytes 1179656 | tf_op jit(solution)/shard_map/ppermute | solution.py:54
  64.1 19.6 %collective-permute-start.13 = (bf16[64,3072]{1,0:T(8,128)(2,1)S(1)}, bf16[64,3072]{1,0:T(8,128)(2,1)S(1)}, u32[]{:S(2)}, u32[]{:S(2)}) collective-permute-start(bf16[64,3072]{1,0:T(8,128)(2,1)S(1)} %give.10), channel_id=1, source_target_pairs={{0,6},{1,49},{2,0},{3,51},{4,2},{5,53},{6,4},{7,55},{8,14},{9,57},... | collective-permute-start | bytes 1179656 | tf_op jit(solution)/shard_map/ppermute | solution.py:54
  65.2 18.5 %collective-permute-start.14 = (bf16[64,3072]{1,0:T(8,128)(2,1)S(1)}, bf16[64,3072]{1,0:T(8,128)(2,1)S(1)}, u32[]{:S(2)}, u32[]{:S(2)}) collective-permute-start(bf16[64,3072]{1,0:T(8,128)(2,1)S(1)} %give.11), channel_id=1, source_target_pairs={{0,2},{1,17},{2,4},{3,19},{4,6},{5,21},{6,0},{7,23},{8,10},{9,25},... | collective-permute-start | bytes 1179656 | tf_op jit(solution)/shard_map/ppermute | solution.py:54
  66.4 17.3 %collective-permute-start.10 = (bf16[64,3072]{1,0:T(8,128)(2,1)S(1)}, bf16[64,3072]{1,0:T(8,128)(2,1)S(1)}, u32[]{:S(2)}, u32[]{:S(2)}) collective-permute-start(bf16[64,3072]{1,0:T(8,128)(2,1)S(1)} %give.7), channel_id=1, source_target_pairs={{0,6},{1,49},{2,0},{3,51},{4,2},{5,53},{6,4},{7,55},{8,14},{9,57},... | collective-permute-start | bytes 1179656 | tf_op jit(solution)/shard_map/ppermute | solution.py:54
  68.7 15.0 %collective-permute-start.11 = (bf16[64,3072]{1,0:T(8,128)(2,1)S(1)}, bf16[64,3072]{1,0:T(8,128)(2,1)S(1)}, u32[]{:S(2)}, u32[]{:S(2)}) collective-permute-start(bf16[64,3072]{1,0:T(8,128)(2,1)S(1)} %give.8), channel_id=1, source_target_pairs={{0,2},{1,17},{2,4},{3,19},{4,6},{5,21},{6,0},{7,23},{8,10},{9,25},... | collective-permute-start | bytes 1179656 | tf_op jit(solution)/shard_map/ppermute | solution.py:54
  69.3 14.3 %collective-permute-start.12 = (bf16[64,3072]{1,0:T(8,128)(2,1)S(1)}, bf16[64,3072]{1,0:T(8,128)(2,1)S(1)}, u32[]{:S(2)}, u32[]{:S(2)}) collective-permute-start(bf16[64,3072]{1,0:T(8,128)(2,1)S(1)} %give.9), channel_id=1, source_target_pairs={{0,4},{1,33},{2,6},{3,35},{4,0},{5,37},{6,2},{7,39},{8,12},{9,41},... | collective-permute-start | bytes 1179656 | tf_op jit(solution)/shard_map/ppermute | solution.py:54

commit v5 on v4

--- a/solution.py
+++ b/solution.py
@@ -85,7 +85,7 @@
     ]
     for copy in copies:
         copy.start()
-    for copy in copies:
+    for copy in copies[1:]:
         copy.wait()
     row = lax.broadcasted_iota(jnp.int32, (4, TOPK), 0)
     place = lax.broadcasted_iota(jnp.int32, (4, TOPK), 1)
@@ -107,8 +107,10 @@
             meta = jnp.where(lane == j * TOPK + k, part[:, k : k + 1], meta)
     meta = meta.astype(BF)
     for target in range(16):
+        out[target, :, D:] = meta
+    copies[0].wait()
+    for target in range(16):
         out[target, :, :D] = x[...]
-        out[target, :, D:] = meta
 
 
 def pack(x, routes, weights):

time: 102 us -> 102 us (level)
  no operation moved by 1% of the time
where the time goes in v5:
time: 102 us; the launch traced here: 100 us
  starting transfers between devices  27.7 us (27%)
  blocking collectives  25.9 us (25%)
  Pallas kernels  24.9 us (24%)
  waiting for transfers between devices  19.6 us (19%)
  local copies, waits for them, and re-layouts  1.56 us (2%)
    pallas_call x17, Pallas kernels, call(): pl.pallas_call(kernel, out_shape=outs, compiler_params=pltpu.CompilerPara...  24.9 us
    ppermute x15, starting transfers between devices, move(): return lax.ppermute(a, ALL, shifted(axes, k % 4 if axes is not CORE else 1))  19.2 us
    all_to_all x1, blocking collectives, body(): lax.all_to_all(join(chosen[0], parts), ALL, 0, 0, axis_index_groups=PLANE...  15.4 us
    ppermute x15, waiting for transfers between devices, move(): return lax.ppermute(a, ALL, shifted(axes, k % 4 if axes is not CORE else 1))  10.9 us
    all_to_all x1, blocking collectives, body(): head_parts = lax.all_to_all(packed, 'ctx', 0, 0, tiled=True)  10.5 us
    all_to_all x1, waiting for transfers between devices, body(): lax.all_to_all(sent, ALL, 0, 0, axis_index_groups=PLANES, tiled=True)  8.64 us
    all_to_all x1, starting transfers between devices, body(): lax.all_to_all(sent, ALL, 0, 0, axis_index_groups=PLANES, tiled=True)  8.44 us
  transfers between devices with their start and end apart: 16, of which 6 were waited for; matrix products, arithmetic and copies ran while one was open for 1% of the time, Pallas kernels for 15%

profile of v5, /device:TPU:1, one launch (start us, length us, event | category | flops | bytes accessed | tf_op | source)
XLA Modules:
  0.0 100.5 jit_solution(6328642456818932245)
XLA Ops:
  0.6 2.0 %pack.1 = bf16[16,4,6272]{2,1,0:T(4,128)(2,1)} custom-call(bf16[4,6144]{1,0:T(4,128)(2,1)} %x_at.1, s32[4,4]{1,0:T(4,128)} %routes_at.1, f32[4,4]{1,0:T(4,128)} %weights_at.1), custom_call_target="tpu_custom_call" | custom-call | tf_op jit(solution)/shard_map/pack/pallas_call | solution.py:58
  2.6 8.4 %all-to-all-start = ((bf16[16,4,6272]{2,1,0:T(4,128)(2,1)}), bf16[16,4,6272]{2,1,0:T(4,128)(2,1)S(1)}, u32[]{:S(2)}, u32[]{:S(2)}) async-start(bf16[16,4,6272]{2,1,0:T(4,128)(2,1)} %pack.1), calls=%async_computation | async-start | bytes 1605632 | tf_op jit(solution)/shard_map/all_to_all | solution.py:379
  11.1 1.4 %reshape.17.refs_0_ = bf16[2,8,6,128]{3,2,1,0:T(8,128)(2,1)} reshape(bf16[2,6144]{1,0:T(2,128)(2,1)} %param.12) | data formatting | bytes 49152 | tf_op jit(solution)/shard_map/reshape | solution.py:331
  12.4 2.2 %attend.1 = bf16[8,16,256]{2,1,0:T(8,128)(2,1)S(1)} custom-call(s32[1]{0:T(128)} %bitcast.place, s32[2]{0:T(128)} %lengths_at.1, bf16[2,8,6,128]{3,2,1,0:T(8,128)(2,1)} %reshape.17.refs_0_, bf16[2,128,1024]{2,1,0:T(8,128)(2,1)} %refs_1_.1, bf16[2,128,1024]{2,1,0:T(8,128)(2,1)} %refs_2_.1, bf16[2,1024]{1,0:T(2,128)(2,1)} %refs_3_.1, bf16[2,1024]{1,0:T(2,128)(2,1)} %refs_4_.1), custom_call_target="tpu_custom_call" | custom-call | tf_op jit(solution)/shard_map/attend/pallas_call | solution.py:58
  14.6 8.6 %all-to-all-done = bf16[16,4,6272]{2,1,0:T(4,128)(2,1)S(1)} async-done(((bf16[16,4,6272]{2,1,0:T(4,128)(2,1)}), bf16[16,4,6272]{2,1,0:T(4,128)(2,1)S(1)}, u32[]{:S(2)}, u32[]{:S(2)}) %all-to-all-start) | async-done | bytes 802848 | tf_op jit(solution)/shard_map/all_to_all | solution.py:379
  23.2 0.2 reshape.19.rows
  23.4 2.7 %collective-permute-start.2 = (bf16[64,6272]{1,0:T(8,128)(2,1)S(1)}, bf16[64,6272]{1,0:T(8,128)(2,1)S(1)}, u32[]{:S(2)}, u32[]{:S(2)}) collective-permute-start(bf16[64,6272]{1,0:T(8,128)(2,1)S(1)} %reshape.19.rows), channel_id=1, source_target_pairs={{0,6},{1,49},{2,0},{3,51},{4,2},{5,53},{6,4},{7,55},{8,14},{9,57},... | collective-permute-start | bytes 2408456 | tf_op jit(solution)/shard_map/ppermute | solution.py:54
  26.2 0.8 collective-permute-start
  27.0 0.7 collective-permute-start.1
  27.7 0.5 choose.5
  28.2 1.1 %collective-permute-start.3 = (bf16[32,6272]{1,0:T(8,128)(2,1)S(1)}, bf16[32,6272]{1,0:T(8,128)(2,1)S(1)}, u32[]{:S(2)}, u32[]{:S(2)}) collective-permute-start(bf16[32,6272]{1,0:T(8,128)(2,1)S(1)} %get-tuple-element.45), channel_id=1, source_target_pairs={{0,1},{1,0},{2,3},{3,2},{4,5},{5,4},{6,7},{7,6},{8,9},{9,8},{10,11... | collective-permute-start | bytes 1204232 | tf_op jit(solution)/shard_map/ppermute | solution.py:54
  29.3 8.2 %load.1 = (bf16[672,6144]{1,0:T(8,128)(2,1)S(1)}, bf16[672,6144]{1,0:T(8,128)(2,1)S(1)}, bf16[672,6144]{1,0:T(8,128)(2,1)S(1)}) custom-call(bf16[672,6144]{1,0:T(8,128)(2,1)} %bitcast.9, bf16[672,6144]{1,0:T(8,128)(2,1)} %bitcast.10, bf16[672,6144]{1,0:T(8,128)(2,1)} %bitcast.11), custom_call_target="tpu_custom_call" | custom-call | tf_op jit(solution)/shard_map/load/pallas_call | solution.py:58
  37.5 6.4 %collective-permute-done.2.rows = bf16[64,6272]{1,0:T(8,128)(2,1)S(1)} collective-permute-done((bf16[64,6272]{1,0:T(8,128)(2,1)S(1)}, bf16[64,6272]{1,0:T(8,128)(2,1)S(1)}, u32[]{:S(2)}, u32[]{:S(2)}) %collective-permute-start.2) | collective-permute-done | bytes 802848 | tf_op jit(solution)/shard_map/ppermute | solution.py:54
  43.9 0.5 choose.7
  44.4 1.5 %collective-permute-start.6 = (bf16[32,6272]{1,0:T(8,128)(2,1)S(1)}, bf16[32,6272]{1,0:T(8,128)(2,1)S(1)}, u32[]{:S(2)}, u32[]{:S(2)}) collective-permute-start(bf16[32,6272]{1,0:T(8,128)(2,1)S(1)} %get-tuple-element.48), channel_id=1, source_target_pairs={{0,1},{1,0},{2,3},{3,2},{4,5},{5,4},{6,7},{7,6},{8,9},{9,8},{10,11... | collective-permute-start | bytes 1204232 | tf_op jit(solution)/shard_map/ppermute | solution.py:54
  45.9 0.0 collective-permute-done.rows
  45.9 0.5 choose.4
  46.4 0.1 collective-permute-start.5
  46.5 1.1 %collective-permute-done.1.rows = bf16[64,6272]{1,0:T(8,128)(2,1)S(1)} collective-permute-done((bf16[64,6272]{1,0:T(8,128)(2,1)S(1)}, bf16[64,6272]{1,0:T(8,128)(2,1)S(1)}, u32[]{:S(2)}, u32[]{:S(2)}) %collective-permute-start.1) | collective-permute-done | bytes 802848 | tf_op jit(solution)/shard_map/ppermute | solution.py:54
  47.6 0.5 choose.6
  48.1 1.8 %collective-permute-start.4 = (bf16[32,6272]{1,0:T(8,128)(2,1)S(1)}, bf16[32,6272]{1,0:T(8,128)(2,1)S(1)}, u32[]{:S(2)}, u32[]{:S(2)}) collective-permute-start(bf16[32,6272]{1,0:T(8,128)(2,1)S(1)} %get-tuple-element.46), channel_id=1, source_target_pairs={{0,1},{1,0},{2,3},{3,2},{4,5},{5,4},{6,7},{7,6},{8,9},{9,8},{10,11... | collective-permute-start | bytes 1204232 | tf_op jit(solution)/shard_map/ppermute | solution.py:54
  49.9 0.0 collective-permute-done.3.refs_4_
  49.9 0.0 collective-permute-done.6.refs_7_
  49.9 0.0 collective-permute-done.5.refs_6_
  49.9 1.3 %collective-permute-done.4.refs_5_ = bf16[32,6272]{1,0:T(8,128)(2,1)S(1)} collective-permute-done((bf16[32,6272]{1,0:T(8,128)(2,1)S(1)}, bf16[32,6272]{1,0:T(8,128)(2,1)S(1)}, u32[]{:S(2)}, u32[]{:S(2)}) %collective-permute-start.4) | collective-permute-done | bytes 401440 | tf_op jit(solution)/shard_map/ppermute | solution.py:54
  51.2 7.0 %expert.1 = (bf16[128,3072]{1,0:T(8,128)(2,1)S(1)}, bf16[128,3072]{1,0:T(8,128)(2,1)S(1)}, bf16[128,3072]{1,0:T(8,128)(2,1)S(1)}, bf16[128,3072]{1,0:T(8,128)(2,1)S(1)}) custom-call(s32[1]{0:T(128)} %bitcast.6.expert, bf16[32,6272]{1,0:T(8,128)(2,1)S(1)} %get-tuple-element.36.refs_0_, bf16[32,6272]{1,0:T(8,128)(2,1)S(1)} %get-tuple-element.42.refs_1_, ...), custom_call_target="tpu_custom_call" | custom-call | tf_op jit(solution)/shard_map/expert/pallas_call | solution.py:58
  58.3 0.5 collective-permute-start.7
  58.7 0.1 collective-permute-start.9
  58.9 1.8 %collective-permute-done.7.theirs.refs_6_ = bf16[128,3072]{1,0:T(8,128)(2,1)S(1)} collective-permute-done((bf16[128,3072]{1,0:T(8,128)(2,1)S(1)}, bf16[128,3072]{1,0:T(8,128)(2,1)S(1)}, u32[]{:S(2)}, u32[]{:S(2)}) %collective-permute-start.7) | collective-permute-done | bytes 786464 | tf_op jit(solution)/shard_map/ppermute | solution.py:54
  60.6 0.2 give.6
  60.9 3.0 %collective-permute-start.8 = (bf16[64,3072]{1,0:T(8,128)(2,1)S(1)}, bf16[64,3072]{1,0:T(8,128)(2,1)S(1)}, u32[]{:S(2)}, u32[]{:S(2)}) collective-permute-start(bf16[64,3072]{1,0:T(8,128)(2,1)S(1)} %give.6), channel_id=1, source_target_pairs={{0,4},{1,33},{2,6},{3,35},{4,0},{5,37},{6,2},{7,39},{8,12},{9,41},... | collective-permute-start | bytes 1179656 | tf_op jit(solution)/shard_map/ppermute | solution.py:54
  63.9 0.2 give.10
  64.1 0.8 collective-permute-start.13
  65.0 0.2 give.11
  65.2 0.9 collective-permute-start.14
  66.2 0.0 collective-permute-done.9.theirs.refs_1_
  66.2 0.2 give.7
  66.4 2.0 %collective-permute-start.10 = (bf16[64,3072]{1,0:T(8,128)(2,1)S(1)}, bf16[64,3072]{1,0:T(8,128)(2,1)S(1)}, u32[]{:S(2)}, u32[]{:S(2)}) collective-permute-start(bf16[64,3072]{1,0:T(8,128)(2,1)S(1)} %give.7), channel_id=1, source_target_pairs={{0,6},{1,49},{2,0},{3,51},{4,2},{5,53},{6,4},{7,55},{8,14},{9,57},... | collective-permute-start | bytes 1179656 | tf_op jit(solution)/shard_map/ppermute | solution.py:54
  68.5 0.2 give.8
  68.7 0.1 collective-permute-start.11
  68.8 0.2 give.9
  69.0 0.4 collective-permute-done.8.refs_9_
  69.4 3.0 %collective-permute-start.12 = (bf16[64,3072]{1,0:T(8,128)(2,1)S(1)}, bf16[64,3072]{1,0:T(8,128)(2,1)S(1)}, u32[]{:S(2)}, u32[]{:S(2)}) collective-permute-start(bf16[64,3072]{1,0:T(8,128)(2,1)S(1)} %give.9), channel_id=1, source_target_pairs={{0,4},{1,33},{2,6},{3,35},{4,0},{5,37},{6,2},{7,39},{8,12},{9,41},... | collective-permute-start | bytes 1179656 | tf_op jit(solution)/shard_map/ppermute | solution.py:54
  72.4 10.5 %all_to_all.15.parts = bf16[8,16,256]{2,1,0:T(8,128)(2,1)S(1)} all-to-all(bf16[8,16,256]{2,1,0:T(8,128)(2,1)S(1)} %attend.1), channel_id=1, replica_groups=mesh['ctx'=8,'grp'=16] {'ctx'}, dimensions={0} | all-to-all | bytes 131072 | tf_op jit(solution)/shard_map/all_to_all | solution.py:404
  82.9 0.8 heads.1
  83.7 0.0 collective-permute-done.13.refs_7_
  83.7 0.0 collective-permute-done.14.refs_8_
  83.7 0.0 collective-permute-done.10.refs_2_
  83.7 0.0 collective-permute-done.11.refs_3_
  83.7 0.0 collective-permute-done.12.refs_4_
  83.7 0.6 join.1
  84.3 15.4 %all_to_all.16.parts = bf16[16,4,6144]{2,1,0:T(4,128)(2,1)S(1)} all-to-all(bf16[16,4,6144]{2,1,0:T(4,128)(2,1)S(1)} %join.1), channel_id=1, replica_groups={{0,64,8,72,16,80,24,88,32,96,40,104,48,112,56,120},{2,66,10,74,18,82,26..., dimensions={0} | all-to-all | bytes 1572864 | tf_op jit(solution)/shard_map/all_to_all | solution.py:407
  99.7 0.7 fold.1
Async XLA Ops:
  2.6 20.6 %all-to-all-start = ((bf16[16,4,6272]{2,1,0:T(4,128)(2,1)}), bf16[16,4,6272]{2,1,0:T(4,128)(2,1)S(1)}, u32[]{:S(2)}, u32[]{:S(2)}) async-start(bf16[16,4,6272]{2,1,0:T(4,128)(2,1)} %pack.1), calls=%async_computation | async-start | bytes 1605632 | tf_op jit(solution)/shard_map/all_to_all | solution.py:379
  23.4 20.5 %collective-permute-start.2 = (bf16[64,6272]{1,0:T(8,128)(2,1)S(1)}, bf16[64,6272]{1,0:T(8,128)(2,1)S(1)}, u32[]{:S(2)}, u32[]{:S(2)}) collective-permute-start(bf16[64,6272]{1,0:T(8,128)(2,1)S(1)} %reshape.19.rows), channel_id=1, source_target_pairs={{0,6},{1,49},{2,0},{3,51},{4,2},{5,53},{6,4},{7,55},{8,14},{9,57},... | collective-permute-start | bytes 2408456 | tf_op jit(solution)/shard_map/ppermute | solution.py:54
  26.2 19.7 %collective-permute-start = (bf16[64,6272]{1,0:T(8,128)(2,1)S(1)}, bf16[64,6272]{1,0:T(8,128)(2,1)S(1)}, u32[]{:S(2)}, u32[]{:S(2)}) collective-permute-start(bf16[64,6272]{1,0:T(8,128)(2,1)S(1)} %reshape.19.rows), channel_id=1, source_target_pairs={{0,4},{1,33},{2,6},{3,35},{4,0},{5,37},{6,2},{7,39},{8,12},{9,41},... | collective-permute-start | bytes 2408456 | tf_op jit(solution)/shard_map/ppermute | solution.py:54
  27.0 20.6 %collective-permute-start.1 = (bf16[64,6272]{1,0:T(8,128)(2,1)S(1)}, bf16[64,6272]{1,0:T(8,128)(2,1)S(1)}, u32[]{:S(2)}, u32[]{:S(2)}) collective-permute-start(bf16[64,6272]{1,0:T(8,128)(2,1)S(1)} %reshape.19.rows), channel_id=1, source_target_pairs={{0,2},{1,17},{2,4},{3,19},{4,6},{5,21},{6,0},{7,23},{8,10},{9,25},... | collective-permute-start | bytes 2408456 | tf_op jit(solution)/shard_map/ppermute | solution.py:54
  28.2 21.7 %collective-permute-start.3 = (bf16[32,6272]{1,0:T(8,128)(2,1)S(1)}, bf16[32,6272]{1,0:T(8,128)(2,1)S(1)}, u32[]{:S(2)}, u32[]{:S(2)}) collective-permute-start(bf16[32,6272]{1,0:T(8,128)(2,1)S(1)} %get-tuple-element.45), channel_id=1, source_target_pairs={{0,1},{1,0},{2,3},{3,2},{4,5},{5,4},{6,7},{7,6},{8,9},{9,8},{10,11... | collective-permute-start | bytes 1204232 | tf_op jit(solution)/shard_map/ppermute | solution.py:54
  44.4 5.5 %collective-permute-start.6 = (bf16[32,6272]{1,0:T(8,128)(2,1)S(1)}, bf16[32,6272]{1,0:T(8,128)(2,1)S(1)}, u32[]{:S(2)}, u32[]{:S(2)}) collective-permute-start(bf16[32,6272]{1,0:T(8,128)(2,1)S(1)} %get-tuple-element.48), channel_id=1, source_target_pairs={{0,1},{1,0},{2,3},{3,2},{4,5},{5,4},{6,7},{7,6},{8,9},{9,8},{10,11... | collective-permute-start | bytes 1204232 | tf_op jit(solution)/shard_map/ppermute | solution.py:54
  46.4 3.4 %collective-permute-start.5 = (bf16[32,6272]{1,0:T(8,128)(2,1)S(1)}, bf16[32,6272]{1,0:T(8,128)(2,1)S(1)}, u32[]{:S(2)}, u32[]{:S(2)}) collective-permute-start(bf16[32,6272]{1,0:T(8,128)(2,1)S(1)} %get-tuple-element.47), channel_id=1, source_target_pairs={{0,1},{1,0},{2,3},{3,2},{4,5},{5,4},{6,7},{7,6},{8,9},{9,8},{10,11... | collective-permute-start | bytes 1204232 | tf_op jit(solution)/shard_map/ppermute | solution.py:54
  48.1 3.1 %collective-permute-start.4 = (bf16[32,6272]{1,0:T(8,128)(2,1)S(1)}, bf16[32,6272]{1,0:T(8,128)(2,1)S(1)}, u32[]{:S(2)}, u32[]{:S(2)}) collective-permute-start(bf16[32,6272]{1,0:T(8,128)(2,1)S(1)} %get-tuple-element.46), channel_id=1, source_target_pairs={{0,1},{1,0},{2,3},{3,2},{4,5},{5,4},{6,7},{7,6},{8,9},{9,8},{10,11... | collective-permute-start | bytes 1204232 | tf_op jit(solution)/shard_map/ppermute | solution.py:54
  58.3 2.4 %collective-permute-start.7 = (bf16[128,3072]{1,0:T(8,128)(2,1)S(1)}, bf16[128,3072]{1,0:T(8,128)(2,1)S(1)}, u32[]{:S(2)}, u32[]{:S(2)}) collective-permute-start(bf16[128,3072]{1,0:T(8,128)(2,1)S(1)} %get-tuple-element.53), channel_id=1, source_target_pairs={{0,1},{1,0},{2,3},{3,2},{4,5},{5,4},{6,7},{7,6},{8,9},{9,8},{10,11... | collective-permute-start | bytes 2359304 | tf_op jit(solution)/shard_map/ppermute | solution.py:54
  58.7 7.4 %collective-permute-start.9 = (bf16[128,3072]{1,0:T(8,128)(2,1)S(1)}, bf16[128,3072]{1,0:T(8,128)(2,1)S(1)}, u32[]{:S(2)}, u32[]{:S(2)}) collective-permute-start(bf16[128,3072]{1,0:T(8,128)(2,1)S(1)} %get-tuple-element.60), channel_id=1, source_target_pairs={{0,1},{1,0},{2,3},{3,2},{4,5},{5,4},{6,7},{7,6},{8,9},{9,8},{10,11... | collective-permute-start | bytes 2359304 | tf_op jit(solution)/shard_map/ppermute | solution.py:54
  60.9 8.5 %collective-permute-start.8 = (bf16[64,3072]{1,0:T(8,128)(2,1)S(1)}, bf16[64,3072]{1,0:T(8,128)(2,1)S(1)}, u32[]{:S(2)}, u32[]{:S(2)}) collective-permute-start(bf16[64,3072]{1,0:T(8,128)(2,1)S(1)} %give.6), channel_id=1, source_target_pairs={{0,4},{1,33},{2,6},{3,35},{4,0},{5,37},{6,2},{7,39},{8,12},{9,41},... | collective-permute-start | bytes 1179656 | tf_op jit(solution)/shard_map/ppermute | solution.py:54
  64.1 19.6 %collective-permute-start.13 = (bf16[64,3072]{1,0:T(8,128)(2,1)S(1)}, bf16[64,3072]{1,0:T(8,128)(2,1)S(1)}, u32[]{:S(2)}, u32[]{:S(2)}) collective-permute-start(bf16[64,3072]{1,0:T(8,128)(2,1)S(1)} %give.10), channel_id=1, source_target_pairs={{0,6},{1,49},{2,0},{3,51},{4,2},{5,53},{6,4},{7,55},{8,14},{9,57},... | collective-permute-start | bytes 1179656 | tf_op jit(solution)/shard_map/ppermute | solution.py:54
  65.2 18.5 %collective-permute-start.14 = (bf16[64,3072]{1,0:T(8,128)(2,1)S(1)}, bf16[64,3072]{1,0:T(8,128)(2,1)S(1)}, u32[]{:S(2)}, u32[]{:S(2)}) collective-permute-start(bf16[64,3072]{1,0:T(8,128)(2,1)S(1)} %give.11), channel_id=1, source_target_pairs={{0,2},{1,17},{2,4},{3,19},{4,6},{5,21},{6,0},{7,23},{8,10},{9,25},... | collective-permute-start | bytes 1179656 | tf_op jit(solution)/shard_map/ppermute | solution.py:54
  66.4 17.3 %collective-permute-start.10 = (bf16[64,3072]{1,0:T(8,128)(2,1)S(1)}, bf16[64,3072]{1,0:T(8,128)(2,1)S(1)}, u32[]{:S(2)}, u32[]{:S(2)}) collective-permute-start(bf16[64,3072]{1,0:T(8,128)(2,1)S(1)} %give.7), channel_id=1, source_target_pairs={{0,6},{1,49},{2,0},{3,51},{4,2},{5,53},{6,4},{7,55},{8,14},{9,57},... | collective-permute-start | bytes 1179656 | tf_op jit(solution)/shard_map/ppermute | solution.py:54
  68.7 15.0 %collective-permute-start.11 = (bf16[64,3072]{1,0:T(8,128)(2,1)S(1)}, bf16[64,3072]{1,0:T(8,128)(2,1)S(1)}, u32[]{:S(2)}, u32[]{:S(2)}) collective-permute-start(bf16[64,3072]{1,0:T(8,128)(2,1)S(1)} %give.8), channel_id=1, source_target_pairs={{0,2},{1,17},{2,4},{3,19},{4,6},{5,21},{6,0},{7,23},{8,10},{9,25},... | collective-permute-start | bytes 1179656 | tf_op jit(solution)/shard_map/ppermute | solution.py:54
  69.4 14.3 %collective-permute-start.12 = (bf16[64,3072]{1,0:T(8,128)(2,1)S(1)}, bf16[64,3072]{1,0:T(8,128)(2,1)S(1)}, u32[]{:S(2)}, u32[]{:S(2)}) collective-permute-start(bf16[64,3072]{1,0:T(8,128)(2,1)S(1)} %give.9), channel_id=1, source_target_pairs={{0,4},{1,33},{2,6},{3,35},{4,0},{5,37},{6,2},{7,39},{8,12},{9,41},... | collective-permute-start | bytes 1179656 | tf_op jit(solution)/shard_map/ppermute | solution.py:54
